TPU v7x, 32 devices: a whole 2x2x4 slice. The times are simulated.
32 devices in a mesh: seq: 2 (over core), wide: 16 (over z, y, x).
Axes of the slice: x: 2, y: 2, z: 4, core: 2. Of those that a mesh axis runs over, the one named last changes fastest.
Arguments:
- streams: bfloat16 [16, 1024, 4, 768], P('wide', 'seq'), may hold values from -6 to 6
- cotangent: bfloat16 [16, 1024, 4, 768], P('wide', 'seq'), may hold values from -6 to 6
- doc_lengths: int32 [16, 8], P('wide'), may hold values from 1 to 768, as said below
- attn_in: bfloat16 [768, 2304], replicated, may hold values from -0.21875 to 0.21875
- attn_out: bfloat16 [768, 768], replicated, may hold values from -0.625 to 0.625
- ffn_in: bfloat16 [768, 6144], replicated, may hold values from -0.21875 to 0.21875
- ffn_out: bfloat16 [3072, 768], replicated, may hold values from -0.109375 to 0.109375
- norm_gains: bfloat16 [768, 2], replicated, may hold values from 0.5 to 1.5
- big_state: float32 [3, 12288, 768], P(None, ('seq', 'wide'))
- small_state: float32 [3, 1568], replicated
Outputs:
- new_streams: bfloat16 [16, 1024, 4, 768], P('wide', 'seq')
- streams_grad: bfloat16 [16, 1024, 4, 768], P('wide', 'seq')
- weights_next: float32 [12288, 768], P(('seq', 'wide'))
- first_next: float32 [12288, 768], P(('seq', 'wide'))
- second_next: float32 [12288, 768], P(('seq', 'wide'))
- weight_grads: float32 [12288, 768], P(('seq', 'wide'))
- small_weights_next: float32 [1568], replicated
- small_first_next: float32 [1568], replicated
- small_second_next: float32 [1568], replicated
- small_grads: float32 [1568], replicated
- weights_copy: bfloat16 [12288, 768], replicated
- gains_copy: bfloat16 [768, 2], replicated
Inputs may be any that keep to these rules, and one draw needn't show every extreme that they name: `doc_lengths`: each row sums to 1024; in every sequence the fourth document covers the positions 128 to 895, the documents before it lie within the first 128 positions, those after it within the last 128, and the last document holds one token.
All inputs are finite; a program needn't handle non-finite values.
Results may differ from a plain program's by a relative error of at most 0.013.
Values may be sent and summed in bfloat16 or wider, within the bound.
A program may use at most 256 MiB of HBM per device.

v0:
```python
import jax
import jax.numpy as jnp
from jax import lax
from jax.sharding import PartitionSpec as P

HEADS = 12
HD = 64
NS = 4
STEP = 10


norm_epsilon = 1e-05
rope_base = 10000.0
beta_first = 0.9
beta_second = 0.95
adam_epsilon = 1e-08
weight_decay = 0.1
learn_rate = 0.01
masked_score = -1e30


def shifted(value, axis, by):
    count = lax.axis_size(axis)
    pairs = [(i, i + by) for i in range(count) if 0 <= i + by < count]
    return lax.ppermute(value, axis, pairs)


def doc_layout(lengths, token_total):
    bounds = jnp.cumsum(lengths)
    starts = bounds - lengths
    places = jnp.arange(token_total, dtype=jnp.int32)
    segment = jnp.sum((places[:, None] >= bounds[None, :]).astype(jnp.int32), axis=1)
    picked = segment[:, None] == jnp.arange(lengths.shape[0], dtype=jnp.int32)[None, :]
    offset = jnp.sum(jnp.where(picked, starts[None, :], 0), axis=1)
    return (segment, places - offset)


def rope_tables(position, head_size):
    exponent = jnp.arange(head_size // 2, dtype=jnp.float32) * (2.0 / head_size)
    frequency = jnp.power(jnp.float32(rope_base), -exponent)
    angles = position.astype(jnp.float32)[:, None] * frequency[None, :]
    return (jnp.cos(angles)[:, None, :], jnp.sin(angles)[:, None, :])


def rotate(values, cosine, sine_table):
    half_size = values.shape[-1] // 2
    leading = values[..., :half_size]
    trailing = values[..., half_size:]
    return jnp.concatenate(
        [leading * cosine - trailing * sine_table, trailing * cosine + leading * sine_table],
        axis=-1,
    )


def rotate_back(grads, cosine, sine_table):
    half_size = grads.shape[-1] // 2
    leading = grads[..., :half_size]
    trailing = grads[..., half_size:]
    return jnp.concatenate(
        [leading * cosine + trailing * sine_table, trailing * cosine - leading * sine_table],
        axis=-1,
    )


def norm_parts(values):
    centre = jnp.mean(values, axis=-1, keepdims=True)
    centred = values - centre
    scaling = lax.rsqrt(jnp.mean(centred * centred, axis=-1, keepdims=True) + norm_epsilon)
    return (centred * scaling, scaling)


def norm_back(grads, normal, scaling, gain):
    gain_grad = jnp.sum(grads * normal, axis=0)
    scaled = grads * gain
    centre = jnp.mean(scaled, axis=-1, keepdims=True)
    along_normal = jnp.mean(scaled * normal, axis=-1, keepdims=True)
    return (gain_grad, scaling * (scaled - centre - normal * along_normal))


def right_product(left, right):
    return lax.dot_general(
        left, right, (((1,), (1,)), ((), ())), preferred_element_type=jnp.float32
    )


def left_product(left, right):
    return lax.dot_general(
        left, right, (((0,), (0,)), ((), ())), preferred_element_type=jnp.float32
    )


def forward_layer(stream_values, weights, gain_values, mixing, allowed, cosine, sine_table):
    attn_in, attn_out, ffn_in, ffn_out = weights
    row_count = stream_values.shape[0]
    model_width = attn_out.shape[0]
    stream_count = mixing.shape[0]
    hidden_units = ffn_out.shape[0]
    branch_in = jnp.sum(stream_values * mixing[None, :, stream_count, None], axis=1)
    mixed_streams = jnp.sum(
        stream_values[:, :, None, :] * mixing[None, :, :stream_count, None], axis=1
    )
    normal_one, scale_one = norm_parts(branch_in)
    normed = (normal_one * gain_values[:, 0]).astype(jnp.bfloat16)
    project = jnp.dot(normed, attn_in, preferred_element_type=jnp.float32)
    queries = rotate(
        project[:, :model_width].reshape(row_count, HEADS, HD), cosine, sine_table
    ).astype(jnp.bfloat16)
    keys_rot = rotate(
        project[:, model_width : 2 * model_width].reshape(row_count, HEADS, HD), cosine, sine_table
    ).astype(jnp.bfloat16)
    values_in = project[:, 2 * model_width :].astype(jnp.bfloat16)
    outgoing = jnp.concatenate([keys_rot.reshape(row_count, model_width), values_in], axis=1)
    earlier = shifted(outgoing, "seq", 1)
    key_rows = jnp.concatenate([earlier, outgoing], axis=0)
    keys_all = key_rows[:, :model_width].reshape(2 * row_count, HEADS, HD)
    values_all = key_rows[:, model_width:].reshape(2 * row_count, HEADS, HD)
    scores = jnp.einsum(
        "qhd,khd->hqk", queries, keys_all, preferred_element_type=jnp.float32
    ) * HD ** (-0.5)
    scores = jnp.where(allowed[None], scores, masked_score)
    row_top = jnp.max(scores, axis=-1, keepdims=True)
    lifted = jnp.exp(scores - row_top)
    attend = lifted / jnp.sum(lifted, axis=-1, keepdims=True)
    attend_low = attend.astype(jnp.bfloat16)
    context = jnp.einsum("hqk,khd->qhd", attend_low, values_all, preferred_element_type=jnp.float32)
    context = context.reshape(row_count, model_width).astype(jnp.bfloat16)
    first_out = jnp.dot(context, attn_out, preferred_element_type=jnp.float32)
    streams_mid = mixed_streams + mixing[None, :, stream_count + 1, None] * first_out[:, None, :]
    ffn_read = jnp.sum(streams_mid * mixing[None, :, stream_count + 2, None], axis=1)
    normal_two, scale_two = norm_parts(ffn_read)
    normed_two = (normal_two * gain_values[:, 1]).astype(jnp.bfloat16)
    gate_up = jnp.dot(normed_two, ffn_in, preferred_element_type=jnp.float32)
    gate_part = gate_up[:, :hidden_units]
    up_part = gate_up[:, hidden_units:]
    hidden = (jax.nn.silu(gate_part) * up_part).astype(jnp.bfloat16)
    second_out = jnp.dot(hidden, ffn_out, preferred_element_type=jnp.float32)
    result = streams_mid + mixing[None, :, stream_count + 3, None] * second_out[:, None, :]
    saved = (
        normal_one,
        scale_one,
        normed,
        queries,
        keys_all,
        values_all,
        attend,
        attend_low,
        context,
        first_out,
        streams_mid,
        normal_two,
        scale_two,
        normed_two,
        gate_part,
        up_part,
        hidden,
        second_out,
    )
    return (result, saved)


def backward_layer(
    stream_values, grad_out, weights, gain_values, mixing, cosine, sine_table, saved
):
    attn_in, attn_out, ffn_in, ffn_out = weights
    (
        normal_one,
        scale_one,
        normed,
        queries,
        keys_all,
        values_all,
        attend,
        attend_low,
        context,
        first_out,
        streams_mid,
        normal_two,
        scale_two,
        normed_two,
        gate_part,
        up_part,
        hidden,
        second_out,
    ) = saved
    row_count = stream_values.shape[0]
    model_width = attn_out.shape[0]
    stream_count = mixing.shape[0]
    second_low = jnp.sum(grad_out * mixing[None, :, stream_count + 3, None], axis=1).astype(
        jnp.bfloat16
    )
    grad_depth_two = jnp.sum(grad_out * second_out[:, None, :], axis=(0, 2))
    ffn_out_grad = left_product(hidden, second_low)
    hidden_grad = right_product(second_low, ffn_out)
    sigmoid_gate = jax.nn.sigmoid(gate_part)
    gate_grad = hidden_grad * up_part * sigmoid_gate * (1.0 + gate_part * (1.0 - sigmoid_gate))
    up_grad = hidden_grad * gate_part * sigmoid_gate
    gate_up_low = jnp.concatenate([gate_grad, up_grad], axis=1).astype(jnp.bfloat16)
    ffn_in_grad = left_product(normed_two, gate_up_low)
    normed_two_grad = right_product(gate_up_low, ffn_in)
    gain_two_grad, read_grad = norm_back(normed_two_grad, normal_two, scale_two, gain_values[:, 1])
    mid_grad = grad_out + mixing[None, :, stream_count + 2, None] * read_grad[:, None, :]
    grad_read_two = jnp.sum(streams_mid * read_grad[:, None, :], axis=(0, 2))
    first_low = jnp.sum(mid_grad * mixing[None, :, stream_count + 1, None], axis=1).astype(
        jnp.bfloat16
    )
    grad_depth_one = jnp.sum(mid_grad * first_out[:, None, :], axis=(0, 2))
    attn_out_grad = left_product(context, first_low)
    context_grad = (
        right_product(first_low, attn_out).astype(jnp.bfloat16).reshape(row_count, HEADS, HD)
    )
    attend_grad = jnp.einsum(
        "qhd,khd->hqk", context_grad, values_all, preferred_element_type=jnp.float32
    )
    values_grad = jnp.einsum(
        "hqk,qhd->khd", attend_low, context_grad, preferred_element_type=jnp.float32
    )
    inner_sum = jnp.sum(attend * attend_grad, axis=-1, keepdims=True)
    score_low = (attend * (attend_grad - inner_sum)).astype(jnp.bfloat16)
    query_grad = jnp.einsum(
        "hqk,khd->qhd", score_low, keys_all, preferred_element_type=jnp.float32
    ) * HD ** (-0.5)
    keys_grad = jnp.einsum(
        "hqk,qhd->khd", score_low, queries, preferred_element_type=jnp.float32
    ) * HD ** (-0.5)
    returned = jnp.concatenate(
        [
            keys_grad[:row_count].reshape(row_count, model_width),
            values_grad[:row_count].reshape(row_count, model_width),
        ],
        axis=1,
    )
    from_later = shifted(returned.astype(jnp.bfloat16), "seq", -1).astype(returned.dtype)
    own_keys = keys_grad[row_count:].reshape(row_count, model_width) + from_later[:, :model_width]
    own_values = (
        values_grad[row_count:].reshape(row_count, model_width) + from_later[:, model_width:]
    )
    query_back = rotate_back(query_grad, cosine, sine_table).reshape(row_count, model_width)
    key_back = rotate_back(own_keys.reshape(row_count, HEADS, HD), cosine, sine_table).reshape(
        row_count, model_width
    )
    project_low = jnp.concatenate([query_back, key_back, own_values], axis=1).astype(jnp.bfloat16)
    attn_in_grad = left_product(normed, project_low)
    normed_grad = right_product(project_low, attn_in)
    gain_one_grad, branch_grad = norm_back(normed_grad, normal_one, scale_one, gain_values[:, 0])
    stream_grad = jnp.sum(mid_grad[:, None, :, :] * mixing[None, :, :stream_count, None], axis=2)
    stream_grad = stream_grad + mixing[None, :, stream_count, None] * branch_grad[:, None, :]
    grad_mix = jnp.sum(stream_values[:, :, None, :] * mid_grad[:, None, :, :], axis=(0, 3))
    grad_read_one = jnp.sum(stream_values * branch_grad[:, None, :], axis=(0, 2))
    mixing_grad = jnp.concatenate(
        [
            grad_mix,
            grad_read_one[:, None],
            grad_depth_one[:, None],
            grad_read_two[:, None],
            grad_depth_two[:, None],
        ],
        axis=1,
    )
    gains_grad = jnp.stack([gain_one_grad, gain_two_grad], axis=1)
    return (
        stream_grad,
        (attn_in_grad, attn_out_grad, ffn_in_grad, ffn_out_grad),
        gains_grad,
        mixing_grad,
    )


def adam_step(shard_state, shard_grad):
    weight = shard_state[0]
    first_new = beta_first * shard_state[1] + (1.0 - beta_first) * shard_grad
    second_new = beta_second * shard_state[2] + (1.0 - beta_second) * shard_grad * shard_grad
    first_hat = first_new / (1.0 - beta_first**STEP)
    second_hat = second_new / (1.0 - beta_second**STEP)
    update = first_hat / (jnp.sqrt(second_hat) + adam_epsilon) + weight_decay * weight
    weight_new = weight - learn_rate * update
    return (weight_new, first_new, second_new)


def on_device(
    streams,
    cotangent,
    doc_lengths,
    attn_in,
    attn_out,
    ffn_in,
    ffn_out,
    norm_gains,
    big_state,
    small_state,
):
    row_count = streams.shape[1]
    model_width = attn_out.shape[0]
    member = lax.axis_index("seq")
    token_total = row_count * lax.axis_size("seq")
    token_count = token_total * lax.axis_size("wide")
    segment, position = doc_layout(doc_lengths[0], token_total)
    own_start = member * row_count
    own_index = own_start + jnp.arange(row_count, dtype=jnp.int32)
    seg_query = lax.dynamic_slice_in_dim(segment, own_start, row_count)
    pos_query = lax.dynamic_slice_in_dim(position, own_start, row_count)
    padded_seg = jnp.concatenate([jnp.full((row_count,), -1, jnp.int32), segment])
    key_seg = lax.dynamic_slice_in_dim(padded_seg, own_start, 2 * row_count)
    key_index = own_start - row_count + jnp.arange(2 * row_count, dtype=jnp.int32)
    allowed = (key_seg[None, :] == seg_query[:, None]) & (key_index[None, :] <= own_index[:, None])
    cosine, sine_table = rope_tables(pos_query, HD)
    weights = (attn_in, attn_out, ffn_in, ffn_out)
    gain_values = norm_gains.astype(jnp.float32)
    mixing = small_state[0, 2 * model_width :].reshape(NS, NS + 4)
    stream_values = streams[0].astype(jnp.float32)
    result, saved = forward_layer(
        stream_values, weights, gain_values, mixing, allowed, cosine, sine_table
    )
    again_streams, again_weights, again_gains = lax.optimization_barrier(
        (stream_values, weights, gain_values)
    )
    unused, saved = forward_layer(
        again_streams, again_weights, again_gains, mixing, allowed, cosine, sine_table
    )
    grad_out = cotangent[0].astype(jnp.float32)
    stream_grad, matrix_grads, gains_local, mixing_local = backward_layer(
        stream_values, grad_out, weights, gain_values, mixing, cosine, sine_table, saved
    )
    flat_local = jnp.concatenate([grad.reshape(-1, model_width) for grad in matrix_grads], axis=0)
    summed = lax.psum_scatter(flat_local, ("seq", "wide"), scatter_dimension=0, tiled=True)
    owned_grads = summed / token_count
    gains_total, mixing_total = lax.psum((gains_local, mixing_local), ("seq", "wide"))
    small_grads = (
        jnp.concatenate([gains_total.T.reshape(-1), mixing_total.reshape(-1)]) / token_count
    )
    weight_new, first_new, second_new = adam_step(big_state, owned_grads)
    small_weight, small_first, small_second = adam_step(small_state, small_grads)
    copy_shard = weight_new.astype(jnp.bfloat16)
    gathered = lax.all_gather(copy_shard, ("seq", "wide"), axis=0, tiled=True)
    gains_copy = small_weight[: 2 * model_width].reshape(2, model_width).T.astype(jnp.bfloat16)
    return (
        result.astype(jnp.bfloat16)[None],
        stream_grad.astype(jnp.bfloat16)[None],
        weight_new,
        first_new,
        second_new,
        owned_grads,
        small_weight,
        small_first,
        small_second,
        small_grads,
        gathered,
        gains_copy,
    )


def solution(mesh):
    in_specs = (
        P("wide", "seq", None, None),
        P("wide", "seq", None, None),
        P("wide", None),
        P(),
        P(),
        P(),
        P(),
        P(),
        P(None, ("seq", "wide"), None),
        P(),
    )
    out_specs = (
        P("wide", "seq", None, None),
        P("wide", "seq", None, None),
        P(("seq", "wide"), None),
        P(("seq", "wide"), None),
        P(("seq", "wide"), None),
        P(("seq", "wide"), None),
        P(),
        P(),
        P(),
        P(),
        P(),
        P(),
    )
    return jax.shard_map(
        on_device, mesh=mesh, in_specs=in_specs, out_specs=out_specs, check_vma=False
    )
```

profile of v0, /device:TPU:0, one launch (start us, length us, event | category | flops | bytes accessed | tf_op | source)
XLA Modules:
  0.0 958.6 jit_solution(13121050289708896632)
XLA Ops:
  81.4 13.4 %fusion.51 = f32[12,512,1024]{2,1,0:T(8,128)} fusion(bf16[1024,12,64]{0,2,1:T(8,128)(2,1)} %bitcast.126, bf16[512,12,32]{0,2,1:T(8,128)(2,1)} %get-tuple-element.103, bf16[512,12,32]{0,2,1:T(8,128)(2,1)} %get-tuple-element.102), kind=kOutput, calls=%fused_computation.139 | convolution fusion | flops 806879232 | bytes 27525120 | tf_op jit(solution)/shard_map/qhd,khd->hqk/dot_general | solution.py:117
  94.9 34.1 %fusion.79 = (f32[12,512]{1,0:T(8,128)}, f32[12,512,1024]{2,1,0:T(8,128)}) fusion(f32[12,512,1024]{2,1,0:T(8,128)} %fusion.51, pred[512,1024]{1,0:T(8,128)(4,1)} %compare_and_fusion), kind=kOutput, calls=%fused_computation.212 | output fusion | flops 37749760 | bytes 50880512 | tf_op jit(solution)/shard_map/sub | solution.py:122
  128.9 10.9 %fusion.32 = bf16[12,64,512]{2,1,0:T(8,128)(2,1)S(1)} fusion(bf16[1024,12,64]{0,2,1:T(8,128)(2,1)} %bitcast.138, f32[12,512,1024]{2,1,0:T(8,128)} %get-tuple-element.115, f32[12,512]{1,0:T(8,128)} %get-tuple-element.114), kind=kOutput, calls=%fused_computation.98 | convolution fusion | flops 818282496 | bytes 27549696 | tf_op jit(solution)/shard_map/hqk,khd->qhd/dot_general | solution.py:125
  145.5 12.5 %fusion.73 = f32[512,6144]{1,0:T(8,128)} fusion(bf16[768,6144]{1,0:T(8,128)(2,1)} %param.15, f32[512,768]{1,0:T(8,128)S(1)} %get-tuple-element.37, f32[768]{0:T(1024)S(1)} %get-tuple-element.61, f32[512]{0:T(512)S(1)} %add_rsqrt_fusion, f32[512]{0:T(512)S(1)} %broadcast_multiply_fusion.6), kind=kOutput, calls=%fused_computation.206 | convolution fusion | flops 4833411072 | bytes 23600128 | tf_op jit(solution)/shard_map/dot_general | solution.py:132
  158.0 10.1 %multiply_convert_fusion.3 = (bf16[512,3072]{1,0:T(8,128)(2,1)}, bf16[512,3072]{1,0:T(8,128)(2,1)}, bf16[512,3072]{1,0:T(8,128)(2,1)}) fusion(f32[512,6144]{1,0:T(8,128)} %fusion.73, bf16[512,768]{1,0:T(8,128)(2,1)S(1)} %get-tuple-element.122, bf16[3072,768]{1,0:T(8,128)(2,1)S(1)} %bitcast.158), kind=kOutput, calls=%fused_computation.43 | convolution fusion | flops 2441084928 | bytes 27525120 | tf_op jit(solution)/shard_map/dot_general | solution.py:81
  168.1 11.0 %multiply_reduce_fusion.15 = (f32[768]{0:T(1024)}, f32[512]{0:T(512)S(1)}, f32[512]{0:T(512)S(1)}, f32[512,768]{1,0:T(8,128)S(1)}) fusion(f32[512,768]{1,0:T(8,128)S(1)} %get-tuple-element.37, f32[512]{0:T(512)S(1)} %add_rsqrt_fusion, f32[512]{0:T(512)S(1)} %broadcast_multiply_fusion.6, f32[768]{0:T(1024)S(1)} %copy-done.41, bf16[768,6144]{1,0:T(8,128)(2,1)} %param.15, ...), kind=kOutput, calls=%fused_computation.79 | convolution fusion | flops 4847564800 | bytes 18888704 | tf_op jit(solution)/shard_map/dot_general | solution.py:81
  187.5 9.0 multiply_reduce_fusion.6
  201.3 17.5 %multiply_reduce_fusion.1 = (f32[12,512]{1,0:T(8,128)}, f32[12,512,1024]{2,1,0:T(8,128)}) fusion(f32[12,512,1024]{2,1,0:T(8,128)} %get-tuple-element.115, f32[12,512]{1,0:T(8,128)} %get-tuple-element.114, bf16[512,12,64]{0,2,1:T(8,128)(2,1)} %bitcast.145, bf16[1024,12,64]{0,2,1:T(8,128)(2,1)} %bitcast.139), kind=kOutput, calls=%fused_computation.5 | convolution fusion | flops 824174592 | bytes 52740096 | tf_op jit(solution)/shard_map/qhd,khd->hqk/dot_general | solution.py:211
  218.8 10.8 %fusion.27 = f32[1024,12,64]{0,2,1:T(8,128)S(1)} fusion(bf16[512,12,64]{0,2,1:T(8,128)(2,1)} %bitcast.146, f32[12,512,1024]{2,1,0:T(8,128)} %get-tuple-element.115, f32[12,512]{1,0:T(8,128)} %get-tuple-element.114), kind=kOutput, calls=%fused_computation.68 | convolution fusion | flops 817889280 | bytes 29122560 | tf_op jit(solution)/shard_map/hqk,qhd->khd/dot_general | solution.py:214
  229.7 17.6 %multiply_convert_fusion = bf16[12,512,1024]{2,1,0:T(8,128)(2,1)S(1)} fusion(f32[12,512,1024]{2,1,0:T(8,128)} %get-tuple-element.118, f32[12,512]{1,0:T(8,128)S(1)} %copy-done.37, f32[12,512,1024]{2,1,0:T(8,128)} %get-tuple-element.115, f32[12,512]{1,0:T(8,128)S(1)} %copy-done.36), kind=kLoop, calls=%fused_computation.4 | loop fusion | flops 25165824 | bytes 62963712 | tf_op jit(solution)/shard_map/convert_element_type | solution.py:218
  255.8 9.8 %fusion.23 = f32[768,6144]{1,0:T(8,128)} fusion(bf16[512,3072]{1,0:T(8,128)(2,1)S(1)} %copy-done.22, bf16[512,3072]{1,0:T(8,128)(2,1)S(1)} %copy-done.21, f32[512,768]{1,0:T(8,128)S(1)} %copy-done.3, f32[768]{0:T(1024)S(1)} %get-tuple-element.61, f32[512]{0:T(512)S(1)} %add_rsqrt_fusion, f32[512]{0:T(512)S(1)} %broadcast_multiply_fusion.6), kind=kOutput, calls=%fused_computation.59 | convolution fusion | flops 4845993984 | bytes 26745856 | tf_op jit(solution)/shard_map/dot_general | solution.py:87
  268.1 19.7 %reshape.385 = f32[6144,768]{1,0:T(8,128)} reshape(f32[768,6144]{1,0:T(8,128)} %fusion.23) | data formatting | bytes 37748736 | tf_op jit(solution)/shard_map/reshape | solution.py:323
  296.8 8.5 multiply_bitcast_fusion.1
  315.7 8.4 reshape.384
  324.1 26.8 %pad_maximum_fusion = f32[12288,768]{1,0:T(8,128)} fusion(f32[3072,768]{1,0:T(8,128)} %fusion.85, f32[6144,768]{1,0:T(8,128)} %reshape.385, f32[768,768]{1,0:T(8,128)} %fusion.84, f32[2304,768]{1,0:T(8,128)} %reshape.384), kind=kLoop, calls=%fused_computation.2 | loop fusion | flops 28311552 | bytes 75497472 | tf_op jit(solution)/shard_map/concatenate | solution.py:323
  351.2 351.2 %reduce-scatter.2.cloned.1.call-done = f32[384,768]{1,0:T(8,128)} async-done(((f32[12288,768]{1,0:T(8,128)}), f32[384,768]{1,0:T(8,128)}) %reduce-scatter.2.cloned.1.call-update) | async-done | bytes 1179664 | tf_op jit(solution)/shard_map/reduce_scatter | solution.py:324
  723.6 10.5 %multiply_reduce_fusion.13 = (f32[512]{0:T(512)S(1)}, f32[512,768]{1,0:T(8,128)S(1)}, f32[4]{0:T(128)}) fusion(bf16[1,512,4,768]{3,2,1,0:T(4,128)(2,1)S(1)} %copy-done.11, f32[4]{0:T(128)S(1)} %copy-done.49, f32[512,768]{1,0:T(8,128)S(1)} %subtract_multiply_fusion), kind=kLoop, calls=%fused_computation.55 | loop fusion | flops 9043452 | bytes 6293536 | tf_op jit(solution)/shard_map/reduce_sum | solution.py:66
  757.1 15.3 %multiply_reduce_fusion = (f32[4,4]{1,0:T(4,128)}, f32[512,4,768]{2,0,1:T(8,128)}, f32[512,4,768]{2,0,1:T(8,128)}) fusion(f32[512,4,768]{2,0,1:T(8,128)} %get-tuple-element.83, f32[512,4,768]{2,0,1:T(8,128)} %copy.57, f32[4,4]{1,0:T(4,128)S(1)} %bitcast.150), kind=kLoop, calls=%fused_computation.3 | loop fusion | flops 34602992 | bytes 25165952 | tf_op jit(solution)/shard_map/reduce_sum | solution.py:247
  782.3 43.2 %all-reduce.1 = (f32[1536]{0:T(1024)}, f32[32]{0:T(128)}) all-reduce(f32[1536]{0:T(1024)S(1)} %reshape.386, f32[32]{0:T(128)} %reshape.387), channel_id=1, replica_groups=mesh['seq'=2,'wide'=16] {'seq','wide'}, use_global_device_ids=true, to_apply=%region_32.33 | all-reduce | flops 1568 | bytes 12544 | tf_op jit(solution)/shard_map/psum | solution.py:326
  847.2 13.4 %fusion.41 = f32[12,512,1024]{2,1,0:T(8,128)} fusion(bf16[1024,12,64]{0,2,1:T(8,128)(2,1)} %bitcast.128, bf16[512,12,32]{0,2,1:T(8,128)(2,1)} %get-tuple-element.95, bf16[512,12,32]{0,2,1:T(8,128)(2,1)} %get-tuple-element.94), kind=kOutput, calls=%fused_computation.112 | convolution fusion | flops 806879232 | bytes 27525120 | tf_op jit(solution)/shard_map/qhd,khd->hqk/dot_general | solution.py:117
  860.6 34.8 %fusion.80 = (f32[12,512]{1,0:T(8,128)}, f32[12,512,1024]{2,1,0:T(8,128)}) fusion(f32[12,512,1024]{2,1,0:T(8,128)} %fusion.41, pred[512,1024]{1,0:T(8,128)(4,1)} %compare_and_fusion), kind=kOutput, calls=%fused_computation.213 | output fusion | flops 37749760 | bytes 50880512 | tf_op jit(solution)/shard_map/sub | solution.py:122
  895.5 11.8 %fusion.31 = bf16[12,64,512]{2,1,0:T(8,128)(2,1)} fusion(bf16[1024,12,64]{0,2,1:T(8,128)(2,1)} %bitcast.140, f32[12,512,1024]{2,1,0:T(8,128)} %get-tuple-element.121, f32[12,512]{1,0:T(8,128)} %get-tuple-element.120), kind=kOutput, calls=%fused_computation.96 | convolution fusion | flops 818282496 | bytes 27549696 | tf_op jit(solution)/shard_map/hqk,khd->qhd/dot_general | solution.py:125
  911.1 11.9 %fusion.40 = f32[512,6144]{1,0:T(8,128)} fusion(bf16[768,6144]{1,0:T(8,128)(2,1)} %param.15, f32[512,768]{1,0:T(8,128)S(1)} %get-tuple-element.39, f32[768]{0:T(1024)S(1)} %copy-done.42, f32[512]{0:T(512)S(1)} %add_rsqrt_fusion.2, f32[512]{0:T(512)S(1)} %broadcast_multiply_fusion.8), kind=kOutput, calls=%fused_computation.110 | convolution fusion | flops 4833411072 | bytes 23600128 | tf_op jit(solution)/shard_map/dot_general | solution.py:132
  935.1 16.5 %copy.87 = bf16[12288,768]{1,0:T(8,128)(2,1)} copy(bf16[12288,768]{1,0:T(8,128)(2,1)} %all-gather.2.cloned.1.call-done) | data formatting | bytes 37748736
  (272 shorter events, 214.7 us)
Async XLA Ops:
  7.2 15.8 %copy-start = (bf16[768,2304]{1,0:T(8,128)(2,1)S(1)}, bf16[768,2304]{1,0:T(8,128)(2,1)}, u32[]{:S(2)}) copy-start(bf16[768,2304]{1,0:T(8,128)(2,1)} %param.13) | copy-start | bytes 10616836
  7.2 695.2 %reduce-scatter.2.cloned.1.call-start = ((), (), s32[]{:S(2)}) async-start(), calls=%async_computation.1 | async-start | bytes 38928384 | tf_op jit(solution)/shard_map/reduce_scatter | solution.py:324
  14.2 50.1 %copy-start.33 = (f32[4,8]{1,0:T(4,128)}, f32[4,8]{1,0:T(4,128)S(1)}, u32[]{:S(2)}) copy-start(f32[4,8]{1,0:T(4,128)S(1)} %reshape_squeeze.3) | copy-start | bytes 388
  49.0 23.3 %collective-permute-start.1 = (bf16[512,1536]{1,0:T(8,128)(2,1)}, bf16[512,1536]{1,0:T(8,128)(2,1)}, u32[]{:S(2)}, u32[]{:S(2)}) collective-permute-start(bf16[512,1536]{1,0:T(8,128)(2,1)} %pad_maximum_fusion.6), channel_id=1, source_target_pairs={{0,16},{1,17},{2,18},{3,19},{4,20},{5,21},{6,22},{7,23},{8,24},{9,... | collective-permute-start | bytes 4718600 | tf_op jit(solution)/shard_map/ppermute | solution.py:25
  128.9 13.4 %slice-start = ((s8[6291456]{0:T(1024)(128)(4,1)}), s8[4194304]{0:T(1024)(128)(4,1)S(1)}, s32[]{:S(2)}) async-start(s8[6291456]{0:T(1024)(128)(4,1)} %bitcast.120), calls=%async_computation.3 | async-start | bytes 8388608
  128.9 13.4 %slice-start.1 = ((s8[6291456]{0:T(1024)(128)(4,1)}), s8[2097152]{0:T(1024)(128)(4,1)S(1)}, s32[]{:S(2)}) async-start(s8[6291456]{0:T(1024)(128)(4,1)} %bitcast.120), calls=%async_computation.4 | async-start | bytes 4194304
  142.4 15.5 %slice-start.7 = ((s8[4718592]{0:T(1024)(128)(4,1)}), s8[4194304]{0:T(1024)(128)(4,1)S(1)}, s32[]{:S(2)}) async-start(s8[4718592]{0:T(1024)(128)(4,1)} %bitcast.157), calls=%async_computation.10 | async-start | bytes 8388608
  145.1 12.9 %copy-start.27 = (bf16[512,768]{1,0:T(8,128)(2,1)}, bf16[512,768]{1,0:T(8,128)(2,1)S(1)}, u32[]{:S(2)}) copy-start(bf16[512,768]{1,0:T(8,128)(2,1)S(1)} %get-tuple-element.122) | copy-start | bytes 2359300
  145.1 40.0 %copy-start.2 = (f32[512,768]{1,0:T(8,128)}, f32[512,768]{1,0:T(8,128)S(1)}, u32[]{:S(2)}) copy-start(f32[512,768]{1,0:T(8,128)S(1)} %get-tuple-element.37) | copy-start | bytes 4718596
  145.5 12.5 %slice-start.8 = ((s8[4718592]{0:T(1024)(128)(4,1)}), s8[524288]{0:T(1024)(128)(4,1)S(1)}, s32[]{:S(2)}) async-start(s8[4718592]{0:T(1024)(128)(4,1)} %bitcast.157), calls=%async_computation.11 | async-start | bytes 1048576
  218.8 10.9 %copy-start.36 = (f32[12,512]{1,0:T(8,128)S(1)}, f32[12,512]{1,0:T(8,128)}, u32[]{:S(2)}) copy-start(f32[12,512]{1,0:T(8,128)} %get-tuple-element.114) | copy-start | bytes 73732
  218.8 10.9 %copy-start.37 = (f32[12,512]{1,0:T(8,128)S(1)}, f32[12,512]{1,0:T(8,128)}, u32[]{:S(2)}) copy-start(f32[12,512]{1,0:T(8,128)} %get-tuple-element.117) | copy-start | bytes 73732
  229.6 23.8 %copy-start.17 = (f32[1024,12,64]{0,2,1:T(8,128)}, f32[1024,12,64]{0,2,1:T(8,128)S(1)}, u32[]{:S(2)}) copy-start(f32[1024,12,64]{0,2,1:T(8,128)S(1)} %fusion.27) | copy-start | bytes 9437188
  229.6 17.6 %copy-start.18 = (bf16[512,12,32]{0,2,1:T(8,128)(2,1)S(1)}, bf16[512,12,32]{0,2,1:T(8,128)(2,1)}, u32[]{:S(2)}) copy-start(bf16[512,12,32]{0,2,1:T(8,128)(2,1)} %get-tuple-element.102) | copy-start | bytes 1179652
  229.6 17.6 %copy-start.19 = (bf16[512,12,32]{0,2,1:T(8,128)(2,1)S(1)}, bf16[512,12,32]{0,2,1:T(8,128)(2,1)}, u32[]{:S(2)}) copy-start(bf16[512,12,32]{0,2,1:T(8,128)(2,1)} %get-tuple-element.103) | copy-start | bytes 1179652
  266.9 38.4 %collective-permute-start.2 = (bf16[512,1536]{0,1:T(8,128)(2,1)}, bf16[512,1536]{0,1:T(8,128)(2,1)}, u32[]{:S(2)}, u32[]{:S(2)}) collective-permute-start(bf16[512,1536]{0,1:T(8,128)(2,1)} %pad_maximum_fusion.7), channel_id=1, source_target_pairs={{16,0},{17,1},{18,2},{19,3},{20,4},{21,5},{22,6},{23,7},{24,8},{25... | collective-permute-start | bytes 4718600 | tf_op jit(solution)/shard_map/ppermute | solution.py:25
  350.9 584.2 %all-gather.2.cloned.1.call-start = ((), (), s32[]{:S(2)}) async-start(), calls=%async_computation.2 | async-start | bytes 19464192 | tf_op jit(solution)/shard_map/all_gather | solution.py:333
  723.6 10.5 %copy-start.8 = (f32[512,768]{1,0:T(8,128)}, f32[512,768]{1,0:T(8,128)S(1)}, u32[]{:S(2)}) copy-start(f32[512,768]{1,0:T(8,128)S(1)} %subtract_multiply_fusion) | copy-start | bytes 4718596
  754.7 83.8 %collective-permute-start = (bf16[512,1536]{1,0:T(8,128)(2,1)}, bf16[512,1536]{1,0:T(8,128)(2,1)}, u32[]{:S(2)}, u32[]{:S(2)}) collective-permute-start(bf16[512,1536]{1,0:T(8,128)(2,1)} %pad_maximum_fusion.5), channel_id=1, source_target_pairs={{0,16},{1,17},{2,18},{3,19},{4,20},{5,21},{6,22},{7,23},{8,24},{9,... | collective-permute-start | bytes 4718600 | tf_op jit(solution)/shard_map/ppermute | solution.py:25
  895.4 13.8 %slice-start.4 = ((s8[6291456]{0:T(1024)(128)(4,1)}), s8[4194304]{0:T(1024)(128)(4,1)S(1)}, s32[]{:S(2)}) async-start(s8[6291456]{0:T(1024)(128)(4,1)} %bitcast.124), calls=%async_computation.7 | async-start | bytes 8388608
  895.4 11.8 %copy-start.59 = (bf16[768,768]{1,0:T(8,128)(2,1)S(1)}, bf16[768,768]{1,0:T(8,128)(2,1)}, u32[]{:S(2)}) copy-start(bf16[768,768]{1,0:T(8,128)(2,1)} %param.14) | copy-start | bytes 3538948
  895.5 13.8 %slice-start.5 = ((s8[6291456]{0:T(1024)(128)(4,1)}), s8[2097152]{0:T(1024)(128)(4,1)S(1)}, s32[]{:S(2)}) async-start(s8[6291456]{0:T(1024)(128)(4,1)} %bitcast.124), calls=%async_computation.8 | async-start | bytes 4194304
  909.3 13.8 %slice-start.9 = ((s8[4718592]{0:T(1024)(128)(4,1)}), s8[4194304]{0:T(1024)(128)(4,1)S(1)}, s32[]{:S(2)}) async-start(s8[4718592]{0:T(1024)(128)(4,1)} %bitcast.159), calls=%async_computation.12 | async-start | bytes 8388608
  911.1 12.0 %slice-start.10 = ((s8[4718592]{0:T(1024)(128)(4,1)}), s8[524288]{0:T(1024)(128)(4,1)S(1)}, s32[]{:S(2)}) async-start(s8[4718592]{0:T(1024)(128)(4,1)} %bitcast.159), calls=%async_computation.13 | async-start | bytes 1048576
  (53 other events, 185.1 us)
Sparse Core Ops, SparseCore 0:
  351.1 351.2 reduce-scatter.1
  708.0 124.6 all-gather.1
where the time goes:
time: 969 us; the launch traced here: 959 us
  waiting for transfers between devices  351 us (36%)
  other arithmetic  220 us (23%)
  matrix products  187 us (19%)
  local copies, waits for them, and re-layouts  135 us (14%)
  blocking collectives  43.2 us (4%)
  between operations  15.1 us (2%)
    reduce_scatter x1, waiting for transfers between devices, on_device(): lax.psum_scatter(flat_local, ('seq', 'wide'), scatter_dimension=0, tiled=...  351 us
    sub x2, other arithmetic, forward_layer(): lifted = jnp.exp(scores - row_top)  68.9 us
    psum x1, blocking collectives, on_device(): lax.psum((gains_local, mixing_local), ('seq', 'wide'))  43.2 us
    unnamed x146, local copies, waits for them, and re-layouts  36.8 us
    dot_general x4, matrix products, right_product(): lax.dot_general(left, right, (((1,), (1,)), ((), ())), preferred_element_...  28.3 us
    reshape x2, local copies, waits for them, and re-layouts, on_device(): grad.reshape(-1, model_width)  28.1 us
    dot_general x2, matrix products, forward_layer(): jnp.einsum('qhd,khd->hqk', queries, keys_all, preferred_element_type=jnp....  26.8 us
    concatenate x1, other arithmetic, on_device(): jnp.concatenate([grad.reshape(-1, model_width) for grad in matrix_grads],...  26.8 us
  transfers between devices with their start and end apart: 5, of which 1 were waited for; matrix products, arithmetic and copies ran while one was open for 25% of the time, Pallas kernels for 0%

commit v1 on v0

--- a/solution.py
+++ b/solution.py
@@ -1,6 +1,10 @@
+import functools
+
 import jax
 import jax.numpy as jnp
 from jax import lax
+from jax.experimental import pallas as pl
+from jax.experimental.pallas import tpu as pltpu
 from jax.sharding import PartitionSpec as P
 
 HEADS = 12
@@ -16,6 +20,7 @@
 adam_epsilon = 1e-08
 weight_decay = 0.1
 learn_rate = 0.01
+MESH = pl.DeviceIdType.MESH
 masked_score = -1e30
 
 
@@ -276,7 +281,332 @@
     return (weight_new, first_new, second_new)
 
 
+def torus(mesh):
+    wide = mesh.shape["wide"]
+    where = [getattr(d, "coords", None) for d in mesh.devices.flat]
+    if all(c is not None for c in where):
+        x, y, z = (len({c[i] for c in where}) for i in range(3))
+        if x * y * z == wide:
+            return z, y, x
+    known = {16: (4, 2, 2), 64: (4, 4, 4)}
+    return known.get(wide, (wide, 1, 1))
+
+
+def sync_kernel(
+    dims, rows, half, lr_consts,
+    grads, small_in, state_in,
+    copy_out, weight_out, first_out, second_out, grad_out, small_out,
+    acc, from_core, from_a0, from_a1, from_b0, from_b1, from_c,
+    state, new_w, new_m, new_v, new_g, low, small_box,
+    load_sem, store_sem, send_sem, recv_sem, small_send, small_recv,
+):
+    nz, ny, nx = dims
+    chunk = 2 * half
+    chunks = rows // chunk
+    s = lax.axis_index("seq")
+    w = lax.axis_index("wide")
+    z, y, x = w // (ny * nx), (w // nx) % ny, w % nx
+
+    def chip(cz, cy, cx):
+        return (s, (cz * ny + cy) * nx + cx)
+
+    core = (1 - s, w)
+    z_peers = [chip((z + d) % nz, y, x) for d in range(1, nz)]
+    y_peers = [chip(z, (y + d) % ny, x) for d in range(1, ny)]
+    x_peers = [chip(z, y, (x + d) % nx) for d in range(1, nx)]
+    peers = [core] + z_peers + y_peers + x_peers
+
+    barrier = pltpu.get_barrier_semaphore()
+    for peer in peers:
+        pl.semaphore_signal(barrier, inc=1, device_id=peer, device_id_type=MESH)
+
+    loads = [
+        pltpu.make_async_copy(
+            grads.at[s, :, :, :, pl.ds(c * chunk, chunk)],
+            acc.at[:, :, :, pl.ds(c * chunk, chunk)],
+            load_sem.at[c],
+        )
+        for c in range(chunks)
+    ]
+    for copy in loads:
+        copy.start()
+    state_load = pltpu.make_async_copy(state_in, state, load_sem.at[chunks])
+    state_load.start()
+    pl.semaphore_wait(barrier, len(peers))
+
+    sends = []
+    counter = [0]
+
+    def remote(src, dst, peer):
+        i = counter[0]
+        counter[0] += 1
+        copy = pltpu.make_async_remote_copy(
+            src, dst, send_sem.at[i], recv_sem.at[i], device_id=peer, device_id_type=MESH
+        )
+        copy.start()
+        sends.append(copy)
+        return copy
+
+    def lo(c):
+        return pl.ds(c * chunk, half)
+
+    def hi(c):
+        return pl.ds(c * chunk + half, half)
+
+    def both(c):
+        return pl.ds(c * chunk, chunk)
+
+    def packed(c):
+        return pl.ds(c * half, half)
+
+    f32 = jnp.float32
+
+    def add_into(count, where, terms):
+        def body(i, carry):
+            ref, index = where(i)
+            total = ref[index].astype(f32)
+            for term_ref, term_index in terms(i):
+                total = total + term_ref[term_index].astype(f32)
+            ref[index] = total.astype(ref.dtype)
+            return carry
+
+        lax.fori_loop(0, count, body, 0)
+
+    def small_step(k, mine, others, count):
+        copies = []
+        for j, peer in enumerate(others):
+            i = small_index[0]
+            small_index[0] += 1
+            copy = pltpu.make_async_remote_copy(
+                small_box.at[k, mine], small_box.at[k, mine], small_send.at[i], small_recv.at[i],
+                device_id=peer, device_id_type=MESH,
+            )
+            copy.start()
+            copies.append(copy)
+        return copies
+
+    def small_sum(k, copies, count):
+        for copy in copies:
+            copy.wait()
+        total = small_box[k, 0]
+        for j in range(1, count):
+            total = total + small_box[k, j]
+        return total
+
+    small_index = [0]
+    axes = [(s, [core], 2), (x, x_peers, nx), (y, y_peers, ny), (z, z_peers, nz)]
+    small_box[0, s] = small_in[...]
+    small_copies = [small_step(0, s, [core], 2)]
+
+    def small_stage(k):
+        total = small_sum(k, small_copies[k], axes[k][2])
+        if k + 1 < len(axes):
+            place, others, count = axes[k + 1]
+            small_box[k + 1, place] = total
+            small_copies.append(small_step(k + 1, place, others, count))
+        else:
+            small_out[...] = total
+
+    state_done = [False]
+    flying = {}
+
+    def stage(k, c):
+        if k == 0:
+            loads[c].wait()
+            for copy in flying[0, c]:
+                copy.wait_recv()
+
+            def where(i):
+                return acc, (i // (ny * nx), (i // nx) % ny, i % nx, both(c))
+
+            def terms(i):
+                return [(from_core, (i // (ny * nx), (i // nx) % ny, i % nx, both(c)))]
+
+            add_into(nz * ny * nx, where, terms)
+            out = []
+            for d in range(1, nx):
+                out.append(remote(
+                    acc.at[:, :, (x + d) % nx, lo(c)], from_a0.at[d - 1, :, :, packed(c)], x_peers[d - 1]))
+            for d in range(1, ny):
+                out.append(remote(
+                    acc.at[:, (y + d) % ny, :, hi(c)], from_a1.at[d - 1, :, :, packed(c)], y_peers[d - 1]))
+            flying[1, c] = out
+        elif k == 1:
+            for copy in flying[1, c]:
+                copy.wait_recv()
+            add_into(
+                nz * ny,
+                lambda i: (acc, (i // ny, i % ny, x, lo(c))),
+                lambda i: [(from_a0, (d, i // ny, i % ny, packed(c))) for d in range(nx - 1)],
+            )
+            add_into(
+                nz * nx,
+                lambda i: (acc, (i // nx, y, i % nx, hi(c))),
+                lambda i: [(from_a1, (d, i // nx, i % nx, packed(c))) for d in range(ny - 1)],
+            )
+            out = []
+            for d in range(1, ny):
+                out.append(remote(
+                    acc.at[:, (y + d) % ny, x, lo(c)], from_b0.at[d - 1, :, packed(c)], y_peers[d - 1]))
+            for d in range(1, nx):
+                out.append(remote(
+                    acc.at[:, y, (x + d) % nx, hi(c)], from_b1.at[d - 1, :, packed(c)], x_peers[d - 1]))
+            flying[2, c] = out
+        elif k == 2:
+            for copy in flying[2, c]:
+                copy.wait_recv()
+            add_into(
+                nz,
+                lambda i: (acc, (i, y, x, lo(c))),
+                lambda i: [(from_b0, (d, i, packed(c))) for d in range(ny - 1)],
+            )
+            add_into(
+                nz,
+                lambda i: (acc, (i, y, x, hi(c))),
+                lambda i: [(from_b1, (d, i, packed(c))) for d in range(nx - 1)],
+            )
+            out = []
+            for d in range(1, nz):
+                out.append(remote(
+                    acc.at[(z + d) % nz, y, x, both(c)], from_c.at[d - 1, both(c)], z_peers[d - 1]))
+            flying[3, c] = out
+        elif k == 3:
+            for copy in flying[3, c]:
+                copy.wait_recv()
+            if not state_done[0]:
+                state_load.wait()
+                state_done[0] = True
+            step = 16
+
+            def body(i, carry):
+                r = pl.ds(c * chunk + i * step, step)
+                total = acc[z, y, x, r].astype(f32)
+                for d in range(nz - 1):
+                    total = total + from_c[d, r].astype(f32)
+                grad = total * lr_consts
+                w_new, m_new, v_new = adam_step((state[0, r], state[1, r], state[2, r]), grad)
+                new_g[r] = grad
+                new_w[r] = w_new
+                new_m[r] = m_new
+                new_v[r] = v_new
+                low[r] = w_new.astype(low.dtype)
+                return carry
+
+            lax.fori_loop(0, chunk // step, body, 0)
+            out = []
+            for peer in z_peers:
+                out.append(remote(low.at[both(c)], copy_out.at[s, z, y, x, both(c)], peer))
+            own = pltpu.make_async_copy(low.at[both(c)], copy_out.at[s, z, y, x, both(c)], store_sem.at[0, c])
+            own.start()
+            for j, (a, b) in enumerate(((new_w, weight_out), (new_m, first_out), (new_v, second_out), (new_g, grad_out))):
+                st = pltpu.make_async_copy(a.at[both(c)], b.at[both(c)], store_sem.at[j + 1, c])
+                st.start()
+                stores.append(st)
+            flying[4, c] = (out, own)
+        elif k == 4:
+            out, own = flying[4, c]
+            own.wait()
+            for copy in out:
+                copy.wait_recv()
+            nxt = []
+            for peer in y_peers:
+                nxt.append(remote(copy_out.at[s, :, y, x, lo(c)], copy_out.at[s, :, y, x, lo(c)], peer))
+            for peer in x_peers:
+                nxt.append(remote(copy_out.at[s, :, y, x, hi(c)], copy_out.at[s, :, y, x, hi(c)], peer))
+            flying[5, c] = nxt
+        elif k == 5:
+            for copy in flying[5, c]:
+                copy.wait_recv()
+            nxt = []
+            for peer in x_peers:
+                nxt.append(remote(copy_out.at[s, :, :, x, lo(c)], copy_out.at[s, :, :, x, lo(c)], peer))
+            for peer in y_peers:
+                nxt.append(remote(copy_out.at[s, :, y, :, hi(c)], copy_out.at[s, :, y, :, hi(c)], peer))
+            flying[6, c] = nxt
+        elif k == 6:
+            for copy in flying[6, c]:
+                copy.wait_recv()
+            flying[7, c] = [
+                remote(copy_out.at[s, :, :, :, both(c)], copy_out.at[s, :, :, :, both(c)], core)]
+        elif k == 7:
+            for copy in flying[7, c]:
+                copy.wait_recv()
+
+    stores = []
+    for c in range(chunks):
+        flying[0, c] = [remote(
+            grads.at[1 - s, :, :, :, both(c)], from_core.at[:, :, :, both(c)], core)]
+    stages = 8
+    for t in range(chunks + stages - 1):
+        for k in reversed(range(stages)):
+            c = t - k
+            if 0 <= c < chunks:
+                stage(k, c)
+        if 1 <= t <= 4:
+            small_stage(t - 1)
+    for copy in sends:
+        copy.wait_send()
+    for copy in stores:
+        copy.wait()
+
+
+def sync_grads(dims, flat_low, small_local, big_state, token_count):
+    nz, ny, nx = dims
+    wide = nz * ny * nx
+    model_width = flat_low.shape[1]
+    rows = big_state.shape[1]
+    half = next(h for h in (48, 32, 16) if rows % (2 * h) == 0)
+    chunks = rows // (2 * half)
+    bf16, f32 = jnp.bfloat16, jnp.float32
+    copies = chunks * (2 + 4 * (nx - 1) + 4 * (ny - 1) + 2 * (nz - 1))
+    small_copies = 1 + (nx - 1) + (ny - 1) + (nz - 1)
+    hbm = pl.BlockSpec(memory_space=pl.ANY)
+    vmem = pl.BlockSpec(memory_space=pltpu.VMEM)
+    state_shape = jax.ShapeDtypeStruct((rows, model_width), f32)
+    small_shape = small_local.shape
+    outs = pl.pallas_call(
+        functools.partial(sync_kernel, dims, rows, half, 1.0 / token_count),
+        out_shape=[
+            jax.ShapeDtypeStruct((2, nz, ny, nx, rows, model_width), bf16),
+            state_shape, state_shape, state_shape, state_shape,
+            jax.ShapeDtypeStruct(small_shape, f32),
+        ],
+        in_specs=[hbm, vmem, hbm],
+        out_specs=[hbm] * 5 + [vmem],
+        scratch_shapes=[
+            pltpu.VMEM((nz, ny, nx, rows, model_width), bf16),
+            pltpu.VMEM((nz, ny, nx, rows, model_width), bf16),
+            pltpu.VMEM((max(nx - 1, 1), nz, ny, rows // 2, model_width), bf16),
+            pltpu.VMEM((max(ny - 1, 1), nz, nx, rows // 2, model_width), bf16),
+            pltpu.VMEM((max(ny - 1, 1), nz, rows // 2, model_width), bf16),
+            pltpu.VMEM((max(nx - 1, 1), nz, rows // 2, model_width), bf16),
+            pltpu.VMEM((max(nz - 1, 1), rows, model_width), bf16),
+            pltpu.VMEM((3, rows, model_width), f32),
+            pltpu.VMEM((rows, model_width), f32),
+            pltpu.VMEM((rows, model_width), f32),
+            pltpu.VMEM((rows, model_width), f32),
+            pltpu.VMEM((rows, model_width), f32),
+            pltpu.VMEM((rows, model_width), bf16),
+            pltpu.VMEM((4, max(2, nx, ny, nz)) + small_shape, f32),
+            pltpu.SemaphoreType.DMA((chunks + 1,)),
+            pltpu.SemaphoreType.DMA((5, chunks)),
+            pltpu.SemaphoreType.DMA((copies,)),
+            pltpu.SemaphoreType.DMA((copies,)),
+            pltpu.SemaphoreType.DMA((small_copies,)),
+            pltpu.SemaphoreType.DMA((small_copies,)),
+        ],
+        compiler_params=pltpu.CompilerParams(
+            collective_id=1, has_side_effects=True, vmem_limit_bytes=56 * 2**20
+        ),
+        name="sync_grads",
+    )(
+        flat_low.reshape(2, nz, ny, nx, rows, model_width), small_local, big_state
+    )
+    return (outs[0].reshape(2 * wide * rows, model_width),) + tuple(outs[1:])
+
+
 def on_device(
+    dims,
     streams,
     cotangent,
     doc_lengths,
@@ -310,27 +640,21 @@
     result, saved = forward_layer(
         stream_values, weights, gain_values, mixing, allowed, cosine, sine_table
     )
-    again_streams, again_weights, again_gains = lax.optimization_barrier(
-        (stream_values, weights, gain_values)
-    )
-    unused, saved = forward_layer(
-        again_streams, again_weights, again_gains, mixing, allowed, cosine, sine_table
-    )
     grad_out = cotangent[0].astype(jnp.float32)
     stream_grad, matrix_grads, gains_local, mixing_local = backward_layer(
         stream_values, grad_out, weights, gain_values, mixing, cosine, sine_table, saved
     )
-    flat_local = jnp.concatenate([grad.reshape(-1, model_width) for grad in matrix_grads], axis=0)
-    summed = lax.psum_scatter(flat_local, ("seq", "wide"), scatter_dimension=0, tiled=True)
-    owned_grads = summed / token_count
-    gains_total, mixing_total = lax.psum((gains_local, mixing_local), ("seq", "wide"))
-    small_grads = (
-        jnp.concatenate([gains_total.T.reshape(-1), mixing_total.reshape(-1)]) / token_count
-    )
-    weight_new, first_new, second_new = adam_step(big_state, owned_grads)
+    flat_low = jnp.concatenate(
+        [grad.astype(jnp.bfloat16).reshape(-1, model_width) for grad in matrix_grads], axis=0
+    )
+    small_local = jnp.concatenate([gains_local.T.reshape(-1), mixing_local.reshape(-1)])
+    small_count = small_local.shape[0]
+    padded = jnp.pad(small_local, (0, -small_count % 1024)).reshape(-1, 128)
+    gathered, weight_new, first_new, second_new, owned_grads, small_total = sync_grads(
+        dims, flat_low, padded, big_state, token_count
+    )
+    small_grads = small_total.reshape(-1)[:small_count] / token_count
     small_weight, small_first, small_second = adam_step(small_state, small_grads)
-    copy_shard = weight_new.astype(jnp.bfloat16)
-    gathered = lax.all_gather(copy_shard, ("seq", "wide"), axis=0, tiled=True)
     gains_copy = small_weight[: 2 * model_width].reshape(2, model_width).T.astype(jnp.bfloat16)
     return (
         result.astype(jnp.bfloat16)[None],
@@ -376,5 +700,5 @@
         P(),
     )
     return jax.shard_map(
-        on_device, mesh=mesh, in_specs=in_specs, out_specs=out_specs, check_vma=False
-    )
+        functools.partial(on_device, torus(mesh)), mesh=mesh, in_specs=in_specs, out_specs=out_specs, check_vma=False
+    )

time: 969 us -> 570 us (0.59)
  waiting for transfers between devices: 351 us -> 0.01 us
  Pallas kernels: 0 us -> 172 us
  other arithmetic: 220 us -> 147 us
  matrix products: 187 us -> 137 us
  blocking collectives: 43.2 us -> 0 us
  local copies, waits for them, and re-layouts: 135 us -> 95.4 us
  between operations: 15.1 us -> 1.56 us
    reduce_scatter x1 -> x0, waiting for transfers between devices: 351 us -> none  [on_device(): lax.psum_scatter(flat_local, ('seq', 'wide'), scatter_dimension=0, tiled=...]
    pallas_call x0 -> x1, Pallas kernels: none -> 172 us  [sync_grads(): pl.pallas_call(functools.partial(sync_kernel, dims, rows, half, 1.0 / tok...]
    psum x1 -> x0, blocking collectives: 43.2 us -> none  [on_device(): lax.psum((gains_local, mixing_local), ('seq', 'wide'))]
    sub x2 -> x1, other arithmetic: 68.9 us -> 34 us  [forward_layer(): lifted = jnp.exp(scores - row_top)]
    dot_general x2 -> x1, matrix products: 26.8 us -> 13.4 us  [forward_layer(): jnp.einsum('qhd,khd->hqk', queries, keys_all, preferred_element_type=jnp....]
    reduce_sum x4 -> x2, other arithmetic: 22.3 us -> 9.81 us  [norm_parts(): centre = jnp.mean(values, axis=-1, keepdims=True)]
    dot_general x2 -> x1, matrix products: 24.4 us -> 12.5 us  [forward_layer(): gate_up = jnp.dot(normed_two, ffn_in, preferred_element_type=jnp.float32)]
    dot_general x2 -> x1, matrix products: 22.7 us -> 11.8 us  [forward_layer(): jnp.einsum('hqk,khd->qhd', attend_low, values_all, preferred_element_type...]
  transfers between devices with their start and end apart: 5 -> 2, of which waited for: 1 -> 0; matrix products, arithmetic and copies ran while one was open for 25% -> 8% of each run, Pallas kernels for 0% -> 0%
where the time goes in v1:
time: 570 us; the launch traced here: 559 us
  Pallas kernels  172 us (30%)
  other arithmetic  147 us (26%)
  matrix products  137 us (24%)
  local copies, waits for them, and re-layouts  95.4 us (17%)
    pallas_call x1, Pallas kernels, sync_grads(): pl.pallas_call(functools.partial(sync_kernel, dims, rows, half, 1.0 / tok...  172 us
    unnamed x123, local copies, waits for them, and re-layouts  41.1 us
    sub x1, other arithmetic, forward_layer(): lifted = jnp.exp(scores - row_top)  34 us
    dot_general x4, matrix products, right_product(): lax.dot_general(left, right, (((1,), (1,)), ((), ())), preferred_element_...  27.4 us
    concatenate x1, other arithmetic, on_device(): jnp.concatenate([grad.astype(jnp.bfloat16).reshape(-1, model_width) for g...  25 us
    dot_general x4, matrix products, left_product(): lax.dot_general(left, right, (((0,), (0,)), ((), ())), preferred_element_...  24 us
    reshape x2, local copies, waits for them, and re-layouts, on_device(): grad.astype(jnp.bfloat16).reshape(-1, model_width)  20.8 us
    dot_general x1, matrix products, backward_layer(): jnp.einsum('qhd,khd->hqk', context_grad, values_all, preferred_element_ty...  17.4 us
  transfers between devices with their start and end apart: 2, of which 0 were waited for; matrix products, arithmetic and copies ran while one was open for 8% of the time, Pallas kernels for 0%

profile of v1, /device:TPU:0, one launch (start us, length us, event | category | flops | bytes accessed | tf_op | source)
XLA Modules:
  0.0 559.0 jit_solution(16735808953231031236)
XLA Ops:
  3.1 7.2 %multiply_reduce_fusion.10 = (f32[512]{0:T(512)S(1)}, f32[512,768]{1,0:T(8,128)S(1)}) fusion(bf16[1,512,4,768]{3,2,1,0:T(4,128)(2,1)} %param.10, f32[4]{0:T(128)S(1)} %get-tuple-element.59), kind=kLoop, calls=%fused_computation.41 | loop fusion | flops 5897728 | bytes 4720656 | tf_op jit(solution)/shard_map/reduce_sum | solution.py:71
  44.5 7.9 %multiply_reduce_fusion.3 = f32[512,4,768]{2,0,1:T(8,128)} fusion(f32[4,4]{1,0:T(4,128)S(1)} %bitcast.114, f32[512,4,768]{2,0,1:T(8,128)} %copy.47), kind=kLoop, calls=%fused_computation.7 | loop fusion | flops 11010048 | bytes 12582976 | tf_op jit(solution)/shard_map/reduce_sum | solution.py:104
  61.5 13.4 %fusion.23 = f32[12,512,1024]{2,1,0:T(8,128)} fusion(bf16[1024,12,64]{0,2,1:T(8,128)(2,1)} %bitcast.97, bf16[512,12,32]{0,2,1:T(8,128)(2,1)} %get-tuple-element.80, bf16[512,12,32]{0,2,1:T(8,128)(2,1)} %get-tuple-element.79), kind=kOutput, calls=%fused_computation.91 | convolution fusion | flops 806879232 | bytes 27525120 | tf_op jit(solution)/shard_map/qhd,khd->hqk/dot_general | solution.py:122
  74.9 34.0 %fusion.43 = (f32[12,512]{1,0:T(8,128)}, f32[12,512,1024]{2,1,0:T(8,128)}) fusion(f32[12,512,1024]{2,1,0:T(8,128)} %fusion.23, pred[512,1024]{1,0:T(8,128)(4,1)} %compare_and_fusion), kind=kOutput, calls=%fused_computation.150 | output fusion | flops 37749760 | bytes 50880512 | tf_op jit(solution)/shard_map/sub | solution.py:127
  109.0 11.8 %fusion.19 = bf16[12,64,512]{2,1,0:T(8,128)(2,1)} fusion(bf16[1024,12,64]{0,2,1:T(8,128)(2,1)} %bitcast.106, f32[12,512,1024]{2,1,0:T(8,128)} %get-tuple-element.90, f32[12,512]{1,0:T(8,128)} %get-tuple-element.89), kind=kOutput, calls=%fused_computation.75 | convolution fusion | flops 818282496 | bytes 27549696 | tf_op jit(solution)/shard_map/hqk,khd->qhd/dot_general | solution.py:130
  126.3 12.5 %fusion.40 = f32[512,6144]{1,0:T(8,128)} fusion(bf16[768,6144]{1,0:T(8,128)(2,1)} %param.15, f32[512,768]{1,0:T(8,128)S(1)} %get-tuple-element.37, f32[768]{0:T(1024)S(1)} %get-tuple-element.55, f32[512]{0:T(512)S(1)} %add_rsqrt_fusion, f32[512]{0:T(512)S(1)} %broadcast_multiply_fusion.4), kind=kOutput, calls=%fused_computation.147 | convolution fusion | flops 4833411072 | bytes 23600128 | tf_op jit(solution)/shard_map/dot_general | solution.py:137
  138.9 9.6 %multiply_convert_fusion.2 = (bf16[512,3072]{1,0:T(8,128)(2,1)}, bf16[512,3072]{1,0:T(8,128)(2,1)}, bf16[512,3072]{1,0:T(8,128)(2,1)S(1)}) fusion(f32[512,6144]{1,0:T(8,128)} %fusion.40, bf16[512,768]{1,0:T(8,128)(2,1)S(1)} %get-tuple-element.95, bf16[3072,768]{1,0:T(8,128)(2,1)S(1)} %bitcast.124), kind=kOutput, calls=%fused_computation.31 | convolution fusion | flops 2441084928 | bytes 27525120 | tf_op jit(solution)/shard_map/dot_general | solution.py:86
  154.0 13.0 %multiply_reduce_fusion.12 = (f32[768]{0:T(1024)}, f32[512]{0:T(512)S(1)}, f32[512]{0:T(512)S(1)}, f32[512,768]{1,0:T(8,128)}) fusion(f32[512,768]{1,0:T(8,128)} %copy-done.5, f32[512]{0:T(512)S(1)} %add_rsqrt_fusion, f32[512]{0:T(512)S(1)} %broadcast_multiply_fusion.4, f32[768]{0:T(1024)S(1)} %get-tuple-element.55, bf16[768,6144]{1,0:T(8,128)(2,1)} %param.15, ...), kind=kOutput, calls=%fused_computation.60 | convolution fusion | flops 4847564800 | bytes 18888704 | tf_op jit(solution)/shard_map/dot_general | solution.py:86
  169.8 10.9 %multiply_reduce_fusion.5 = (f32[4]{0:T(128)}, bf16[512,768]{1,0:T(8,128)(2,1)S(1)}, f32[4]{0:T(128)}, f32[4]{0:T(128)}, f32[512,4,768]{2,0,1:T(8,128)}) fusion(f32[512,768]{1,0:T(8,128)S(1)} %fusion.44, f32[512,768]{1,0:T(8,128)S(1)} %subtract_multiply_fusion.1, f32[4]{0:T(128)S(1)} %copy-done.43, bf16[1,512,4,768]{3,2,1,0:T(4,128)(2,1)S(1)} %copy-done.12, ...), kind=kLoop, calls=%fused_computation.27 | loop fusion | flops 20054004 | bytes 21233744 | tf_op jit(solution)/shard_map/reduce_sum | solution.py:211
  185.6 11.7 %fusion.15 = f32[1024,12,64]{0,2,1:T(8,128)} fusion(bf16[512,12,64]{0,2,1:T(8,128)(2,1)} %bitcast.112, f32[12,512,1024]{2,1,0:T(8,128)} %get-tuple-element.90, f32[12,512]{1,0:T(8,128)} %get-tuple-element.89), kind=kOutput, calls=%fused_computation.51 | convolution fusion | flops 817889280 | bytes 29122560 | tf_op jit(solution)/shard_map/hqk,qhd->khd/dot_general | solution.py:219
  197.3 17.4 %multiply_reduce_fusion.1 = (f32[12,512]{1,0:T(8,128)}, f32[12,512,1024]{2,1,0:T(8,128)}) fusion(f32[12,512,1024]{2,1,0:T(8,128)} %get-tuple-element.90, f32[12,512]{1,0:T(8,128)} %get-tuple-element.89, bf16[512,12,64]{0,2,1:T(8,128)(2,1)} %bitcast.113, bf16[1024,12,64]{0,2,1:T(8,128)(2,1)} %bitcast.107), kind=kOutput, calls=%fused_computation.3 | convolution fusion | flops 824174592 | bytes 52740096 | tf_op jit(solution)/shard_map/qhd,khd->hqk/dot_general | solution.py:216
  214.7 16.6 %multiply_convert_fusion = bf16[12,512,1024]{2,1,0:T(8,128)(2,1)S(1)} fusion(f32[12,512,1024]{2,1,0:T(8,128)} %get-tuple-element.93, f32[12,512]{1,0:T(8,128)} %get-tuple-element.92, f32[12,512,1024]{2,1,0:T(8,128)} %get-tuple-element.90, f32[12,512]{1,0:T(8,128)} %get-tuple-element.89), kind=kLoop, calls=%fused_computation.2 | loop fusion | flops 25165824 | bytes 62963712 | tf_op jit(solution)/shard_map/convert_element_type | solution.py:223
  239.7 9.8 %multiply_bitcast_fusion.1 = f32[512,12,64]{0,2,1:T(8,128)} fusion(bf16[1024,12,64]{0,2,1:T(8,128)(2,1)S(1)} %bitcast.98, bf16[12,512,1024]{2,1,0:T(8,128)(2,1)} %copy-done.1), kind=kOutput, calls=%fused_computation.64 | convolution fusion | flops 805699584 | bytes 15728640 | tf_op jit(solution)/shard_map/hqk,khd->qhd/dot_general | solution.py:224
  249.4 11.1 %convolution_convert_fusion = bf16[768,6144]{1,0:T(8,128)(2,1)} fusion(bf16[512,3072]{1,0:T(8,128)(2,1)} %get-tuple-element.66, bf16[512,3072]{1,0:T(8,128)(2,1)} %get-tuple-element.65, f32[512,768]{1,0:T(8,128)S(1)} %copy-done.7, f32[768]{0:T(1024)S(1)} %get-tuple-element.55, f32[512]{0:T(512)S(1)} %add_rsqrt_fusion, f32[512]{0:T(512)S(1)} %broadcast_multiply_fusion.4), kind=kOutput, calls=%fused_computation.14 | convolution fusion | flops 4850712576 | bytes 17308672 | tf_op jit(solution)/shard_map/dot_general | solution.py:92
  262.8 4.1 copy.59
  269.6 14.2 %reshape.341 = bf16[6144,768]{1,0:T(8,128)(2,1)} reshape(bf16[768,6144]{1,0:T(8,128)(2,1)} %convolution_convert_fusion) | data formatting | bytes 18874368 | tf_op jit(solution)/shard_map/reshape | solution.py:648
  285.3 7.0 %convolution_convert_fusion.1 = bf16[3072,768]{1,0:T(8,128)(2,1)} fusion(bf16[512,3072]{1,0:T(8,128)(2,1)} %copy-done.53, bf16[512,768]{1,0:T(8,128)(2,1)} %copy-done.25), kind=kOutput, calls=%fused_computation.43 | convolution fusion | flops 2418278400 | bytes 8650752 | tf_op jit(solution)/shard_map/dot_general | solution.py:92
  292.3 9.3 %multiply_reduce_fusion = (f32[4,4]{1,0:T(4,128)S(1)}, f32[512,4,768]{2,0,1:T(8,128)S(1)}) fusion(f32[512,4,768]{2,0,1:T(8,128)} %get-tuple-element.68, f32[512,4,768]{2,0,1:T(8,128)} %copy.47, f32[4,4]{1,0:T(4,128)S(1)} %bitcast.115), kind=kLoop, calls=%fused_computation.1 | loop fusion | flops 23592944 | bytes 18874496 | tf_op jit(solution)/shard_map/reduce_sum | solution.py:252
  309.9 4.1 convolution_convert_fusion.2
  320.6 4.3 copy.60
  324.9 6.6 %reshape.340 = bf16[2304,768]{1,0:T(8,128)(2,1)} reshape(bf16[768,2304]{1,0:T(8,128)(2,1)} %convolution_convert_fusion.2) | data formatting | bytes 7077888 | tf_op jit(solution)/shard_map/reshape | solution.py:648
  337.4 25.0 %pad_maximum_fusion = bf16[12288,768]{1,0:T(8,128)(2,1)} fusion(bf16[3072,768]{1,0:T(8,128)(2,1)} %convolution_convert_fusion.1, bf16[6144,768]{1,0:T(8,128)(2,1)} %reshape.341, bf16[768,768]{1,0:T(8,128)(2,1)} %convolution_convert_fusion.3, bf16[2304,768]{1,0:T(8,128)(2,1)} %reshape.340), kind=kLoop, calls=%fused_computation.9 | loop fusion | flops 75497472 | bytes 37748736 | tf_op jit(solution)/shard_map/concatenate | solution.py:647
  362.5 172.3 %sync_grads.1 = (bf16[2,4,2,2,384,768]{5,4,3,2,1,0:T(8,128)(2,1)}, f32[384,768]{1,0:T(8,128)}, f32[384,768]{1,0:T(8,128)}, f32[384,768]{1,0:T(8,128)}, f32[384,768]{1,0:T(8,128)}, /*index=5*/f32[16,128]{1,0:T(8,128)}) custom-call(bf16[2,4,2,2,384,768]{5,4,3,2,1,0:T(8,128)(2,1)} %bitcast.96, f32[16,128]{1,0:T(8,128)} %fusion.29.small_in, f32[3,384,768]{2,1,0:T(8,128)} %state_in.1), custom_call_target="tpu_custom_call" | custom-call | tf_op jit(solution)/shard_map/sync_grads/pallas_call | solution.py:567
  542.3 16.5 %copy.77 = bf16[12288,768]{1,0:T(8,128)(2,1)} copy(bf16[12288,768]{1,0:T(8,128)(2,1)} %bitcast.99) | data formatting | bytes 37748736
  (209 shorter events, 107.2 us)
Async XLA Ops:
  0.6 10.0 %copy-start = (bf16[768,2304]{1,0:T(8,128)(2,1)S(1)}, bf16[768,2304]{1,0:T(8,128)(2,1)}, u32[]{:S(2)}) copy-start(bf16[768,2304]{1,0:T(8,128)(2,1)} %param.13) | copy-start | bytes 10616836
  1.6 42.9 %copy-start.30 = (f32[4,8]{1,0:T(4,128)}, f32[4,8]{1,0:T(4,128)S(1)}, u32[]{:S(2)}) copy-start(f32[4,8]{1,0:T(4,128)S(1)} %reshape_squeeze.3) | copy-start | bytes 388
  2.4 7.9 %copy-start.44 = (f32[4]{0:T(128)}, f32[4]{0:T(128)S(1)}, u32[]{:S(2)}) copy-start(f32[4]{0:T(128)S(1)} %get-tuple-element.59) | copy-start | bytes 52
  33.0 19.3 %collective-permute-start = (bf16[512,1536]{1,0:T(8,128)(2,1)}, bf16[512,1536]{1,0:T(8,128)(2,1)}, u32[]{:S(2)}, u32[]{:S(2)}) collective-permute-start(bf16[512,1536]{1,0:T(8,128)(2,1)} %pad_maximum_fusion.5), channel_id=1, source_target_pairs={{0,16},{1,17},{2,18},{3,19},{4,20},{5,21},{6,22},{7,23},{8,24},{9,... | collective-permute-start | bytes 4718600 | tf_op jit(solution)/shard_map/ppermute | solution.py:30
  109.0 14.3 %slice-start = ((s8[6291456]{0:T(1024)(128)(4,1)}), s8[4194304]{0:T(1024)(128)(4,1)S(1)}, s32[]{:S(2)}) async-start(s8[6291456]{0:T(1024)(128)(4,1)} %bitcast.94), calls=%async_computation | async-start | bytes 8388608
  109.0 14.3 %slice-start.1 = ((s8[6291456]{0:T(1024)(128)(4,1)}), s8[2097152]{0:T(1024)(128)(4,1)S(1)}, s32[]{:S(2)}) async-start(s8[6291456]{0:T(1024)(128)(4,1)} %bitcast.94), calls=%async_computation.1 | async-start | bytes 4194304
  123.3 15.5 %slice-start.4 = ((s8[4718592]{0:T(1024)(128)(4,1)}), s8[4194304]{0:T(1024)(128)(4,1)S(1)}, s32[]{:S(2)}) async-start(s8[4718592]{0:T(1024)(128)(4,1)} %bitcast.123), calls=%async_computation.4 | async-start | bytes 8388608
  126.0 12.9 %copy-start.5 = (f32[512,768]{1,0:T(8,128)}, f32[512,768]{1,0:T(8,128)S(1)}, u32[]{:S(2)}) copy-start(f32[512,768]{1,0:T(8,128)S(1)} %get-tuple-element.37) | copy-start | bytes 4718596
  126.0 12.8 %copy-start.25 = (bf16[512,768]{1,0:T(8,128)(2,1)}, bf16[512,768]{1,0:T(8,128)(2,1)S(1)}, u32[]{:S(2)}) copy-start(bf16[512,768]{1,0:T(8,128)(2,1)S(1)} %get-tuple-element.95) | copy-start | bytes 2359300
  126.3 12.5 %slice-start.5 = ((s8[4718592]{0:T(1024)(128)(4,1)}), s8[524288]{0:T(1024)(128)(4,1)S(1)}, s32[]{:S(2)}) async-start(s8[4718592]{0:T(1024)(128)(4,1)} %bitcast.123), calls=%async_computation.5 | async-start | bytes 1048576
  154.0 13.0 %copy-start.6 = (f32[512,768]{1,0:T(8,128)S(1)}, f32[512,768]{1,0:T(8,128)}, u32[]{:S(2)}) copy-start(f32[512,768]{1,0:T(8,128)} %copy-done.5) | copy-start | bytes 4718596
  169.8 11.8 %copy-start.50 = (bf16[768,768]{1,0:T(8,128)(2,1)S(1)}, bf16[768,768]{1,0:T(8,128)(2,1)}, u32[]{:S(2)}) copy-start(bf16[768,768]{1,0:T(8,128)(2,1)} %param.14) | copy-start | bytes 3538948
  214.7 16.6 %copy-start.18 = (bf16[512,12,32]{0,2,1:T(8,128)(2,1)S(1)}, bf16[512,12,32]{0,2,1:T(8,128)(2,1)}, u32[]{:S(2)}) copy-start(bf16[512,12,32]{0,2,1:T(8,128)(2,1)} %get-tuple-element.79) | copy-start | bytes 1179652
  214.7 16.7 %copy-start.19 = (bf16[512,12,32]{0,2,1:T(8,128)(2,1)S(1)}, bf16[512,12,32]{0,2,1:T(8,128)(2,1)}, u32[]{:S(2)}) copy-start(bf16[512,12,32]{0,2,1:T(8,128)(2,1)} %get-tuple-element.80) | copy-start | bytes 1179652
  239.7 9.8 %copy-start.7 = (f32[512,768]{1,0:T(8,128)S(1)}, f32[512,768]{1,0:T(8,128)}, u32[]{:S(2)}) copy-start(f32[512,768]{1,0:T(8,128)} %copy-done.5) | copy-start | bytes 4718596
  249.4 11.1 %copy-start.24 = (bf16[512,768]{1,0:T(8,128)(2,1)S(1)}, bf16[512,768]{1,0:T(8,128)(2,1)}, u32[]{:S(2)}) copy-start(bf16[512,768]{1,0:T(8,128)(2,1)} %copy-done.23) | copy-start | bytes 2359300
  249.4 11.1 %copy-start.52 = (bf16[12,64,512]{2,1,0:T(8,128)(2,1)S(1)}, bf16[12,64,512]{2,1,0:T(8,128)(2,1)}, u32[]{:S(2)}) copy-start(bf16[12,64,512]{2,1,0:T(8,128)(2,1)} %fusion.19) | copy-start | bytes 2359300
  268.2 15.6 %copy-start.49 = (f32[4]{0:T(128)S(1)}, f32[4]{0:T(128)}, u32[]{:S(2)}) copy-start(f32[4]{0:T(128)} %get-tuple-element.40) | copy-start | bytes 52
  268.2 16.5 %copy-start.48 = (f32[4]{0:T(128)S(1)}, f32[4]{0:T(128)}, u32[]{:S(2)}) copy-start(f32[4]{0:T(128)} %get-tuple-element.49) | copy-start | bytes 52
  268.2 17.1 %copy-start.47 = (f32[768]{0:T(1024)S(1)}, f32[768]{0:T(1024)}, u32[]{:S(2)}) copy-start(f32[768]{0:T(1024)} %get-tuple-element.44) | copy-start | bytes 9220
  268.2 33.5 %collective-permute-start.1 = (bf16[512,1536]{0,1:T(8,128)(2,1)}, bf16[512,1536]{0,1:T(8,128)(2,1)}, u32[]{:S(2)}, u32[]{:S(2)}) collective-permute-start(bf16[512,1536]{0,1:T(8,128)(2,1)} %pad_maximum_fusion.6), channel_id=1, source_target_pairs={{16,0},{17,1},{18,2},{19,3},{20,4},{21,5},{22,6},{23,7},{24,8},{25... | collective-permute-start | bytes 4718600 | tf_op jit(solution)/shard_map/ppermute | solution.py:30
  362.4 172.4 %copy-start.32 = (f32[1568]{0:T(1024)S(1)}, f32[1568]{0:T(1024)}, u32[]{:S(2)}) copy-start(f32[1568]{0:T(1024)} %get-tuple-element.52) | copy-start | bytes 18820
  362.4 172.4 %copy-start.33 = (f32[1568]{0:T(1024)S(1)}, f32[1568]{0:T(1024)}, u32[]{:S(2)}) copy-start(f32[1568]{0:T(1024)} %get-tuple-element.53) | copy-start | bytes 18820
  362.4 172.4 %copy-start.34 = (f32[1568]{0:T(1024)S(1)}, f32[1568]{0:T(1024)}, u32[]{:S(2)}) copy-start(f32[1568]{0:T(1024)} %get-tuple-element.54) | copy-start | bytes 18820
  (38 other events, 114.8 us)

commit v2 on v1

--- a/solution.py
+++ b/solution.py
@@ -2,6 +2,7 @@
 
 import jax
 import jax.numpy as jnp
+import numpy as np
 from jax import lax
 from jax.experimental import pallas as pl
 from jax.experimental.pallas import tpu as pltpu
@@ -281,6 +282,1174 @@
     return (weight_new, first_new, second_new)
 
 
+def rope_constants(length, head_size):
+    half_size = head_size // 2
+    exponent = np.arange(half_size, dtype=np.float32) * np.float32(2.0 / head_size)
+    frequency = np.power(np.float64(rope_base), -exponent.astype(np.float64)).astype(np.float32)
+    angles = np.arange(length, dtype=np.float32)[:, None] * frequency[None, :]
+    cosine = np.cos(angles.astype(np.float64)).astype(np.float32)
+    sine = np.sin(angles.astype(np.float64)).astype(np.float32)
+    return np.tile(cosine, (1, 4)), np.tile(np.concatenate([-sine, sine], axis=1), (1, 2))
+
+
+def swapped(values):
+    lane = lax.broadcasted_iota(jnp.int32, values.shape, 1)
+    return jnp.where(lane % HD < HD // 2, pltpu.roll(values, 128 - HD // 2, 1), pltpu.roll(values, HD // 2, 1))
+
+
+def unpacked(block):
+    count = block.shape[0]
+    flat = block.reshape(count * NS, block.shape[2])
+    row = lax.broadcasted_iota(jnp.int32, (count * NS, count * NS), 0)
+    col = lax.broadcasted_iota(jnp.int32, (count * NS, count * NS), 1)
+    pick = ((row % count) * NS + row // count == col).astype(jnp.bfloat16)
+    out = jnp.dot(pick, flat, preferred_element_type=jnp.float32)
+    return [out[i * count : (i + 1) * count] for i in range(NS)]
+
+
+def packed_streams(parts):
+    count = parts[0].shape[0]
+    flat = jnp.concatenate(parts, axis=0)
+    row = lax.broadcasted_iota(jnp.int32, (count * NS, count * NS), 0)
+    col = lax.broadcasted_iota(jnp.int32, (count * NS, count * NS), 1)
+    place = ((col % count) * NS + col // count == row).astype(jnp.bfloat16)
+    out = jnp.dot(place, flat, preferred_element_type=jnp.float32).astype(jnp.bfloat16)
+    return out.reshape(count, NS, parts[0].shape[1])
+
+
+def normal_of(values):
+    centre = jnp.mean(values, axis=-1, keepdims=True)
+    centred = values - centre
+    scaling = lax.rsqrt(jnp.mean(centred * centred, axis=-1, keepdims=True) + norm_epsilon)
+    return centred * scaling, scaling
+
+
+def nt(left, right):
+    return lax.dot_general(left, right, (((1,), (1,)), ((), ())), preferred_element_type=jnp.float32)
+
+
+def tn(left, right):
+    return lax.dot_general(left, right, (((0,), (0,)), ((), ())), preferred_element_type=jnp.float32)
+
+
+def nn(left, right):
+    return jnp.dot(left, right, preferred_element_type=jnp.float32)
+
+
+def doc_starts(docs, place):
+    start = jnp.zeros(place.shape, jnp.int32)
+    bound = 0
+    for j in range(docs.shape[1] - 1):
+        bound = bound + docs[0, j]
+        start = jnp.where(place >= bound, bound, start)
+    return start
+
+
+EIGHTH = 128
+
+
+def q_blocks(s):
+    if s == 0:
+        return [(0, 0, 1, False)] + [(i, 1, i, True) for i in (1, 2, 3)]
+    return [(i - 4, 1, i, True) for i in (4, 5, 6)] + [(3, 7, 1, False)]
+
+
+def block_mask(docs, s, block):
+    row, key, count, single = block
+    shape = (EIGHTH, 2 * EIGHTH)
+    place = lax.broadcasted_iota(jnp.int32, shape, 1) % EIGHTH
+    at = lax.broadcasted_iota(jnp.int32, shape, 0)
+    if single:
+        return at <= place
+    first = (4 * s + row) * EIGHTH
+    start = doc_starts(docs, place + first)
+    return (at + first >= start) & (at <= place)
+
+
+def two_heads(pair):
+    lane = lax.broadcasted_iota(jnp.int32, pair.shape, 1)
+    none = jnp.zeros_like(pair)
+    return jnp.concatenate([jnp.where(lane < HD, pair, none), jnp.where(lane < HD, none, pair)], axis=0)
+
+
+def one_pair(stacked):
+    rows = stacked.shape[1] // 2
+    return jnp.concatenate([stacked[:HD, :rows], stacked[HD:, rows:]], axis=0).T
+
+
+def masked_scores(k2, qs, allow):
+    scores = nt(k2, qs)
+    keys = scores.shape[0]
+    last = jnp.where(allow, scores[keys - EIGHTH :], masked_score)
+    if keys == EIGHTH:
+        return last
+    return jnp.concatenate([scores[: keys - EIGHTH], last], axis=0)
+
+
+def forward_kernel(
+    docs, small, streams, attn_in, attn_out, gains, cos_table, sin_table,
+    normed, queries, keys, values, context, lse, first_out, ffn_read, cos_own, sin_own,
+    stream_out, send_sem, recv_sem,
+):
+    f32, bf16 = jnp.float32, jnp.bfloat16
+    rows, width = normed.shape
+    s = lax.axis_index("seq")
+    w = lax.axis_index("wide")
+    partner = (1 - s, w)
+    barrier = pltpu.get_barrier_semaphore()
+    pl.semaphore_signal(barrier, inc=1, device_id=partner, device_id_type=MESH)
+
+    base = 2 * width
+    mix = [[small[0, base + i * 2 * NS + j] for j in range(2 * NS)] for i in range(NS)]
+
+    def norm_block(i, carry):
+        r = pl.ds(i * 64, 64)
+        parts = unpacked(streams[r])
+        branch = parts[0] * mix[0][NS]
+        for k in range(1, NS):
+            branch = branch + parts[k] * mix[k][NS]
+        for k in range(NS):
+            stream_out[k, r] = parts[k].astype(bf16)
+        normal, _ = normal_of(branch)
+        normed[r] = (normal * gains[0:1].astype(f32)).astype(bf16)
+        return carry
+
+    lax.fori_loop(0, rows // 64, norm_block, 0)
+
+    def tables(first_special, special, plain_rows, plain_from):
+        place = lax.broadcasted_iota(jnp.int32, (EIGHTH, EIGHTH), 0) + first_special
+        start = doc_starts(docs, place)
+        lane = lax.broadcasted_iota(jnp.int32, (EIGHTH, EIGHTH), 1)
+        pick = (place - start == lane).astype(f32)
+        for table, own in ((cos_table, cos_own), (sin_table, sin_own)):
+            own[special] = jnp.dot(pick, table[:EIGHTH], precision=lax.Precision.HIGHEST, preferred_element_type=f32)
+            own[plain_rows] = table[plain_from]
+
+    @pl.when(s == 0)
+    def _():
+        tables(0, pl.ds(0, EIGHTH), pl.ds(EIGHTH, 3 * EIGHTH), pl.ds(0, 3 * EIGHTH))
+
+    @pl.when(s == 1)
+    def _():
+        tables(7 * EIGHTH, pl.ds(3 * EIGHTH, EIGHTH), pl.ds(0, 3 * EIGHTH), pl.ds(3 * EIGHTH, 3 * EIGHTH))
+
+    own_rows = pl.ds(s * rows, rows)
+
+    def rotated(dest, dest_rows, offset):
+        def body(j, carry):
+            cols = pl.ds(pl.multiple_of(j * 256, 256), 256)
+            source = pl.ds(pl.multiple_of(offset + j * 256, 256), 256)
+            part = nn(normed[...], attn_in[:, source])
+            cosine, sine = cos_own[...], sin_own[...]
+            halves = []
+            for k in range(2):
+                piece = part[:, k * 128 : (k + 1) * 128]
+                halves.append(piece * cosine + swapped(piece) * sine)
+            dest[dest_rows, cols] = jnp.concatenate(halves, axis=1).astype(bf16)
+            return carry
+
+        lax.fori_loop(0, width // 256, body, 0)
+
+    def plain(j, carry):
+        cols = pl.ds(pl.multiple_of(j * 256, 256), 256)
+        source = pl.ds(pl.multiple_of(2 * width + j * 256, 256), 256)
+        values[own_rows, cols] = nn(normed[...], attn_in[:, source]).astype(bf16)
+        return carry
+
+    lax.fori_loop(0, width // 256, plain, 0)
+    rotated(keys, own_rows, width)
+    pl.semaphore_wait(barrier, 1)
+
+    shared = pl.ds(EIGHTH, 3 * EIGHTH)
+    copies = [
+        pltpu.make_async_remote_copy(
+            ref.at[shared], ref.at[shared], send_sem.at[i], recv_sem.at[i],
+            device_id=partner, device_id_type=MESH,
+        )
+        for i, ref in enumerate((keys, values))
+    ]
+
+    @pl.when(s == 0)
+    def _():
+        for copy in copies:
+            copy.start()
+
+    rotated(queries, pl.ds(0, rows), 0)
+
+    def attend(side):
+        for bi, block in enumerate(q_blocks(side)):
+            row, key, count, single = block
+            r = pl.ds(row * EIGHTH, EIGHTH)
+            kr = pl.ds(key * EIGHTH, count * EIGHTH)
+            allow = block_mask(docs, side, block)
+
+            def pair(hp, carry):
+                cols = pl.ds(pl.multiple_of(hp * 128, 128), 128)
+                qs = two_heads(queries[r, cols]) * HD ** (-0.5)
+                scores = masked_scores(keys[kr, cols], qs, allow)
+                top = jnp.max(scores, axis=0, keepdims=True)
+                lifted = jnp.exp(scores - top)
+                total = jnp.sum(lifted, axis=0, keepdims=True)
+                low = (lifted * (1.0 / total)).astype(bf16)
+                context[r, cols] = one_pair(tn(values[kr, cols], low)).astype(bf16)
+                lse[pl.ds(bi * 8 + hp, 1), :] = top + jnp.log(total)
+                return carry
+
+            lax.fori_loop(0, width // 128, pair, 0)
+
+    @pl.when(s == 0)
+    def _():
+        attend(0)
+        for copy in copies:
+            copy.wait_send()
+
+    @pl.when(s == 1)
+    def _():
+        for copy in copies:
+            copy.wait_recv()
+        attend(1)
+
+    carry_first = sum(mix[j][NS + 1] * mix[j][NS + 2] for j in range(NS))
+    carry_stream = [sum(mix[i][j] * mix[j][NS + 2] for j in range(NS)) for i in range(NS)]
+
+    def out_block(j, carry):
+        cols = pl.ds(pl.multiple_of(j * 256, 256), 256)
+        first = nn(context[...], attn_out[:, cols])
+        first_out[:, cols] = first
+        total = first * carry_first
+        for i in range(NS):
+            total = total + stream_out[i, :, cols].astype(f32) * carry_stream[i]
+        ffn_read[:, cols] = total
+        return carry
+
+    lax.fori_loop(0, width // 256, out_block, 0)
+
+
+def forward_part(streams, docs, small_state, weights, gains):
+    attn_in, attn_out = weights
+    rows, width = streams.shape[0], attn_out.shape[0]
+    bf16, f32 = jnp.bfloat16, jnp.float32
+    cos_table, sin_table = rope_constants(6 * EIGHTH, HD)
+    smem = pl.BlockSpec(memory_space=pltpu.SMEM)
+    vmem = pl.BlockSpec(memory_space=pltpu.VMEM)
+    shape = jax.ShapeDtypeStruct
+    return pl.pallas_call(
+        forward_kernel,
+        out_shape=[
+            shape((rows, width), bf16), shape((rows, width), bf16),
+            shape((2 * rows, width), bf16), shape((2 * rows, width), bf16),
+            shape((rows, width), bf16), shape((32, 2 * EIGHTH), f32),
+            shape((rows, width), f32), shape((rows, width), f32),
+            shape((rows, 128), f32), shape((rows, 128), f32),
+        ],
+        in_specs=[smem, smem] + [vmem] * 6,
+        out_specs=[vmem] * 10,
+        scratch_shapes=[pltpu.VMEM((NS, rows, width), bf16), pltpu.SemaphoreType.DMA((2,)), pltpu.SemaphoreType.DMA((2,))],
+        compiler_params=pltpu.CompilerParams(
+            collective_id=2, has_side_effects=True, vmem_limit_bytes=56 * 2**20
+        ),
+        name="forward_attention",
+    )(docs, small_state, streams, attn_in, attn_out, gains, jnp.asarray(cos_table), jnp.asarray(sin_table))
+
+
+def when(test, f):
+    def go():
+        f()
+
+    pl.when(test)(go)
+
+
+def rest_kernel(
+    dims, token_count,
+    docs, small, gains, small_rows, streams, cotangent, attn_in, attn_out, ffn_in, ffn_out, state_in,
+    normed_in, queries_in, keys_in, values_in, context_in, lse_in, first_in, read_in, cos_in, sin_in,
+    new_out, stream_grad_out, copy_out, weight_out, first_moment_out, second_moment_out, grad_out,
+    small_out, from_core,
+    grads, from_a0, from_a1, from_b0, from_b1, from_c, stage_box, kv_box, kv_send, gfirst, second, dread, read,
+    low, small_box,
+    send_sem, recv_sem, load_sem, local_sem, stage_sem, store_sem, out_sem, small_send, small_recv,
+):
+    f32, bf16 = jnp.float32, jnp.bfloat16
+    nz, ny, nx = dims
+    rows, width = second.shape
+    hidden = ffn_out.shape[0]
+    shard = low.shape[0]
+    piece = shard // 3
+    unit = 6 * piece
+    half = unit // 2
+    planes = nz // 2
+    s = lax.axis_index("seq")
+    w = lax.axis_index("wide")
+    z, y, x = w // (ny * nx), (w // nx) % ny, w % nx
+
+    def chip(cz, cy, cx):
+        return (s, (cz * ny + cy) * nx + cx)
+
+    core = (1 - s, w)
+    z_peers = [chip((z + d) % nz, y, x) for d in range(1, nz)]
+    y_peers = [chip(z, (y + d) % ny, x) for d in range(1, ny)]
+    x_peers = [chip(z, y, (x + d) % nx) for d in range(1, nx)]
+    peers = [core] + z_peers + y_peers + x_peers
+    barrier = pltpu.get_barrier_semaphore()
+    for peer in peers:
+        pl.semaphore_signal(barrier, inc=1, device_id=peer, device_id_type=MESH)
+
+    base = 2 * width
+    mix = [[small[0, base + i * 2 * NS + j] for j in range(2 * NS)] for i in range(NS)]
+    read_one = [mix[i][NS] for i in range(NS)]
+    depth_one = [mix[i][NS + 1] for i in range(NS)]
+    read_two = [mix[i][NS + 2] for i in range(NS)]
+    depth_two = [mix[i][NS + 3] for i in range(NS)]
+
+    ids = {}
+    unsent = []
+
+    def number(kind, key, count=1):
+        if (kind, key) not in ids:
+            ids[kind, key] = ids.get(kind, 0)
+            ids[kind] = ids.get(kind, 0) + count
+        return ids[kind, key]
+
+    def remote(key, ends, guard=None, recv=None):
+        sent = number("send", key)
+        got = (lambda: number("recv", key)) if recv is None else recv
+
+        def copy():
+            src, dst, peer = ends()
+            return pltpu.make_async_remote_copy(
+                src, dst, send_sem.at[sent], recv_sem.at[got()], device_id=peer, device_id_type=MESH)
+
+        copy().start()
+        unsent.append((copy, guard))
+        return copy
+
+    def wait_sends():
+        for copy, guard in unsent:
+            if guard is None:
+                copy().wait_send()
+            else:
+                pl.when(guard())(lambda copy=copy: copy().wait_send())
+        unsent.clear()
+
+    one, zero = s == 1, s == 0
+    group_of = {"h": 1, "e": 0, "l": 0}
+    guard_of = {"h": None, "e": lambda: one, "l": lambda: zero}
+    flying = {}
+
+    def zs_of(v):
+        return pl.ds(planes * group_of[v], planes)
+
+    def zlist(v):
+        return list(range(planes * group_of[v], planes * (group_of[v] + 1)))
+
+    def guarded(v, f):
+        if guard_of[v] is None:
+            f()
+        else:
+            pl.when(guard_of[v]())(f)
+
+    def more(v, test):
+        if guard_of[v] is None:
+            return test
+        return lambda: guard_of[v]() & test()
+
+    lo, hi = pl.ds(0, half), pl.ds(half, half)
+
+    def core_send(v, c):
+        sender = {"h": None, "e": lambda: zero, "l": lambda: one}[v]
+
+        def go():
+            flying[0, v, c] = [remote(
+                ("core", group_of[v], c),
+                lambda: (grads.at[1 - s, zs_of(v), :, :, c], from_core.at[zs_of(v), :, :, c], core),
+                guard=sender)]
+
+        if sender is None:
+            go()
+        else:
+            pl.when(sender())(go)
+
+    def wait_recvs(k, v, c):
+        for copy in flying[k, v, c]:
+            copy().wait_recv()
+
+    def add_core(v, c):
+        def go():
+            wait_recvs(0, v, c)
+            g = group_of[v]
+            load = pltpu.make_async_copy(from_core.at[zs_of(v), :, :, c], stage_box.at[g], stage_sem.at[g])
+            load.start()
+            load.wait()
+
+            def body(i, carry):
+                zi, yi, xi = i // (ny * nx), (i // nx) % ny, i % nx
+                at = (s, planes * g + zi, yi, xi, c)
+                grads[at] = (grads[at].astype(f32) + stage_box[g, zi, yi, xi].astype(f32)).astype(bf16)
+                return carry
+
+            lax.fori_loop(0, planes * ny * nx, body, 0)
+            out = []
+            for d in range(1, nx):
+                out.append(remote(
+                    ("a0", g, c, d),
+                    lambda d=d: (grads.at[s, zs_of(v), :, (x + d) % nx, c, lo],
+                                 from_a0.at[d - 1, zs_of(v), :, c], x_peers[d - 1]),
+                    guard=guard_of[v]))
+            for d in range(1, ny):
+                out.append(remote(
+                    ("a1", g, c, d),
+                    lambda d=d: (grads.at[s, zs_of(v), (y + d) % ny, :, c, hi],
+                                 from_a1.at[d - 1, zs_of(v), :, c], y_peers[d - 1]),
+                    guard=guard_of[v]))
+            flying[1, v, c] = out
+
+        guarded(v, go)
+
+    def add_a(v, c):
+        def go():
+            wait_recvs(1, v, c)
+            g = group_of[v]
+
+            def body_lo(i, carry):
+                zi, yi = planes * g + i // ny, i % ny
+                at = (s, zi, yi, x, c, lo)
+                total = grads[at].astype(f32)
+                for d in range(nx - 1):
+                    total = total + from_a0[d, zi, yi, c].astype(f32)
+                grads[at] = total.astype(bf16)
+                return carry
+
+            def body_hi(i, carry):
+                zi, xi = planes * g + i // nx, i % nx
+                at = (s, zi, y, xi, c, hi)
+                total = grads[at].astype(f32)
+                for d in range(ny - 1):
+                    total = total + from_a1[d, zi, xi, c].astype(f32)
+                grads[at] = total.astype(bf16)
+                return carry
+
+            lax.fori_loop(0, planes * ny, body_lo, 0)
+            lax.fori_loop(0, planes * nx, body_hi, 0)
+            out = []
+            for d in range(1, ny):
+                out.append(remote(
+                    ("b0", g, c, d),
+                    lambda d=d: (grads.at[s, zs_of(v), (y + d) % ny, x, c, lo],
+                                 from_b0.at[d - 1, zs_of(v), c], y_peers[d - 1]),
+                    guard=guard_of[v]))
+            for d in range(1, nx):
+                out.append(remote(
+                    ("b1", g, c, d),
+                    lambda d=d: (grads.at[s, zs_of(v), y, (x + d) % nx, c, hi],
+                                 from_b1.at[d - 1, zs_of(v), c], x_peers[d - 1]),
+                    guard=guard_of[v]))
+            flying[2, v, c] = out
+
+        guarded(v, go)
+
+    def add_b(v, c):
+        def go():
+            wait_recvs(2, v, c)
+            g = group_of[v]
+
+            def body(i, carry):
+                zi = planes * g + i
+                for at_rows, box, count in ((lo, from_b0, ny - 1), (hi, from_b1, nx - 1)):
+                    at = (s, zi, y, x, c, at_rows)
+                    total = grads[at].astype(f32)
+                    for d in range(count):
+                        total = total + box[d, zi, c].astype(f32)
+                    grads[at] = total.astype(bf16)
+                return carry
+
+            lax.fori_loop(0, planes, body, 0)
+            for zd in zlist(v):
+                first = number("recv", ("z", c), nz - 1)
+                when(z != zd, lambda zd=zd, first=first: remote(
+                    ("z", g, c, zd),
+                    lambda: (grads.at[s, zd, y, x, c], from_c.at[(z - zd + nz) % nz - 1, c], chip(zd, y, x)),
+                    guard=more(v, lambda: z != zd),
+                    recv=lambda: first + (z - zd + nz) % nz - 1))
+
+        guarded(v, go)
+
+    def in_group(g):
+        return (z // planes) == g
+
+    def owner_update(state, flat, outs):
+        for c in range(3):
+            for slot in range(nz - 1):
+                pltpu.make_async_remote_copy(
+                    grads.at[s, z, y, x, c], from_c.at[slot, c], send_sem.at[0],
+                    recv_sem.at[number("recv", ("z", c), nz - 1) + slot],
+                    device_id=core, device_id_type=MESH,
+                ).wait_recv()
+        pltpu.make_async_copy(state_in, state, load_sem.at[0]).wait()
+        index = s * (nz * ny * nx) + w
+        in_rows = attn_in.shape[0] * attn_in.shape[1] // width // shard
+        out_rows = in_rows + attn_out.shape[0] // shard
+        ffn_rows = out_rows + ffn_in.shape[0] * ffn_in.shape[1] // width // shard
+        blocks = ffn_in.shape[1] // width
+        thirds = attn_in.shape[1] // width
+
+        def total_of(c, at_rows):
+            total = grads[s, z, y, x, c, at_rows].astype(f32)
+            for slot in range(nz - 1):
+                total = total + from_c[slot, c, at_rows].astype(f32)
+            return total * (1.0 / token_count)
+
+        @pl.when(index < in_rows)
+        def _():
+            for c in range(3):
+                for lane in range(6):
+                    flat[lane, pl.ds(c, piece, stride=thirds), :] = total_of(c, pl.ds(lane * piece, piece))
+
+        @pl.when(((index >= in_rows) & (index < out_rows)) | (index >= ffn_rows))
+        def _():
+            for c in range(3):
+                for lane in range(6):
+                    flat[lane, pl.ds(c * piece, piece), :] = total_of(c, pl.ds(lane * piece, piece))
+
+        @pl.when((index >= out_rows) & (index < ffn_rows))
+        def _():
+            part = shard // blocks
+            for c in range(3):
+                for side in range(2):
+                    for j in range(blocks):
+                        flat[side * 3 + c, pl.ds(j, part, stride=blocks), :] = total_of(
+                            c, pl.ds(side * half + j * part, part))
+
+        def body(i, carry):
+            r = pl.ds(i * 16, 16)
+            grad = jnp.concatenate([flat[lane, r] for lane in range(6)], axis=1)
+            new = adam_step((state[0, r], state[1, r], state[2, r]), grad)
+            for box, value in zip(outs, new + (grad,)):
+                box[r] = value
+            low[r] = new[0].astype(bf16)
+            return carry
+
+        lax.fori_loop(0, shard // 16, body, 0)
+        for k, (box, dest) in enumerate(zip(outs, (weight_out, first_moment_out, second_moment_out, grad_out))):
+            pltpu.make_async_copy(box, dest, store_sem.at[k]).start()
+        keep = pltpu.make_async_copy(low, copy_out.at[s, z, y, x], store_sem.at[4])
+        keep.start()
+        keep.wait()
+
+    gather_parts = 4
+    part_rows = shard // gather_parts
+
+    def part(k):
+        return pl.ds(k * part_rows, part_rows)
+
+    def part_lo(k):
+        return pl.ds(k * part_rows, part_rows // 2)
+
+    def part_hi(k):
+        return pl.ds(k * part_rows + part_rows // 2, part_rows // 2)
+
+    def gather_z(v, k):
+        def go():
+            for zd in zlist(v):
+                got = number("recv", ("gz", zd, k))
+
+                def send(zd=zd, got=got):
+                    for d in range(1, nz):
+                        remote(
+                            ("gz", zd, k, d),
+                            lambda d=d: (low.at[part(k)], copy_out.at[s, zd, y, x, part(k)],
+                                         chip((zd + d) % nz, y, x)),
+                            guard=more(v, lambda: z == zd), recv=lambda: got)
+
+                pl.when(z == zd)(send)
+
+        guarded(v, go)
+
+    def gather_b(v, k):
+        def go():
+            g = group_of[v]
+            for zd in zlist(v):
+                when(z != zd, lambda zd=zd: pltpu.make_async_remote_copy(
+                    low.at[part(k)], copy_out.at[s, zd, y, x, part(k)], send_sem.at[0],
+                    recv_sem.at[number("recv", ("gz", zd, k))], device_id=core, device_id_type=MESH).wait_recv())
+            out = []
+            for d, peer in enumerate(y_peers):
+                out.append(remote(
+                    ("gb0", g, k, d), lambda peer=peer: (copy_out.at[s, zs_of(v), y, x, part_lo(k)],
+                                                         copy_out.at[s, zs_of(v), y, x, part_lo(k)], peer),
+                    guard=guard_of[v]))
+            for d, peer in enumerate(x_peers):
+                out.append(remote(
+                    ("gb1", g, k, d), lambda peer=peer: (copy_out.at[s, zs_of(v), y, x, part_hi(k)],
+                                                         copy_out.at[s, zs_of(v), y, x, part_hi(k)], peer),
+                    guard=guard_of[v]))
+            flying[5, v, k] = out
+
+        guarded(v, go)
+
+    def gather_a(v, k):
+        def go():
+            wait_recvs(5, v, k)
+            g = group_of[v]
+            out = []
+            for d, peer in enumerate(x_peers):
+                out.append(remote(
+                    ("ga0", g, k, d), lambda peer=peer: (copy_out.at[s, zs_of(v), :, x, part_lo(k)],
+                                                         copy_out.at[s, zs_of(v), :, x, part_lo(k)], peer),
+                    guard=guard_of[v]))
+            for d, peer in enumerate(y_peers):
+                out.append(remote(
+                    ("ga1", g, k, d), lambda peer=peer: (copy_out.at[s, zs_of(v), y, :, part_hi(k)],
+                                                         copy_out.at[s, zs_of(v), y, :, part_hi(k)], peer),
+                    guard=guard_of[v]))
+            flying[6, v, k] = out
+
+        guarded(v, go)
+
+    def gather_core(v, k):
+        def go():
+            wait_recvs(6, v, k)
+            flying[7, v, k] = [remote(
+                ("gc", group_of[v], k), lambda: (copy_out.at[s, zs_of(v), :, :, part(k)],
+                                                 copy_out.at[s, zs_of(v), :, :, part(k)], core),
+                guard=guard_of[v])]
+
+        guarded(v, go)
+
+    def gather_end(v, k):
+        taker = {"h": None, "e": lambda: zero, "l": lambda: one}[v]
+
+        def go():
+            other = copy_out.at[1 - s, zs_of(v), :, :, part(k)]
+            pltpu.make_async_remote_copy(
+                other, other, send_sem.at[0], recv_sem.at[number("recv", ("gc", group_of[v], k))],
+                device_id=core, device_id_type=MESH).wait_recv()
+
+        if taker is None:
+            go()
+        else:
+            pl.when(taker())(go)
+
+    wide_piece = piece
+    tile = hidden // 3
+    tile_pieces = tile // wide_piece
+
+    def load(src, dst, sem):
+        copy = pltpu.make_async_copy(src, dst, sem)
+        copy.start()
+        return copy
+
+    read_load = load(read_in, read, load_sem.at[1])
+
+    def ffn_scope(raw, gate_w, up_w, out_w, normed_two, normed_two_t, dsecond, gate_s, up_s, dhid_s, hid, dgate, dup):
+        raw_load = load(cotangent, raw, load_sem.at[2])
+
+        def tile_loads(c):
+            slot = c % 2
+            copies = []
+            for p in range(tile_pieces):
+                at = p * 3 * wide_piece + c * wide_piece
+                to = pl.ds(p * wide_piece, wide_piece)
+                for k, (src, dst) in enumerate((
+                    (ffn_in.at[:, pl.ds(at, wide_piece)], gate_w.at[slot, :, to]),
+                    (ffn_in.at[:, pl.ds(hidden + at, wide_piece)], up_w.at[slot, :, to]),
+                    (ffn_out.at[pl.ds(at, wide_piece)], out_w.at[slot, to]),
+                )):
+                    copies.append(load(src, dst, local_sem.at[slot, k, p]))
+            return copies
+
+        loads = {0: tile_loads(0), 1: tile_loads(1)}
+        raw_load.wait()
+        read_load.wait()
+
+        def first_block(i, carry):
+            r = pl.ds(i * 64, 64)
+            parts = unpacked(raw[r])
+            dsecond[r] = sum(parts[j] * depth_two[j] for j in range(NS)).astype(bf16)
+            gfirst[r] = sum(parts[j] * depth_one[j] for j in range(NS))
+            normal, _ = normal_of(read[r])
+            normed_two[r] = (normal * gains[1:2].astype(f32)).astype(bf16)
+            second[r] = jnp.zeros((64, width), f32)
+            dread[r] = jnp.zeros((64, width), f32)
+            return carry
+
+        lax.fori_loop(0, rows // 64, first_block, 0)
+        normed_two_t[...] = normed_two[...].T
+
+        for c in range(3):
+            slot = c % 2
+            for copy in loads[c]:
+                copy.wait()
+
+            def sub(u, carry, c=c, slot=slot):
+                cols = pl.ds(pl.multiple_of(u * 2 * wide_piece, 2 * wide_piece), 2 * wide_piece)
+                wg, wu, wo = gate_w[slot, :, cols], up_w[slot, :, cols], out_w[slot, cols]
+                gate_s[...] = nn(normed_two[...], wg)
+                up_s[...] = nn(normed_two[...], wu)
+                dhid_s[...] = nt(dsecond[...], wo)
+                for i in range(rows // 64):
+                    r = pl.ds(i * 64, 64)
+                    gate, up, dhid = gate_s[r], up_s[r], dhid_s[r]
+                    sig = 1.0 / (1.0 + jnp.exp(-gate))
+                    silu = gate * sig
+                    hid[r] = (silu * up).astype(bf16)
+                    dgate[r] = (dhid * up * sig * (1.0 + gate - silu)).astype(bf16)
+                    dup[r] = (dhid * silu).astype(bf16)
+                second[...] += nn(hid[...], wo)
+                dread[...] += nt(dgate[...], wg) + nt(dup[...], wu)
+                dwo = tn(hid[...], dsecond[...]).astype(bf16)
+                for q in range(2):
+                    p = 2 * u + q
+                    zi, yi, xi = planes + p // (ny * nx), (p // nx) % ny, p % nx
+                    for lane in range(6):
+                        grads[1, zi, yi, xi, c, pl.ds(lane * piece, piece)] = dwo[
+                            q * piece : (q + 1) * piece, lane * 128 : (lane + 1) * 128]
+                blocks = 2 * (hidden // width)
+                part = shard // blocks
+                for k, dact in enumerate((dgate, dup)):
+                    dwi = nn(normed_two_t[...], dact[...]).astype(bf16)
+                    j = u + k * (blocks // 2)
+                    for b in range(width // part):
+                        at_half, at = b // (width // part // 2), b % (width // part // 2)
+                        at = at + (nz * ny * nx // 2 if at_half == 0 else 0)
+                        zi, yi, xi = at // (ny * nx), (at // nx) % ny, at % nx
+                        for q in range(2):
+                            grads[at_half, zi, yi, xi, c, pl.ds(pl.multiple_of(q * half + j * part, 16), part)] = dwi[
+                                b * part : (b + 1) * part, q * 128 : (q + 1) * 128]
+                return carry
+
+            lax.fori_loop(0, tile_pieces // 2, sub, 0)
+            if c == 0:
+                loads[2] = tile_loads(2)
+                pl.semaphore_wait(barrier, len(peers))
+            core_send("h", c)
+            core_send("e", c)
+            if c >= 1:
+                add_core("h", c - 1)
+                add_core("e", c - 1)
+
+    pl.run_scoped(
+        ffn_scope,
+        pltpu.VMEM((rows, NS, width), bf16),
+        pltpu.VMEM((2, width, tile), bf16), pltpu.VMEM((2, width, tile), bf16), pltpu.VMEM((2, tile, width), bf16),
+        pltpu.VMEM((rows, width), bf16), pltpu.VMEM((width, rows), bf16), pltpu.VMEM((rows, width), bf16),
+        pltpu.VMEM((rows, 2 * piece), f32), pltpu.VMEM((rows, 2 * piece), f32), pltpu.VMEM((rows, 2 * piece), f32),
+        pltpu.VMEM((rows, 2 * piece), bf16), pltpu.VMEM((rows, 2 * piece), bf16), pltpu.VMEM((rows, 2 * piece), bf16),
+    )
+
+    gain_sums = {}
+
+    def attention_scope(normed, queries, keys, values, context, lse, cosine, sine, w_in, w_out, dfirst, dcontext,
+                        dkeys, dvalues, dproject, turned):
+        loads = [
+            load(src, dst, load_sem.at[3 + k])
+            for k, (src, dst) in enumerate((
+                (attn_out, w_out), (context_in, context), (queries_in, queries), (keys_in, keys), (values_in, values),
+                (lse_in, lse), (cos_in, cosine), (sin_in, sine), (normed_in, normed), (attn_in, w_in),
+            ))
+        ]
+        carry_first = sum(depth_one[j] * read_two[j] for j in range(NS))
+
+        def norm_block(i, total):
+            r = pl.ds(i * 64, 64)
+            normal, scaling = normal_of(read[r])
+            grad = dread[r]
+            total = total + jnp.sum((grad * normal).reshape(8, 8, width), axis=0)
+            scaled = grad * gains[1:2].astype(f32)
+            centre = jnp.mean(scaled, axis=-1, keepdims=True)
+            along = jnp.mean(scaled * normal, axis=-1, keepdims=True)
+            value = scaling * (scaled - centre - normal * along)
+            dread[r] = value
+            dfirst[r] = (gfirst[r] + carry_first * value).astype(bf16)
+            return total
+
+        gain_two = lax.fori_loop(0, rows // 64, norm_block, jnp.zeros((8, width), f32))
+        row = jnp.sum(gain_two, axis=0, keepdims=True)
+        for k in range(width // 128):
+            small_box[0, s, width // 128 + k : width // 128 + k + 1, :] = row[:, k * 128 : (k + 1) * 128]
+
+        for copy in loads[:2]:
+            copy.wait()
+
+        def context_block(j, carry):
+            cols = pl.ds(pl.multiple_of(j * 256, 256), 256)
+            dcontext[:, cols] = nt(dfirst[...], w_out[cols]).astype(bf16)
+            return carry
+
+        lax.fori_loop(0, width // 256, context_block, 0)
+        turned[...] = context[...].T
+        shards_in = w_in.shape[1] // width * (width // piece) // 3
+
+        def out_block(j, carry):
+            cols = pl.ds(pl.multiple_of(j * 256, 256), 256)
+            part = nn(turned[...], dfirst[:, cols]).astype(bf16)
+            for b in range(width // piece):
+                at, c = shards_in + b // 3, b % 3
+                zi, yi, xi = at // (ny * nx), (at // nx) % ny, at % nx
+                for q in range(2):
+                    grads[0, zi, yi, xi, c, pl.ds(pl.multiple_of((2 * j + q) * piece, piece), piece)] = part[
+                        b * piece : (b + 1) * piece, q * 128 : (q + 1) * 128]
+            return carry
+
+        lax.fori_loop(0, width // 256, out_block, 0)
+        for copy in loads[2:]:
+            copy.wait()
+
+        def clear(i, carry):
+            r = pl.ds(i * 64, 64)
+            dkeys[r] = jnp.zeros((64, width), f32)
+            dvalues[r] = jnp.zeros((64, width), f32)
+            return carry
+
+        lax.fori_loop(0, 2 * rows // 64, clear, 0)
+
+        def block_back(side, bi):
+            block = q_blocks(side)[bi]
+            row, key, count, single = block
+            r = pl.ds(row * EIGHTH, EIGHTH)
+            kr = pl.ds(key * EIGHTH, count * EIGHTH)
+            allow = block_mask(docs, side, block)
+
+            def pair(hp, carry):
+                cols = pl.ds(pl.multiple_of(hp * 128, 128), 128)
+                qs = two_heads(queries[r, cols]) * HD ** (-0.5)
+                dstack = two_heads(dcontext[r, cols])
+                k2 = keys[kr, cols]
+                probs = jnp.exp(masked_scores(k2, qs, allow) - lse[pl.ds(bi * 8 + hp, 1), :])
+                dprobs = nt(values[kr, cols], dstack)
+                inner = jnp.sum(probs * dprobs, axis=0, keepdims=True)
+                dscores = (probs * (dprobs - inner)).astype(bf16)
+                dkeys[kr, cols] += nn(dscores, qs)
+                dvalues[kr, cols] += nn(probs.astype(bf16), dstack)
+                dq = one_pair(tn(k2, dscores)) * HD ** (-0.5)
+                dproject[r, cols] = (dq * cosine[r] - swapped(dq) * sine[r]).astype(bf16)
+                return carry
+
+            lax.fori_loop(0, width // 128, pair, 0)
+
+        between = {
+            0: [lambda: add_core("h", 2), lambda: add_core("e", 2)],
+            1: [lambda: add_a("h", 0), lambda: add_a("e", 0)],
+            2: [lambda: add_a("h", 1), lambda: add_a("e", 1)],
+            3: [lambda: add_b("h", 0), lambda: add_b("e", 0)],
+        }
+        for bi in range(4):
+            for side in range(2):
+                pl.when(s == side)(lambda side=side: block_back(side, bi))
+            for action in between[bi]:
+                action()
+
+        shared = pl.ds(EIGHTH, 3 * EIGHTH)
+
+        @pl.when(one)
+        def _():
+            def body(i, carry):
+                r = pl.ds(i * 64, 64)
+                kr = pl.ds(EIGHTH + i * 64, 64)
+                kv_send[0, r] = dkeys[kr].astype(bf16)
+                kv_send[1, r] = dvalues[kr].astype(bf16)
+                return carry
+
+            lax.fori_loop(0, 3 * EIGHTH // 64, body, 0)
+            flying["kv"] = remote(("kv",), lambda: (kv_send, kv_box, core), guard=lambda: one)
+
+        @pl.when(zero)
+        def _():
+            flying["kv"]().wait_recv()
+
+            def body(i, carry):
+                r = pl.ds(i * 64, 64)
+                kr = pl.ds(EIGHTH + i * 64, 64)
+                dkeys[kr] += kv_box[0, r].astype(f32)
+                dvalues[kr] += kv_box[1, r].astype(f32)
+                return carry
+
+            lax.fori_loop(0, 3 * EIGHTH // 64, body, 0)
+
+        def turn_block(i, carry):
+            r = pl.ds(i * 64, 64)
+            kr = pl.ds(s * rows + i * 64, 64)
+            ct, st = cosine[r], sine[r]
+            for k in range(width // 128):
+                cols = pl.ds(k * 128, 128)
+                dk = dkeys[kr, cols]
+                dproject[r, pl.ds(width + k * 128, 128)] = (dk * ct - swapped(dk) * st).astype(bf16)
+            dproject[r, pl.ds(2 * width, width)] = dvalues[kr].astype(bf16)
+            return carry
+
+        lax.fori_loop(0, rows // 64, turn_block, 0)
+        turned[...] = normed[...].T
+
+        for j in range(w_in.shape[1] // width):
+            def in_block(cb, carry, j=j):
+                cols = pl.ds(pl.multiple_of(j * width + cb * 256, 256), 256)
+                part = nn(turned[...], dproject[:, cols]).astype(bf16)
+                for b in range(width // piece):
+                    zi, yi, xi = b // (ny * nx), (b // nx) % ny, b % nx
+                    for q in range(2):
+                        grads[0, zi, yi, xi, j, pl.ds(pl.multiple_of((2 * cb + q) * piece, piece), piece)] = part[
+                            b * piece : (b + 1) * piece, q * 128 : (q + 1) * 128]
+                return carry
+
+            lax.fori_loop(0, width // 256, in_block, 0)
+            core_send("l", j)
+
+        def dnormed_block(j, carry):
+            cols = pl.ds(pl.multiple_of(j * 256, 256), 256)
+            gfirst[:, cols] = nt(dproject[...], w_in[cols])
+            return carry
+
+        lax.fori_loop(0, width // 256, dnormed_block, 0)
+
+    pl.run_scoped(
+        attention_scope,
+        pltpu.VMEM((rows, width), bf16), pltpu.VMEM((rows, width), bf16),
+        pltpu.VMEM((2 * rows, width), bf16), pltpu.VMEM((2 * rows, width), bf16),
+        pltpu.VMEM((rows, width), bf16), pltpu.VMEM((32, 2 * EIGHTH), f32),
+        pltpu.VMEM((rows, 128), f32), pltpu.VMEM((rows, 128), f32),
+        pltpu.VMEM(attn_in.shape, bf16), pltpu.VMEM(attn_out.shape, bf16),
+        pltpu.VMEM((rows, width), bf16), pltpu.VMEM((rows, width), bf16),
+        pltpu.VMEM((2 * rows, width), f32), pltpu.VMEM((2 * rows, width), f32),
+        pltpu.VMEM((rows, 3 * width), bf16), pltpu.VMEM((width, rows), bf16),
+    )
+
+    def tail_scope(raw_h, raw_g, first, new_box, back_box, state, flat, out_w, out_m, out_v, out_g):
+        loads = [load(streams, raw_h, load_sem.at[13]), load(cotangent, raw_g, load_sem.at[14]),
+                 load(first_in, first, load_sem.at[15]), load(state_in, state, load_sem.at[0])]
+        for copy in loads[:3]:
+            copy.wait()
+        mixed_read = [sum(mix[i][j] * read_two[j] for j in range(NS)) for i in range(NS)]
+        pairs = 33
+        block = 32
+
+        def out_copies(i, slot):
+            r = pl.ds(i * block, block)
+            return [pltpu.make_async_copy(new_box.at[slot], new_out.at[r], out_sem.at[0, slot]),
+                    pltpu.make_async_copy(back_box.at[slot], stream_grad_out.at[r], out_sem.at[1, slot])]
+
+        def body(i, carry):
+            gain_one, sums = carry
+            r = pl.ds(i * block, block)
+            slot = i % 2
+
+            @pl.when(i >= 2)
+            def _():
+                for copy in out_copies(i, slot):
+                    copy.wait()
+
+            hs, gs = unpacked(raw_h[r]), unpacked(raw_g[r])
+            first_r, second_r, dread_r = first[r], second[r], dread[r]
+            branch = sum(hs[k] * read_one[k] for k in range(NS))
+            normal, scaling = normal_of(branch)
+            grad = gfirst[r]
+            gain_one = gain_one + jnp.sum((grad * normal).reshape(block // 8, 8, width), axis=0)
+            scaled = grad * gains[0:1].astype(f32)
+            centre = jnp.mean(scaled, axis=-1, keepdims=True)
+            along = jnp.mean(scaled * normal, axis=-1, keepdims=True)
+            dbranch = scaling * (scaled - centre - normal * along)
+            back = [
+                (sum(gs[j] * mix[k][j] for j in range(NS)) + dread_r * mixed_read[k] + dbranch * read_one[k]).astype(bf16)
+                for k in range(NS)
+            ]
+            back_box[slot] = packed_streams(back)
+            new = [
+                (sum(hs[k] * mix[k][j] for k in range(NS)) + first_r * depth_one[j] + second_r * depth_two[j]).astype(bf16)
+                for j in range(NS)
+            ]
+            new_box[slot] = packed_streams(new)
+            for copy in out_copies(i, slot):
+                copy.start()
+            products = [(hs[a], gs[b]) for a in range(NS) for b in range(NS)]
+            products += [(hs[a], dread_r) for a in range(NS)]
+            products += [(hs[a], dbranch) for a in range(NS)]
+            products += [(first_r, gs[b]) for b in range(NS)] + [(first_r, dread_r)]
+            products += [(second_r, gs[b]) for b in range(NS)]
+            new_sums = []
+            for total, (a, b) in zip(sums, products):
+                p = jnp.sum((a * b).reshape(block // 8, 8, width), axis=0)
+                new_sums.append(total + sum(p[:, q * 128 : (q + 1) * 128] for q in range(width // 128)))
+            return gain_one, tuple(new_sums)
+
+        zero_tile = jnp.zeros((8, 128), f32)
+        gain_one, sums = lax.fori_loop(
+            0, rows // block, body, (jnp.zeros((8, width), f32), tuple(zero_tile for _ in range(pairs))))
+        for i in (rows // block - 2, rows // block - 1):
+            for copy in out_copies(i, i % 2):
+                copy.wait()
+        row = jnp.sum(gain_one, axis=0, keepdims=True)
+        for k in range(width // 128):
+            small_box[0, s, k : k + 1, :] = row[:, k * 128 : (k + 1) * 128]
+        sums = [jnp.sum(jnp.sum(t, axis=0, keepdims=True), axis=1, keepdims=True) for t in sums]
+        hg = [[sums[a * NS + b] for b in range(NS)] for a in range(NS)]
+        h_read = sums[16:20]
+        h_branch = sums[20:24]
+        first_g, first_read, second_g = sums[24:28], sums[28], sums[29:33]
+        lane = lax.broadcasted_iota(jnp.int32, (1, 128), 1)
+        line = jnp.zeros((1, 128), f32)
+        for i in range(NS):
+            entries = [hg[i][j] + read_two[j] * h_read[i] for j in range(NS)]
+            entries.append(h_branch[i])
+            entries.append(first_g[i] + read_two[i] * first_read)
+            entries.append(sum(mix[k][i] * h_read[k] for k in range(NS)) + depth_one[i] * first_read)
+            entries.append(second_g[i])
+            for j, value in enumerate(entries):
+                line = jnp.where(lane == i * 2 * NS + j, value, line)
+        last = 2 * width // 128
+        small_box[0, s, last : last + 1, :] = line
+        small_box[0, s, last + 1 :, :] = jnp.zeros((small_box.shape[2] - last - 1, 128), f32)
+
+        small_index = [0]
+        axes = [(s, [core], 2), (x, x_peers, nx), (y, y_peers, ny), (z, z_peers, nz)]
+        small_copies = []
+
+        def small_send_all(k, place, others):
+            copies = []
+            for peer in others:
+                i = small_index[0]
+                small_index[0] += 1
+                copy = pltpu.make_async_remote_copy(
+                    small_box.at[k, place], small_box.at[k, place], small_send.at[i], small_recv.at[i],
+                    device_id=peer, device_id_type=MESH)
+                copy.start()
+                copies.append(copy)
+            small_copies.append(copies)
+
+        def small_stage(k):
+            for copy in small_copies[k]:
+                copy.wait()
+            total = small_box[k, 0]
+            for j in range(1, axes[k][2]):
+                total = total + small_box[k, j]
+            if k + 1 < len(axes):
+                small_box[k + 1, axes[k + 1][0]] = total
+                small_send_all(k + 1, axes[k + 1][0], axes[k + 1][1])
+            else:
+                grad = total * (1.0 / token_count)
+                new = adam_step((small_rows[0], small_rows[1], small_rows[2]), grad)
+                for k2, value in enumerate(new + (grad,)):
+                    small_out[k2] = value
+
+        small_send_all(0, axes[0][0], axes[0][1])
+
+        boxes = (out_w, out_m, out_v, out_g)
+        parts = range(gather_parts)
+        for c in range(3):
+            add_core("l", c)
+        add_a("h", 2)
+        add_a("e", 2)
+        add_b("h", 1)
+        add_b("e", 1)
+        small_stage(0)
+        add_a("l", 0)
+        add_b("h", 2)
+        add_b("e", 2)
+        small_stage(1)
+        add_a("l", 1)
+        add_a("l", 2)
+        small_stage(2)
+
+        @pl.when(in_group(1) | one)
+        def _():
+            owner_update(state, flat, boxes)
+
+        for k in parts:
+            gather_z("h", k)
+            gather_z("e", k)
+        for c in range(3):
+            add_b("l", c)
+        small_stage(3)
+        for k in parts:
+            gather_b("h", k)
+            gather_b("e", k)
+
+        @pl.when(in_group(0) & zero)
+        def _():
+            owner_update(state, flat, boxes)
+
+        for k in parts:
+            gather_z("l", k)
+        for k in parts:
+            gather_a("h", k)
+            gather_a("e", k)
+            gather_b("l", k)
+        for k in parts:
+            gather_core("h", k)
+            gather_core("e", k)
+            gather_a("l", k)
+        for k in parts:
+            gather_core("l", k)
+        for k in parts:
+            for v in ("h", "e", "l"):
+                gather_end(v, k)
+
+        wait_sends()
+        for k2, (box, dest) in enumerate(zip(boxes, (weight_out, first_moment_out, second_moment_out, grad_out))):
+            pltpu.make_async_copy(box, dest, store_sem.at[k2]).wait()
+
+    pl.run_scoped(
+        tail_scope,
+        pltpu.VMEM((rows, NS, width), bf16), pltpu.VMEM((rows, NS, width), bf16), pltpu.VMEM((rows, width), f32),
+        pltpu.VMEM((2, 32, NS, width), bf16), pltpu.VMEM((2, 32, NS, width), bf16),
+        pltpu.VMEM((3, shard, width), f32), pltpu.VMEM((6, shard, 128), f32),
+        pltpu.VMEM((shard, width), f32), pltpu.VMEM((shard, width), f32),
+        pltpu.VMEM((shard, width), f32), pltpu.VMEM((shard, width), f32),
+    )
+    assert ids["send"] <= send_sem.shape[0] and ids["recv"] <= recv_sem.shape[0], ids
+
+
+def rest_part(dims, token_count, docs, small_state, gains, streams, cotangent, weights, big_state, kept):
+    attn_in, attn_out, ffn_in, ffn_out = weights
+    nz, ny, nx = dims
+    rows, width = streams.shape[0], attn_out.shape[0]
+    shard = big_state.shape[1]
+    unit, half, hidden = 2 * shard, shard, ffn_out.shape[0]
+    bf16, f32 = jnp.bfloat16, jnp.float32
+    shape = jax.ShapeDtypeStruct
+    small_count = small_state.shape[1]
+    small_rows = jnp.pad(small_state, ((0, 0), (0, -small_count % 1024))).reshape(3, -1, 128)
+    small_shape = small_rows.shape[1:]
+    smem = pl.BlockSpec(memory_space=pltpu.SMEM)
+    vmem = pl.BlockSpec(memory_space=pltpu.VMEM)
+    hbm = pl.BlockSpec(memory_space=pl.ANY)
+    state_shape = shape((shard, width), f32)
+    stream_shape = shape((rows, NS, width), bf16)
+    outs = pl.pallas_call(
+        functools.partial(rest_kernel, dims, token_count),
+        out_shape=[
+            stream_shape, stream_shape, shape((2, nz, ny, nx, shard, width), bf16),
+            state_shape, state_shape, state_shape, state_shape, shape((4,) + small_shape, f32),
+            shape((nz, ny, nx, 3, unit, 128), bf16),
+        ],
+        in_specs=[smem, smem, vmem, vmem] + [hbm] * 17,
+        out_specs=[hbm] * 7 + [vmem, hbm],
+        scratch_shapes=[
+            pltpu.VMEM((2, nz, ny, nx, 3, unit, 128), bf16),
+            pltpu.VMEM((max(nx - 1, 1), nz, ny, 3, half, 128), bf16),
+            pltpu.VMEM((max(ny - 1, 1), nz, nx, 3, half, 128), bf16),
+            pltpu.VMEM((max(ny - 1, 1), nz, 3, half, 128), bf16),
+            pltpu.VMEM((max(nx - 1, 1), nz, 3, half, 128), bf16),
+            pltpu.VMEM((max(nz - 1, 1), 3, unit, 128), bf16),
+            pltpu.VMEM((2, nz // 2, ny, nx, unit, 128), bf16),
+            pltpu.VMEM((2, 3 * EIGHTH, width), bf16),
+            pltpu.VMEM((2, 3 * EIGHTH, width), bf16),
+            pltpu.VMEM((rows, width), f32), pltpu.VMEM((rows, width), f32),
+            pltpu.VMEM((rows, width), f32), pltpu.VMEM((rows, width), f32),
+            pltpu.VMEM((shard, width), bf16),
+            pltpu.VMEM((4, max(2, nx, ny, nz)) + small_shape, f32),
+            pltpu.SemaphoreType.DMA((180,)), pltpu.SemaphoreType.DMA((120,)),
+            pltpu.SemaphoreType.DMA((16,)), pltpu.SemaphoreType.DMA((2, 3, 8)),
+            pltpu.SemaphoreType.DMA((2,)), pltpu.SemaphoreType.DMA((5,)), pltpu.SemaphoreType.DMA((2, 2)),
+            pltpu.SemaphoreType.DMA((8,)), pltpu.SemaphoreType.DMA((8,)),
+        ],
+        compiler_params=pltpu.CompilerParams(
+            collective_id=1, has_side_effects=True, vmem_limit_bytes=63 * 2**20
+        ),
+        name="backward_sync",
+    )(docs, small_state, gains, small_rows, streams, cotangent, attn_in, attn_out, ffn_in, ffn_out, big_state, *kept)
+    small_out = outs[7].reshape(4, -1)[:, :small_count]
+    copy = outs[2].reshape(-1, width)
+    return outs[0], outs[1], copy, outs[3], outs[4], outs[5], outs[6], small_out
+
+
 def torus(mesh):
     wide = mesh.shape["wide"]
     where = [getattr(d, "coords", None) for d in mesh.devices.flat]
@@ -620,6 +1789,22 @@
 ):
     row_count = streams.shape[1]
     model_width = attn_out.shape[0]
+    fits = (
+        big_state.shape[1] == 384 and model_width == 768 and row_count == 512 and dims[0] % 2 == 0
+        and ffn_out.shape[0] == 3072 and dims[0] * dims[1] * dims[2] == 16
+    )
+    if fits:
+        kept = forward_part(streams[0], doc_lengths, small_state, (attn_in, attn_out), norm_gains.T)
+        token_count = 2 * row_count * lax.axis_size("wide")
+        result, stream_grad, gathered, weight_new, first_new, second_new, owned_grads, small_out = rest_part(
+            dims, token_count, doc_lengths, small_state, norm_gains.T, streams[0], cotangent[0],
+            (attn_in, attn_out, ffn_in, ffn_out), big_state, kept,
+        )
+        gains_copy = small_out[0, : 2 * model_width].reshape(2, model_width).T.astype(jnp.bfloat16)
+        return (
+            result[None], stream_grad[None], weight_new, first_new, second_new, owned_grads,
+            small_out[0], small_out[1], small_out[2], small_out[3], gathered, gains_copy,
+        )
     member = lax.axis_index("seq")
     token_total = row_count * lax.axis_size("seq")
     token_count = token_total * lax.axis_size("wide")

time: 570 us -> 335 us (0.59)
  the two profiles are of different devices: /device:TPU:0 before, /device:TPU:27 now
where the time goes in v2:
time: 335 us
  Pallas kernels  308 us (92%)
  local copies, waits for them, and re-layouts  26.2 us (8%)
    pallas_call x1, Pallas kernels, rest_part(): pl.pallas_call(functools.partial(rest_kernel, dims, token_count), out_sha...  274 us
    pallas_call x1, Pallas kernels, forward_part(): pl.pallas_call(forward_kernel, out_shape=[shape((rows, width), bf16), sha...  34.3 us
    unnamed x16, local copies, waits for them, and re-layouts  24.9 us

profile of v2, /device:TPU:27, one launch (start us, length us, event | category | flops | bytes accessed | tf_op | source)
XLA Modules:
  0.0 335.0 jit_solution(8107279030061213215)
XLA Ops:
  0.6 0.0 copy-start.2
  0.7 34.3 %forward_attention.1 = (bf16[512,768]{1,0:T(8,128)(2,1)}, bf16[512,768]{1,0:T(8,128)(2,1)}, bf16[1024,768]{1,0:T(8,128)(2,1)}, bf16[1024,768]{1,0:T(8,128)(2,1)}...) custom-call(s32[1,8]{1,0:T(1,128)} %docs.3, ...), custom_call_target="tpu_custom_call" | custom-call | tf_op jit(solution)/shard_map/forward_attention/pallas_call | solution.py:536
  35.0 0.0 copy-done.2
  35.0 0.6 copy.29
  35.6 273.8 %backward_sync.1 = (bf16[512,4,768]{2,1,0:T(4,128)(2,1)}, bf16[512,4,768]{2,1,0:T(4,128)(2,1)}, bf16[2,4,2,2,384,768]{5,4,3,2,1,0:T(8,128)(2,1)}, f32[384,768]{1...) custom-call(s32[1,8]{1,0:T(1,128)} %docs.3, ...), custom_call_target="tpu_custom_call" | custom-call | tf_op jit(solution)/shard_map/backward_sync/pallas_call | solution.py:1415
  309.4 0.8 copy.28
  310.2 0.0 copy-start.1
  310.2 0.7 slice_reduce_fusion
  310.9 0.6 convert_element_type.9
  311.5 0.0 copy-start
  311.5 4.8 %copy.37 = bf16[1,512,4,768]{3,2,1,0:T(4,128)(2,1)} copy(bf16[1,512,4,768]{3,2,1,0:T(4,128)(2,1)} %bitcast.21) | data formatting | bytes 6291456
  316.2 0.0 copy-done.1
  316.2 1.7 copy.38
  317.9 3.1 copy.39
  321.0 2.4 copy.40
  323.4 2.4 copy.41
  325.7 2.4 copy.42
  328.1 0.0 copy-done
  328.1 6.9 %copy.43 = bf16[12288,768]{1,0:T(8,128)(2,1)} copy(bf16[12288,768]{1,0:T(8,128)(2,1)S(1)} %bitcast.16) | data formatting | bytes 37748736
  (2 shorter events, 0.0 us)
Async XLA Ops:
  0.6 34.3 %copy-start.2 = (f32[3,1568]{1,0:T(4,128)S(1)}, f32[3,1568]{1,0:T(4,128)}, u32[]{:S(2)}) copy-start(f32[3,1568]{1,0:T(4,128)} %small.3) | copy-start | bytes 56452
  310.2 6.1 %copy-start.1 = (bf16[512,4,768]{2,1,0:T(4,128)(2,1)S(1)}, bf16[512,4,768]{2,1,0:T(4,128)(2,1)}, u32[]{:S(2)}) copy-start(bf16[512,4,768]{2,1,0:T(4,128)(2,1)} %get-tuple-element.41) | copy-start | bytes 9437188
  311.5 16.6 %copy-start = (bf16[2,4,2,2,384,768]{5,4,3,2,1,0:T(8,128)(2,1)S(1)}, bf16[2,4,2,2,384,768]{5,4,3,2,1,0:T(8,128)(2,1)}, u32[]{:S(2)}) copy-start(bf16[2,4,2,2,384,768]{5,4,3,2,1,0:T(8,128)(2,1)} %get-tuple-element.47) | copy-start | bytes 56623108

commit v3 on v1

--- a/solution.py
+++ b/solution.py
@@ -2,6 +2,7 @@
 
 import jax
 import jax.numpy as jnp
+import numpy as np
 from jax import lax
 from jax.experimental import pallas as pl
 from jax.experimental.pallas import tpu as pltpu
@@ -281,6 +282,1533 @@
     return (weight_new, first_new, second_new)
 
 
+def rope_constants(length, head_size):
+    half_size = head_size // 2
+    exponent = np.arange(half_size, dtype=np.float32) * np.float32(2.0 / head_size)
+    frequency = np.power(np.float64(rope_base), -exponent.astype(np.float64)).astype(np.float32)
+    angles = np.arange(length, dtype=np.float32)[:, None] * frequency[None, :]
+    cosine = np.cos(angles.astype(np.float64)).astype(np.float32)
+    sine = np.sin(angles.astype(np.float64)).astype(np.float32)
+    return np.tile(cosine, (1, 4)), np.tile(np.concatenate([-sine, sine], axis=1), (1, 2))
+
+
+def swapped(values):
+    lane = lax.broadcasted_iota(jnp.int32, values.shape, 1)
+    return jnp.where(lane % HD < HD // 2, pltpu.roll(values, 128 - HD // 2, 1), pltpu.roll(values, HD // 2, 1))
+
+
+def unpacked(block):
+    count = block.shape[0]
+    flat = block.reshape(count * NS, block.shape[2])
+    row = lax.broadcasted_iota(jnp.int32, (count * NS, count * NS), 0)
+    col = lax.broadcasted_iota(jnp.int32, (count * NS, count * NS), 1)
+    pick = ((row % count) * NS + row // count == col).astype(jnp.bfloat16)
+    out = jnp.dot(pick, flat, preferred_element_type=jnp.float32)
+    return [out[i * count : (i + 1) * count] for i in range(NS)]
+
+
+def packed_streams(parts):
+    count = parts[0].shape[0]
+    flat = jnp.concatenate(parts, axis=0)
+    row = lax.broadcasted_iota(jnp.int32, (count * NS, count * NS), 0)
+    col = lax.broadcasted_iota(jnp.int32, (count * NS, count * NS), 1)
+    place = ((col % count) * NS + col // count == row).astype(jnp.bfloat16)
+    out = jnp.dot(place, flat, preferred_element_type=jnp.float32).astype(jnp.bfloat16)
+    return out.reshape(count, NS, parts[0].shape[1])
+
+
+def normal_of(values):
+    centre = jnp.mean(values, axis=-1, keepdims=True)
+    centred = values - centre
+    scaling = lax.rsqrt(jnp.mean(centred * centred, axis=-1, keepdims=True) + norm_epsilon)
+    return centred * scaling, scaling
+
+
+def nt(left, right):
+    return lax.dot_general(left, right, (((1,), (1,)), ((), ())), preferred_element_type=jnp.float32)
+
+
+def tn(left, right):
+    return lax.dot_general(left, right, (((0,), (0,)), ((), ())), preferred_element_type=jnp.float32)
+
+
+def nn(left, right):
+    return jnp.dot(left, right, preferred_element_type=jnp.float32)
+
+
+def doc_starts(docs, place):
+    start = jnp.zeros(place.shape, jnp.int32)
+    bound = 0
+    for j in range(docs.shape[1] - 1):
+        bound = bound + docs[0, j]
+        start = jnp.where(place >= bound, bound, start)
+    return start
+
+
+EIGHTH = 128
+
+
+def q_blocks(s):
+    if s == 0:
+        return [(0, 0, 1, False)] + [(i, 1, i, True) for i in (1, 2, 3)]
+    return [(i - 4, 1, i, True) for i in (4, 5, 6)] + [(3, 7, 1, False)]
+
+
+def block_mask(docs, s, block):
+    row, key, count, single = block
+    shape = (EIGHTH, 2 * EIGHTH)
+    place = lax.broadcasted_iota(jnp.int32, shape, 1) % EIGHTH
+    at = lax.broadcasted_iota(jnp.int32, shape, 0)
+    if single:
+        return at <= place
+    first = (4 * s + row) * EIGHTH
+    start = doc_starts(docs, place + first)
+    return (at + first >= start) & (at <= place)
+
+
+def two_heads(pair):
+    lane = lax.broadcasted_iota(jnp.int32, pair.shape, 1)
+    none = jnp.zeros_like(pair)
+    return jnp.concatenate([jnp.where(lane < HD, pair, none), jnp.where(lane < HD, none, pair)], axis=0)
+
+
+def one_pair(stacked):
+    rows = stacked.shape[1] // 2
+    return jnp.concatenate([stacked[:HD, :rows], stacked[HD:, rows:]], axis=0).T
+
+
+def masked_scores(k2, qs, allow):
+    scores = nt(k2, qs)
+    keys = scores.shape[0]
+    last = jnp.where(allow, scores[keys - EIGHTH :], masked_score)
+    if keys == EIGHTH:
+        return last
+    return jnp.concatenate([scores[: keys - EIGHTH], last], axis=0)
+
+
+def when(test, f):
+    def go():
+        f()
+
+    pl.when(test)(go)
+
+
+UP, EARLY, LATE = range(3)
+(
+    CORE_SEND,
+    ADD_CORE,
+    ADD_A,
+    ADD_B,
+    Z_MID,
+    Z_LAST,
+    GATHER_Z,
+    RELAY_ONE,
+    RELAY_TWO,
+    GATHER_B,
+    GATHER_A,
+    GATHER_CORE,
+    GATHER_END,
+    H_B,
+    H_A,
+    H_Z,
+    H_R1,
+    H_R2,
+    SMALL,
+    OWNER,
+) = range(20)
+PARTS = 4
+Z_LAST = ((UP, 0), (EARLY, 0), )
+PLAN = {
+    4: (
+        ((CORE_SEND, UP, 0),),
+        ((CORE_SEND, UP, 0),),
+    ),
+    5: (
+        (),
+        ((ADD_CORE, UP, 0),),
+    ),
+    8: (
+        ((CORE_SEND, UP, 1), (CORE_SEND, EARLY, 0),),
+        ((ADD_CORE, UP, 1), (CORE_SEND, UP, 1),),
+    ),
+    9: (
+        ((ADD_CORE, UP, 0),),
+        ((ADD_A, UP, 0), (ADD_CORE, EARLY, 1),),
+    ),
+    10: (
+        ((CORE_SEND, EARLY, 1),),
+        (),
+    ),
+    12: (
+        ((CORE_SEND, UP, 2), (CORE_SEND, EARLY, 2), (ADD_A, UP, 0),),
+        ((ADD_A, UP, 1), (ADD_B, UP, 0), (ADD_CORE, EARLY, 0), (CORE_SEND, UP, 2), (ADD_A, EARLY, 1),
+         (ADD_CORE, UP, 2), (ADD_CORE, EARLY, 2),),
+    ),
+    14: (
+        ((ADD_B, UP, 0),),
+        ((Z_MID, UP, 0), (ADD_B, UP, 1),),
+    ),
+    16: (
+        ((ADD_CORE, UP, 2), (Z_MID, UP, 0),),
+        (),
+    ),
+    17: (
+        (),
+        ((ADD_B, EARLY, 1), (ADD_A, UP, 2), (Z_MID, UP, 1), (ADD_A, EARLY, 2),),
+    ),
+    18: (
+        ((ADD_A, UP, 2),),
+        (),
+    ),
+    19: (
+        ((ADD_CORE, UP, 1), (ADD_B, UP, 2),),
+        ((ADD_B, UP, 2),),
+    ),
+    22: (
+        ((ADD_A, UP, 1), (ADD_CORE, LATE, 0),),
+        ((CORE_SEND, LATE, 0), (Z_MID, UP, 2), (ADD_B, EARLY, 2), (Z_LAST, UP, 1), (ADD_A, EARLY, 0), (Z_LAST,
+         UP, 0), (Z_MID, EARLY, 1),),
+    ),
+    23: (
+        ((ADD_CORE, LATE, 1), (Z_MID, UP, 2), (Z_LAST, UP, 0),),
+        ((CORE_SEND, LATE, 1), (Z_MID, EARLY, 2), (ADD_B, EARLY, 0),),
+    ),
+    24: (
+        ((ADD_A, LATE, 0), (ADD_B, UP, 1), (ADD_CORE, LATE, 2), (ADD_A, LATE, 1), (ADD_B, LATE, 0), (Z_MID,
+         UP, 1),),
+        ((CORE_SEND, LATE, 2), (Z_LAST, UP, 2),),
+    ),
+    25: (
+        ((Z_LAST, UP, 2),),
+        ((Z_LAST, EARLY, 1), (Z_MID, EARLY, 0),),
+    ),
+    26: (
+        ((ADD_A, LATE, 2), (ADD_B, LATE, 1),),
+        ((OWNER, UP, 0), (GATHER_Z, UP, 3),),
+    ),
+    27: (
+        (),
+        ((Z_LAST, EARLY, 2), (Z_LAST, EARLY, 0), (OWNER, EARLY, 0), (GATHER_Z, EARLY, 1), (RELAY_TWO, UP, 3),
+         (H_B, EARLY, 0), (RELAY_ONE, UP, 3), (GATHER_Z, UP, 1),),
+    ),
+    28: (
+        ((Z_LAST, UP, 1),),
+        ((GATHER_Z, UP, 2),),
+    ),
+    29: (
+        ((Z_MID, LATE, 0), (Z_LAST, LATE, 0), (ADD_B, LATE, 2), (Z_MID, LATE, 1), (OWNER, UP, 0), (Z_LAST,
+         LATE, 1), (Z_MID, LATE, 2), (GATHER_Z, UP, 2),),
+        (),
+    ),
+    30: (
+        ((Z_LAST, LATE, 2), (H_B, UP, 0),),
+        ((RELAY_ONE, UP, 2), (GATHER_B, UP, 3), (RELAY_TWO, UP, 2), (H_B, UP, 0),),
+    ),
+    31: (
+        ((RELAY_ONE, UP, 2), (RELAY_TWO, UP, 2), (GATHER_Z, UP, 1),),
+        ((GATHER_Z, EARLY, 3), (RELAY_TWO, UP, 1), (H_A, EARLY, 0),),
+    ),
+    32: (
+        ((GATHER_Z, UP, 3), (OWNER, LATE, 0), (GATHER_Z, LATE, 2), (RELAY_ONE, UP, 1), (GATHER_B, UP, 2),),
+        ((RELAY_ONE, UP, 1), (GATHER_Z, EARLY, 2), (GATHER_B, UP, 2), (RELAY_ONE, EARLY, 1), (GATHER_A, UP,
+         3),),
+    ),
+    33: (
+        ((RELAY_TWO, UP, 1), (RELAY_TWO, UP, 3), (RELAY_ONE, UP, 3), (GATHER_Z, LATE, 0),),
+        ((H_A, UP, 0), (GATHER_A, UP, 2), (GATHER_B, UP, 1), (RELAY_ONE, EARLY, 3),),
+    ),
+    34: (
+        ((GATHER_B, UP, 1), (GATHER_Z, LATE, 1),),
+        (),
+    ),
+    35: (
+        ((H_A, UP, 0), (GATHER_Z, LATE, 3), (H_Z, UP, 0),),
+        ((RELAY_ONE, EARLY, 2), (RELAY_TWO, EARLY, 1), (H_Z, EARLY, 0), (GATHER_CORE, UP, 3),),
+    ),
+    36: (
+        ((RELAY_ONE, LATE, 0), (GATHER_A, UP, 2),),
+        ((RELAY_TWO, EARLY, 3), (GATHER_B, EARLY, 1), (GATHER_B, EARLY, 3),),
+    ),
+    37: (
+        ((RELAY_ONE, LATE, 2), (GATHER_B, UP, 3),),
+        (),
+    ),
+    38: (
+        ((RELAY_TWO, LATE, 2), (RELAY_TWO, LATE, 0),),
+        ((RELAY_TWO, EARLY, 2), (GATHER_A, UP, 1), (GATHER_A, EARLY, 3), (H_Z, UP, 0), (GATHER_CORE, UP, 2),
+         (H_R1, EARLY, 0),),
+    ),
+    39: (
+        ((GATHER_A, UP, 1), (H_R1, UP, 0),),
+        (),
+    ),
+    40: (
+        (),
+        ((GATHER_A, EARLY, 1),),
+    ),
+    41: (
+        ((GATHER_A, UP, 3), (GATHER_CORE, UP, 2), (GATHER_B, LATE, 0), (RELAY_ONE, LATE, 1), (GATHER_B, LATE,
+         2), (RELAY_TWO, LATE, 1),),
+        (),
+    ),
+    42: (
+        ((RELAY_ONE, LATE, 3), (GATHER_B, LATE, 1), (GATHER_A, LATE, 0), (GATHER_A, LATE, 2), (GATHER_CORE,
+         UP, 3), (RELAY_TWO, LATE, 3), (H_R2, UP, 0), (GATHER_END, EARLY, 1), (SMALL, UP, 0), (GATHER_END, UP,
+         1), (GATHER_END, EARLY, 3), (SMALL, UP, 1), (GATHER_CORE, LATE, 0), (GATHER_B, LATE, 3), (GATHER_A,
+         LATE, 1), (GATHER_CORE, UP, 1), (GATHER_END, EARLY, 2), (GATHER_CORE, UP, 0), (GATHER_A, LATE, 3),
+         (GATHER_CORE, LATE, 2), (GATHER_CORE, LATE, 1), (SMALL, UP, 2), (GATHER_CORE, LATE, 3), (SMALL, UP,
+         3), (GATHER_END, UP, 2), (SMALL, UP, 4), (GATHER_END, UP, 0), (GATHER_END, UP, 3), (GATHER_END,
+         EARLY, 0),),
+        ((GATHER_B, EARLY, 2), (GATHER_CORE, EARLY, 3), (GATHER_CORE, EARLY, 1), (SMALL, UP, 0), (GATHER_CORE,
+         UP, 1), (GATHER_A, EARLY, 2), (H_R1, UP, 0), (SMALL, UP, 1), (H_R2, UP, 0), (GATHER_CORE, EARLY, 2),
+         (GATHER_END, UP, 2), (H_R2, EARLY, 0), (GATHER_END, LATE, 0), (GATHER_CORE, EARLY, 0), (GATHER_END,
+         UP, 1), (SMALL, UP, 2), (GATHER_CORE, UP, 0), (GATHER_END, UP, 3), (GATHER_END, LATE, 1), (SMALL, UP,
+         3), (SMALL, UP, 4), (GATHER_END, UP, 0), (GATHER_END, LATE, 2), (GATHER_END, LATE, 3),),
+    ),
+}
+
+
+def layer_kernel(
+    dims, token_count,
+    docs, small, gains, small_rows, streams, cotangent, attn_in, attn_out, ffn_in, ffn_out, state_in,
+    cos_table, sin_table,
+    new_out, stream_grad_out, copy_out, grad_out, small_out, from_core,
+    grads, from_a0, from_a1, from_b0, from_b1, from_c, stage_box, kv_box, gfirst, second, dread, read, first,
+    normed, queries, keys, values, context, lse, cosine, sine, starts, low, small_box,
+    kv_send_sem, kv_recv_sem, send_sem, recv_sem, load_sem, local_sem, stage_sem, store_sem, out_sem, small_send, small_recv,
+):
+    f32, bf16 = jnp.float32, jnp.bfloat16
+    nz, ny, nx = dims
+    rows, width = second.shape
+    hidden = ffn_out.shape[0]
+    shard = low.shape[0]
+    piece = shard // 3
+    unit = 6 * piece
+    half = unit // 2
+    planes = nz // 2
+    s = lax.axis_index("seq")
+    w = lax.axis_index("wide")
+    z, y, x = w // (ny * nx), (w // nx) % ny, w % nx
+
+    def chip(cz, cy, cx):
+        return (s, (cz * ny + cy) * nx + cx)
+
+    core = (1 - s, w)
+    z_peers = [chip((z + d) % nz, y, x) for d in range(1, nz)]
+    y_peers = [chip(z, (y + d) % ny, x) for d in range(1, ny)]
+    x_peers = [chip(z, y, (x + d) % nx) for d in range(1, nx)]
+    peers = [core] + z_peers + y_peers + x_peers
+    barrier = pltpu.get_barrier_semaphore()
+    for peer in peers:
+        pl.semaphore_signal(barrier, inc=1, device_id=peer, device_id_type=MESH)
+
+    base = 2 * width
+    mix = [[small[0, base + i * 2 * NS + j] for j in range(2 * NS)] for i in range(NS)]
+    read_one = [mix[i][NS] for i in range(NS)]
+    depth_one = [mix[i][NS + 1] for i in range(NS)]
+    read_two = [mix[i][NS + 2] for i in range(NS)]
+    depth_two = [mix[i][NS + 3] for i in range(NS)]
+
+    def load(src, dst, sem):
+        copy = pltpu.make_async_copy(src, dst, sem)
+        copy.start()
+        return copy
+
+    ids = {}
+    unsent = {}
+    unit_now = [None]
+
+    def number(kind, key, count=1):
+        if (kind, key) not in ids:
+            ids[kind, key] = ids.get(kind, 0)
+            ids[kind] = ids.get(kind, 0) + count
+        return ids[kind, key]
+
+    def copy_of(key, ends, recv=None):
+        src, dst, peer = ends()
+        got = number("recv", key) if recv is None else recv()
+        return pltpu.make_async_remote_copy(
+            src, dst, send_sem.at[number("send", key)], recv_sem.at[got], device_id=peer, device_id_type=MESH)
+
+    def remote(key, ends, guard=None, recv=None):
+        copy_of(key, ends, recv).start()
+        unsent.setdefault((key, unit_now[-1]), (lambda: copy_of(key, ends, recv), guard))
+
+    def wait_sends():
+        for copy, guard in unsent.values():
+            if guard is None:
+                copy().wait_send()
+            else:
+                pl.when(guard())(lambda copy=copy: copy().wait_send())
+        unsent.clear()
+
+    one, zero = s == 1, s == 0
+    group_of = {UP: 1, EARLY: 0, LATE: 0}
+    guard_of = {UP: None, EARLY: lambda: one, LATE: lambda: zero}
+
+    def zs_of(v):
+        return pl.ds(planes * group_of[v], planes)
+
+    def zlist(v):
+        return list(range(planes * group_of[v], planes * (group_of[v] + 1)))
+
+    def guarded(v, f):
+        f()
+
+    def more(v, test):
+        if guard_of[v] is None:
+            return test
+        return lambda: guard_of[v]() & test()
+
+    lo, hi = pl.ds(0, half), pl.ds(half, half)
+
+    def core_moves(v, c):
+        return [(
+            ("core", group_of[v], c),
+            lambda: (grads.at[1 - s, zs_of(v), :, :, c], from_core.at[zs_of(v), :, :, c], core))]
+
+    def a_moves(v, c):
+        g = group_of[v]
+        return [
+            (("a0", g, c, d), lambda d=d: (
+                grads.at[s, zs_of(v), :, (x + d) % nx, c, lo], from_a0.at[d - 1, zs_of(v), :, c], x_peers[d - 1]))
+            for d in range(1, nx)
+        ] + [
+            (("a1", g, c, d), lambda d=d: (
+                grads.at[s, zs_of(v), (y + d) % ny, :, c, hi], from_a1.at[d - 1, zs_of(v), :, c], y_peers[d - 1]))
+            for d in range(1, ny)
+        ]
+
+    def b_moves(v, c):
+        g = group_of[v]
+        return [
+            (("b0", g, c, d), lambda d=d: (
+                grads.at[s, zs_of(v), (y + d) % ny, x, c, lo], from_b0.at[d - 1, zs_of(v), c], y_peers[d - 1]))
+            for d in range(1, ny)
+        ] + [
+            (("b1", g, c, d), lambda d=d: (
+                grads.at[s, zs_of(v), y, (x + d) % nx, c, hi], from_b1.at[d - 1, zs_of(v), c], x_peers[d - 1]))
+            for d in range(1, nx)
+        ]
+
+    def same(ref, peer):
+        return ref, ref, peer
+
+    def gb_moves(v, k):
+        g = group_of[v]
+        return [
+            (("gb0", g, k, d), lambda peer=peer: same(copy_out.at[s, zs_of(v), y, x, part_lo(k)], peer))
+            for d, peer in enumerate(y_peers)
+        ] + [
+            (("gb1", g, k, d), lambda peer=peer: same(copy_out.at[s, zs_of(v), y, x, part_hi(k)], peer))
+            for d, peer in enumerate(x_peers)
+        ]
+
+    def ga_moves(v, k):
+        g = group_of[v]
+        return [
+            (("ga0", g, k, d), lambda peer=peer: same(copy_out.at[s, zs_of(v), :, x, part_lo(k)], peer))
+            for d, peer in enumerate(x_peers)
+        ] + [
+            (("ga1", g, k, d), lambda peer=peer: same(copy_out.at[s, zs_of(v), y, :, part_hi(k)], peer))
+            for d, peer in enumerate(y_peers)
+        ]
+
+    def gc_moves(v, k):
+        return [(("gc", group_of[v], k), lambda: same(copy_out.at[s, zs_of(v), :, :, part(k)], core))]
+
+    def start(moves, v, c, guard="unit"):
+        for key, ends in moves(v, c):
+            remote(key, ends, guard=guard_of[v] if guard == "unit" else guard)
+
+    def wait_recvs(moves, v, c):
+        for key, ends in moves(v, c):
+            copy_of(key, ends).wait_recv()
+
+    def core_send(v, c):
+        start(core_moves, v, c, {UP: None, EARLY: lambda: zero, LATE: lambda: one}[v])
+
+    def add_core(v, c):
+        def go():
+            wait_recvs(core_moves, v, c)
+            g = group_of[v]
+            loads = [
+                load(from_core.at[planes * g + i, :, :, c], stage_box.at[i], stage_sem.at[i]) for i in range(planes)
+            ]
+            for plane, copy in enumerate(loads):
+                copy.wait()
+
+                def body(i, carry, plane=plane):
+                    yi, xi = i // nx, i % nx
+                    at = (s, planes * g + plane, yi, xi, c)
+                    grads[at] = (grads[at].astype(f32) + stage_box[plane, yi, xi].astype(f32)).astype(bf16)
+                    return carry
+
+                lax.fori_loop(0, ny * nx, body, 0)
+            start(a_moves, v, c)
+
+        guarded(v, go)
+
+    def add_a(v, c):
+        def go():
+            wait_recvs(a_moves, v, c)
+            g = group_of[v]
+
+            def body_lo(i, carry):
+                zi, yi = planes * g + i // ny, i % ny
+                at = (s, zi, yi, x, c, lo)
+                total = grads[at].astype(f32)
+                for d in range(nx - 1):
+                    total = total + from_a0[d, zi, yi, c].astype(f32)
+                grads[at] = total.astype(bf16)
+                return carry
+
+            def body_hi(i, carry):
+                zi, xi = planes * g + i // nx, i % nx
+                at = (s, zi, y, xi, c, hi)
+                total = grads[at].astype(f32)
+                for d in range(ny - 1):
+                    total = total + from_a1[d, zi, xi, c].astype(f32)
+                grads[at] = total.astype(bf16)
+                return carry
+
+            lax.fori_loop(0, planes * ny, body_lo, 0)
+            lax.fori_loop(0, planes * nx, body_hi, 0)
+            start(b_moves, v, c)
+
+        guarded(v, go)
+
+    def add_b(v, c):
+        def go():
+            wait_recvs(b_moves, v, c)
+            g = group_of[v]
+
+            def body(i, carry):
+                zi = planes * g + i
+                for at_rows, box, count in ((lo, from_b0, ny - 1), (hi, from_b1, nx - 1)):
+                    at = (s, zi, y, x, c, at_rows)
+                    total = grads[at].astype(f32)
+                    for d in range(count):
+                        total = total + box[d, zi, c].astype(f32)
+                    grads[at] = total.astype(bf16)
+                return carry
+
+            lax.fori_loop(0, planes, body, 0)
+            hop(v, c, 0)
+
+        guarded(v, go)
+
+    def place_of(v):
+        return z if group_of[v] == 1 else nz - 1 - z
+
+    def z_at(v, place):
+        return place if group_of[v] == 1 else nz - 1 - place
+
+    def hop(v, c, place):
+        g = group_of[v]
+        if place == 0:
+            moves = [(0, 1, 2, 0), (0, 1, 3, 1), (3, 2, 2, 2)]
+        elif place == 1:
+            moves = [(1, 2, 2, 0), (1, 2, 3, 1)]
+        else:
+            moves = [(2, 3, 3, 1)]
+        for start, end, owner, slot in moves:
+            when(place_of(v) == start, lambda start=start, end=end, owner=owner, slot=slot: remote(
+                ("z", g, c, start, owner),
+                lambda: (grads.at[s, z_at(v, owner), y, x, c], from_c.at[g, slot, c], chip(z_at(v, end), y, x)),
+                guard=more(v, lambda: place_of(v) == start),
+                recv=lambda: number("recv", ("z", g, c, slot))))
+
+    def hop_wait(v, c, slot):
+        g = group_of[v]
+        pltpu.make_async_remote_copy(
+            grads.at[s, z, y, x, c], from_c.at[g, slot, c], send_sem.at[0],
+            recv_sem.at[number("recv", ("z", g, c, slot))], device_id=core, device_id_type=MESH).wait_recv()
+
+    def hop_add(v, c, place):
+        def go():
+            for owner, slot in ((2, 0), (3, 1)) if place == 1 else ((3, 1),):
+                hop_wait(v, c, slot)
+                g = group_of[v]
+
+                def body(i, carry, owner=owner, slot=slot):
+                    r = pl.ds(i * 128, 128)
+                    at = (s, z_at(v, owner), y, x, c, r)
+                    grads[at] = (grads[at].astype(f32) + from_c[g, slot, c, r].astype(f32)).astype(bf16)
+                    return carry
+
+                lax.fori_loop(0, unit // 128, body, 0)
+            hop(v, c, place)
+
+        guarded(v, lambda: when(place_of(v) == place, go))
+
+    def z_mid(v, c):
+        hop_add(v, c, 1)
+
+    def z_last(v, c):
+        hop_add(v, c, 2)
+
+    def in_group(g):
+        return (z // planes) == g
+
+    def owner_update(units, state, flat, sums):
+        for v in units:
+            g = group_of[v]
+
+            def total_at(slots, v=v, g=g):
+                for c in range(3):
+                    for slot in slots:
+                        hop_wait(v, c, slot)
+
+                def body(i, carry):
+                    r = pl.ds(i * 128, 128)
+                    for c in range(3):
+                        total = grads[s, z, y, x, c, r].astype(f32)
+                        for slot in slots:
+                            total = total + from_c[g, slot, c, r].astype(f32)
+                        sums[c, r] = total * (1.0 / token_count)
+                    return carry
+
+                lax.fori_loop(0, unit // 128, body, 0)
+
+            guarded(v, lambda v=v, f=total_at: when(place_of(v) == 2, lambda: f((0, 2))))
+            guarded(v, lambda v=v, f=total_at: when(place_of(v) == 3, lambda: f((1,))))
+        mine = {UP: in_group(1), EARLY: in_group(0) & one, LATE: in_group(0) & zero}[units[0]]
+        pl.when(mine)(lambda: owner_step(state, flat, sums))
+
+    def owner_step(state, flat, sums):
+        pltpu.make_async_copy(state_in, state, load_sem.at[0]).wait()
+        index = s * (nz * ny * nx) + w
+        in_rows = attn_in.shape[0] * attn_in.shape[1] // width // shard
+        out_rows = in_rows + attn_out.shape[0] // shard
+        ffn_rows = out_rows + ffn_in.shape[0] * ffn_in.shape[1] // width // shard
+        blocks = ffn_in.shape[1] // width
+        thirds = attn_in.shape[1] // width
+
+        def total_of(c, at_rows):
+            return sums[c, at_rows]
+
+        @pl.when(index < in_rows)
+        def _():
+            for c in range(3):
+                for lane in range(6):
+                    flat[lane, pl.ds(c, piece, stride=thirds), :] = total_of(c, pl.ds(lane * piece, piece))
+
+        @pl.when(((index >= in_rows) & (index < out_rows)) | (index >= ffn_rows))
+        def _():
+            for c in range(3):
+                for lane in range(6):
+                    flat[lane, pl.ds(c * piece, piece), :] = total_of(c, pl.ds(lane * piece, piece))
+
+        @pl.when((index >= out_rows) & (index < ffn_rows))
+        def _():
+            part = shard // blocks
+            for c in range(3):
+                for side in range(2):
+                    for j in range(blocks):
+                        flat[side * 3 + c, pl.ds(j, part, stride=blocks), :] = total_of(
+                            c, pl.ds(side * half + j * part, part))
+
+        def body(i, carry):
+            r = pl.ds(i * 16, 16)
+            grad = jnp.concatenate([flat[lane, r] for lane in range(6)], axis=1)
+            read[r] = grad
+            low[r] = adam_step((state[0, r], state[1, r], state[2, r]), grad)[0].astype(bf16)
+            return carry
+
+        lax.fori_loop(0, shard // 16, body, 0)
+        pltpu.make_async_copy(read.at[pl.ds(0, shard)], grad_out, store_sem.at[0]).start()
+        keep = pltpu.make_async_copy(low, copy_out.at[s, z, y, x], store_sem.at[4])
+        keep.start()
+        keep.wait()
+
+    gather_parts = PARTS
+    part_rows = shard // gather_parts
+
+    def part(k):
+        return pl.ds(k * part_rows, part_rows)
+
+    def part_lo(k):
+        return pl.ds(k * part_rows, part_rows // 2)
+
+    def part_hi(k):
+        return pl.ds(k * part_rows + part_rows // 2, part_rows // 2)
+
+    def relay(v, k, moves):
+        for start, end, owner, mine in moves:
+            def send(start=start, end=end, owner=owner, mine=mine):
+                zd = z_at(v, owner)
+
+                def ends():
+                    dst = copy_out.at[s, zd, y, x, part(k)]
+                    return (low.at[part(k)] if mine else dst), dst, chip(z_at(v, end), y, x)
+
+                remote(("gz", zd, k, start, end), ends, guard=more(v, lambda: place_of(v) == start),
+                       recv=lambda: number("recv", ("gz", zd, k)))
+
+            when(place_of(v) == start, send)
+
+    def relay_wait(v, k, place, owner):
+        zd = z_at(v, owner)
+        when(place_of(v) == place, lambda: pltpu.make_async_remote_copy(
+            low.at[part(k)], copy_out.at[s, zd, y, x, part(k)], send_sem.at[0],
+            recv_sem.at[number("recv", ("gz", zd, k))], device_id=core, device_id_type=MESH).wait_recv())
+
+    def gather_z(v, k):
+        guarded(v, lambda: relay(v, k, [(2, 1, 2, True), (2, 3, 2, True), (3, 2, 3, True)]))
+
+    def relay_one(v, k):
+        def go():
+            relay_wait(v, k, 2, 3)
+            relay_wait(v, k, 1, 2)
+            relay(v, k, [(2, 1, 3, False), (1, 0, 2, False)])
+
+        guarded(v, go)
+
+    def relay_two(v, k):
+        def go():
+            relay_wait(v, k, 1, 3)
+            relay(v, k, [(1, 0, 3, False)])
+
+        guarded(v, go)
+
+    def gather_b(v, k):
+        def go():
+            g = group_of[v]
+            relay_wait(v, k, 0, 2)
+            relay_wait(v, k, 0, 3)
+            relay_wait(v, k, 3, 2)
+            start(gb_moves, v, k)
+
+        guarded(v, go)
+
+    def gather_a(v, k):
+        def go():
+            wait_recvs(gb_moves, v, k)
+            g = group_of[v]
+            start(ga_moves, v, k)
+
+        guarded(v, go)
+
+    def hb_moves(v, k):
+        g = group_of[v]
+        return [
+            (("hb0", g, k, d), lambda peer=peer: same(copy_out.at[s, z, y, x, part_lo(k)], peer))
+            for d, peer in enumerate(y_peers)
+        ] + [
+            (("hb1", g, k, d), lambda peer=peer: same(copy_out.at[s, z, y, x, part_hi(k)], peer))
+            for d, peer in enumerate(x_peers)
+        ]
+
+    def ha_moves(v, k):
+        g = group_of[v]
+        return [
+            (("ha0", g, k, d), lambda peer=peer: same(copy_out.at[s, z, :, x, part_lo(k)], peer))
+            for d, peer in enumerate(x_peers)
+        ] + [
+            (("ha1", g, k, d), lambda peer=peer: same(copy_out.at[s, z, y, :, part_hi(k)], peer))
+            for d, peer in enumerate(y_peers)
+        ]
+
+    def owner_place(v):
+        return lambda: place_of(v) >= 2
+
+    def h_b(v, k):
+        when(place_of(v) >= 2, lambda: start(hb_moves, v, k, more(v, owner_place(v))))
+
+    def h_a(v, k):
+        def go():
+            wait_recvs(hb_moves, v, k)
+            start(ha_moves, v, k, more(v, owner_place(v)))
+
+        when(place_of(v) >= 2, go)
+
+    def plane_ends(v, k, owner, end):
+        return lambda: same(copy_out.at[s, z_at(v, owner), :, :, part(k)], chip(z_at(v, end), y, x))
+
+    def plane_send(v, k, at, end, owner):
+        when(place_of(v) == at, lambda: remote(
+            ("hz", z_at(v, owner), k, at, end), plane_ends(v, k, owner, end), guard=more(v, lambda: place_of(v) == at),
+            recv=lambda: number("recv", ("hz", z_at(v, owner), k))))
+
+    def plane_wait(v, k, at, owner):
+        when(place_of(v) == at, lambda: copy_of(
+            ("hz", z_at(v, owner), k, 2, 1), plane_ends(v, k, owner, 2),
+            lambda: number("recv", ("hz", z_at(v, owner), k))).wait_recv())
+
+    def h_z(v, k):
+        when(place_of(v) >= 2, lambda: wait_recvs(ha_moves, v, k))
+        plane_send(v, k, 2, 1, 2)
+        plane_send(v, k, 2, 3, 2)
+        plane_send(v, k, 3, 2, 3)
+
+    def h_r1(v, k):
+        plane_wait(v, k, 2, 3)
+        plane_wait(v, k, 1, 2)
+        plane_send(v, k, 2, 1, 3)
+        plane_send(v, k, 1, 0, 2)
+
+    def h_r2(v, k):
+        plane_wait(v, k, 1, 3)
+        plane_send(v, k, 1, 0, 3)
+
+    def gather_core(v, k):
+        def go():
+            if (v, k) in Z_LAST:
+                plane_wait(v, k, 0, 2)
+                plane_wait(v, k, 0, 3)
+                plane_wait(v, k, 3, 2)
+            else:
+                wait_recvs(ga_moves, v, k)
+            start(gc_moves, v, k)
+
+        guarded(v, go)
+
+    def gather_end(v, k):
+        wait_recvs(gc_moves, v, k)
+
+    wide_piece = piece
+    tile = hidden // 3
+    tile_pieces = tile // wide_piece
+    steps = tile_pieces // 2
+
+    tiles = []
+
+    def kv_copy(hp):
+        cols = pl.ds(pl.multiple_of(hp * 128, 128), 128)
+        return pltpu.make_async_remote_copy(
+            kv_box.at[:, cols], kv_box.at[:, cols], kv_send_sem.at[hp], kv_recv_sem.at[hp],
+            device_id=core, device_id_type=MESH)
+
+    def tile_loads(c):
+        slot = c % 2
+        copies = []
+        for p in range(tile_pieces):
+            at = p * 3 * wide_piece + c * wide_piece
+            to = pl.ds(p * wide_piece, wide_piece)
+            for k, (src, dst) in enumerate((
+                (ffn_in.at[:, pl.ds(at, wide_piece)], tiles[0].at[slot, :, to]),
+                (ffn_in.at[:, pl.ds(hidden + at, wide_piece)], tiles[1].at[slot, :, to]),
+                (ffn_out.at[pl.ds(at, wide_piece)], tiles[2].at[slot, to]),
+            )):
+                copies.append(pltpu.make_async_copy(src, dst, local_sem.at[slot, k, p]))
+        return copies
+
+    def forward_scope(raw, w_in):
+        w_out = kv_box
+        loads = [load(src, dst, load_sem.at[1 + k]) for k, (src, dst) in enumerate((
+            (streams, raw), (attn_in, w_in), (cos_table.at[pl.ds(0, EIGHTH)], starts.at[0]),
+            (sin_table.at[pl.ds(0, EIGHTH)], starts.at[1]), (attn_out, w_out)))]
+        plain_rows = [pl.ds(EIGHTH, 3 * EIGHTH), pl.ds(0, 3 * EIGHTH)]
+        plain_loads = [
+            [pltpu.make_async_copy(table.at[pl.ds(side * 3 * EIGHTH, 3 * EIGHTH)], own.at[plain_rows[side]],
+                                   load_sem.at[11 + k])
+             for k, (table, own) in enumerate(((cos_table, cosine), (sin_table, sine)))]
+            for side in range(2)
+        ]
+        for side in range(2):
+            @pl.when(s == side)
+            def _(side=side):
+                for copy in plain_loads[side]:
+                    copy.start()
+
+        carry_first = sum(depth_one[j] * read_two[j] for j in range(NS))
+        carry_stream = [sum(mix[i][j] * read_two[j] for j in range(NS)) for i in range(NS)]
+        loads[0].wait()
+
+        def norm_block(i, carry):
+            r = pl.ds(i * 64, 64)
+            parts = unpacked(raw[r])
+            branch = sum(parts[k] * read_one[k] for k in range(NS))
+            read[r] = sum(parts[k] * carry_stream[k] for k in range(NS))
+            normal, _ = normal_of(branch)
+            normed[r] = (normal * gains[0:1].astype(f32)).astype(bf16)
+            return carry
+
+        lax.fori_loop(0, rows // 64, norm_block, 0)
+        for copy in loads[1:]:
+            copy.wait()
+        load(cotangent, raw, load_sem.at[6])
+        for c in range(2):
+            for copy in tile_loads(c):
+                copy.start()
+
+        def tables(side):
+            first_special = 7 * EIGHTH * side
+            special = pl.ds(3 * EIGHTH * side, EIGHTH)
+            place = lax.broadcasted_iota(jnp.int32, (EIGHTH, EIGHTH), 0) + first_special
+            start = doc_starts(docs, place)
+            lane = lax.broadcasted_iota(jnp.int32, (EIGHTH, EIGHTH), 1)
+            pick = (place - start == lane).astype(f32)
+            for k, own in enumerate((cosine, sine)):
+                own[special] = jnp.dot(
+                    pick, starts[k], precision=lax.Precision.HIGHEST, preferred_element_type=f32)
+            for copy in plain_loads[side]:
+                copy.wait()
+
+        for side in range(2):
+            pl.when(s == side)(lambda side=side: tables(side))
+
+        own_rows = pl.ds(s * rows, rows)
+
+        def rotated(dest, dest_rows, offset):
+            def body(j, carry):
+                cols = pl.ds(pl.multiple_of(j * 256, 256), 256)
+                source = pl.ds(pl.multiple_of(offset + j * 256, 256), 256)
+                part = nn(normed[...], w_in[:, source])
+                halves = []
+                for k in range(2):
+                    turn = part[:, k * 128 : (k + 1) * 128]
+                    halves.append(turn * cosine[...] + swapped(turn) * sine[...])
+                dest[dest_rows, cols] = jnp.concatenate(halves, axis=1).astype(bf16)
+                return carry
+
+            lax.fori_loop(0, width // 256, body, 0)
+
+        def plain(j, carry):
+            cols = pl.ds(pl.multiple_of(j * 256, 256), 256)
+            source = pl.ds(pl.multiple_of(2 * width + j * 256, 256), 256)
+            values[own_rows, cols] = nn(normed[...], w_in[:, source]).astype(bf16)
+            return carry
+
+        lax.fori_loop(0, width // 256, plain, 0)
+        rotated(keys, own_rows, width)
+        pl.semaphore_wait(barrier, len(peers))
+        shared = pl.ds(EIGHTH, 3 * EIGHTH)
+        copies = [
+            pltpu.make_async_remote_copy(
+                ref.at[shared], ref.at[shared], kv_send_sem.at[6 + i], kv_recv_sem.at[6 + i],
+                device_id=core, device_id_type=MESH)
+            for i, ref in enumerate((keys, values))
+        ]
+
+        @pl.when(zero)
+        def _():
+            for copy in copies:
+                copy.start()
+
+        rotated(queries, pl.ds(0, rows), 0)
+
+        def attend(side):
+            blocks = q_blocks(side)
+            masks = [block_mask(docs, side, block) for block in blocks]
+
+            def pair(hp, carry):
+                jobs = [
+                    (2 * hp + q, pl.ds(pl.multiple_of((2 * hp + q) * 128, 128), 128), bi,
+                     pl.ds(row * EIGHTH, EIGHTH), pl.ds(key * EIGHTH, count * EIGHTH))
+                    for q in range(2) for bi, (row, key, count, _) in enumerate(blocks)
+                ]
+                scores = [
+                    masked_scores(keys[kr, cols], two_heads(queries[r, cols]) * HD ** (-0.5), masks[bi])
+                    for _, cols, bi, r, kr in jobs
+                ]
+                tops = [jnp.max(score, axis=0, keepdims=True) for score in scores]
+                lifted = [jnp.exp(score - top) for score, top in zip(scores, tops)]
+                totals = [jnp.sum(lift, axis=0, keepdims=True) for lift in lifted]
+                probs = [(lift * (1.0 / total)).astype(bf16) for lift, total in zip(lifted, totals)]
+                outs = [tn(values[job[4], job[1]], prob) for job, prob in zip(jobs, probs)]
+                for (pair_at, cols, bi, r, kr), out, top, total in zip(jobs, outs, tops, totals):
+                    context[r, cols] = one_pair(out).astype(bf16)
+                    lse[pl.ds(bi * 8 + pair_at, 1), :] = top + jnp.log(total)
+                return carry
+
+            lax.fori_loop(0, width // 256, pair, 0)
+
+        @pl.when(zero)
+        def _():
+            attend(0)
+            for copy in copies:
+                copy.wait_send()
+
+        @pl.when(one)
+        def _():
+            for copy in copies:
+                copy.wait_recv()
+            attend(1)
+
+        def out_block(j, carry):
+            cols = pl.ds(pl.multiple_of(j * 256, 256), 256)
+            part = nn(context[...], w_out[:, cols])
+            first[:, cols] = part
+            read[:, cols] += part * carry_first
+            return carry
+
+        lax.fori_loop(0, width // 256, out_block, 0)
+
+    def ffn_scope(raw, normed_two, normed_two_t, dsecond, gate_s, up_s, dhid_s, hid, dgate, dup):
+        pltpu.make_async_copy(cotangent, raw, load_sem.at[6]).wait()
+
+        def first_block(i, carry):
+            r = pl.ds(i * 64, 64)
+            parts = unpacked(raw[r])
+            dsecond[r] = sum(parts[j] * depth_two[j] for j in range(NS)).astype(bf16)
+            gfirst[r] = sum(parts[j] * depth_one[j] for j in range(NS))
+            normal, _ = normal_of(read[r])
+            normed_two[r] = (normal * gains[1:2].astype(f32)).astype(bf16)
+            second[r] = jnp.zeros((64, width), f32)
+            dread[r] = jnp.zeros((64, width), f32)
+            return carry
+
+        lax.fori_loop(0, rows // 64, first_block, 0)
+        normed_two_t[...] = normed_two[...].T
+
+        if True:
+            def sub(step, carry):
+                c, u = step // steps, step % steps
+                slot = c % 2
+                for k in range(3):
+                    def arrive(k=k):
+                        for copy in tile_loads(k):
+                            copy.wait()
+
+                    pl.when(step == k * steps)(arrive)
+                cols = pl.ds(pl.multiple_of(u * 2 * wide_piece, 2 * wide_piece), 2 * wide_piece)
+                wg, wu, wo = tiles[0][slot, :, cols], tiles[1][slot, :, cols], tiles[2][slot, cols]
+                gate_s[...] = nn(normed_two[...], wg)
+                up_s[...] = nn(normed_two[...], wu)
+                dhid_s[...] = nt(dsecond[...], wo)
+                for i in range(rows // 64):
+                    r = pl.ds(i * 64, 64)
+                    gate, up, dhid = gate_s[r], up_s[r], dhid_s[r]
+                    sig = 1.0 / (1.0 + jnp.exp(-gate))
+                    silu = gate * sig
+                    hid[r] = (silu * up).astype(bf16)
+                    dgate[r] = (dhid * up * sig * (1.0 + gate - silu)).astype(bf16)
+                    dup[r] = (dhid * silu).astype(bf16)
+                second[...] += nn(hid[...], wo)
+                dread[...] += nt(dgate[...], wg) + nt(dup[...], wu)
+                dwo = tn(hid[...], dsecond[...]).astype(bf16)
+                for q in range(2):
+                    p = 2 * u + q
+                    zi, yi, xi = planes + p // (ny * nx), (p // nx) % ny, p % nx
+                    for lane in range(6):
+                        grads[1, zi, yi, xi, c, pl.ds(lane * piece, piece)] = dwo[
+                            q * piece : (q + 1) * piece, lane * 128 : (lane + 1) * 128]
+                blocks = 2 * (hidden // width)
+                part = shard // blocks
+                for k, dact in enumerate((dgate, dup)):
+                    dwi = nn(normed_two_t[...], dact[...]).astype(bf16)
+                    j = u + k * (blocks // 2)
+                    for b in range(width // part):
+                        at_half, at = b // (width // part // 2), b % (width // part // 2)
+                        at = at + (nz * ny * nx // 2 if at_half == 0 else 0)
+                        zi, yi, xi = at // (ny * nx), (at // nx) % ny, at % nx
+                        for q in range(2):
+                            grads[at_half, zi, yi, xi, c, pl.ds(pl.multiple_of(q * half + j * part, 16), part)] = dwi[
+                                b * part : (b + 1) * part, q * 128 : (q + 1) * 128]
+                def more_weights():
+                    for copy in tile_loads(2):
+                        copy.start()
+
+                pl.when(step == steps - 1)(more_weights)
+                poll_loop(1, 3 * steps, step)
+                return carry
+
+            lax.fori_loop(0, 3 * steps, sub, 0)
+
+    stages = {
+        CORE_SEND: core_send,
+        ADD_CORE: add_core,
+        ADD_A: add_a,
+        ADD_B: add_b,
+        Z_MID: z_mid,
+        Z_LAST: z_last,
+        GATHER_Z: gather_z,
+        RELAY_ONE: relay_one,
+        RELAY_TWO: relay_two,
+        GATHER_B: gather_b,
+        GATHER_A: gather_a,
+        GATHER_CORE: gather_core,
+        GATHER_END: gather_end,
+        H_B: h_b,
+        H_A: h_a,
+        H_Z: h_z,
+        H_R1: h_r1,
+        H_R2: h_r2,
+    }
+
+    def run(actions):
+        for name, v, c in actions:
+            unit_now.append(v)
+            stages[name](v, c)
+            unit_now.pop()
+
+    def poll(at):
+        for side in range(2):
+            actions = PLAN.get(at, ((), ()))[side]
+            if actions:
+                pl.when(s == side)(lambda actions=actions: run(actions))
+
+    def poll_loop(first, count, step):
+        for i in range(count):
+            for side in range(2):
+                actions = PLAN.get(first + i, ((), ()))[side]
+                if actions:
+                    pl.when((step == i) & (s == side))(lambda actions=actions: run(actions))
+
+    def both_scopes(raw, gate_w, up_w, out_w):
+        tiles.extend((gate_w, up_w, out_w))
+        pl.run_scoped(
+            functools.partial(forward_scope, raw),
+            pltpu.VMEM(attn_in.shape, bf16))
+        pl.run_scoped(
+            functools.partial(ffn_scope, raw),
+            pltpu.VMEM((rows, width), bf16), pltpu.VMEM((width, rows), bf16), pltpu.VMEM((rows, width), bf16),
+            pltpu.VMEM((rows, 2 * piece), f32), pltpu.VMEM((rows, 2 * piece), f32), pltpu.VMEM((rows, 2 * piece), f32),
+            pltpu.VMEM((rows, 2 * piece), bf16), pltpu.VMEM((rows, 2 * piece), bf16), pltpu.VMEM((rows, 2 * piece), bf16))
+
+    pl.run_scoped(
+        both_scopes,
+        pltpu.VMEM((rows, NS, width), bf16), pltpu.VMEM((2, width, tile), bf16),
+        pltpu.VMEM((2, width, tile), bf16), pltpu.VMEM((2, tile, width), bf16))
+
+    gain_sums = {}
+
+    def attention_scope(w_in, w_out, dfirst, dcontext, dkeys, dvalues, own_keys, own_values, dproject, turned):
+        loads = [load(attn_out, w_out, load_sem.at[7]), load(attn_in, w_in, load_sem.at[8])]
+        carry_first = sum(depth_one[j] * read_two[j] for j in range(NS))
+
+        def norm_block(i, total):
+            r = pl.ds(i * 64, 64)
+            normal, scaling = normal_of(read[r])
+            grad = dread[r]
+            total = total + jnp.sum((grad * normal).reshape(8, 8, width), axis=0)
+            scaled = grad * gains[1:2].astype(f32)
+            centre = jnp.mean(scaled, axis=-1, keepdims=True)
+            along = jnp.mean(scaled * normal, axis=-1, keepdims=True)
+            value = scaling * (scaled - centre - normal * along)
+            dread[r] = value
+            dfirst[r] = (gfirst[r] + carry_first * value).astype(bf16)
+            return total
+
+        gain_two = lax.fori_loop(0, rows // 64, norm_block, jnp.zeros((8, width), f32))
+        row = jnp.sum(gain_two, axis=0, keepdims=True)
+        for k in range(width // 128):
+            small_box[0, s, width // 128 + k : width // 128 + k + 1, :] = row[:, k * 128 : (k + 1) * 128]
+
+        loads[0].wait()
+        poll(13)
+
+        def context_block(j, carry):
+            cols = pl.ds(pl.multiple_of(j * 256, 256), 256)
+            dcontext[:, cols] = nt(dfirst[...], w_out[cols]).astype(bf16)
+            return carry
+
+        lax.fori_loop(0, width // 256, context_block, 0)
+        turned[...] = context[...].T
+        shards_in = w_in.shape[1] // width * (width // piece) // 3
+
+        def out_block(j, carry):
+            cols = pl.ds(pl.multiple_of(j * 256, 256), 256)
+            part = nn(turned[...], dfirst[:, cols]).astype(bf16)
+            for b in range(width // piece):
+                at, c = shards_in + b // 3, b % 3
+                zi, yi, xi = at // (ny * nx), (at // nx) % ny, at % nx
+                for q in range(2):
+                    grads[0, zi, yi, xi, c, pl.ds(pl.multiple_of((2 * j + q) * piece, piece), piece)] = part[
+                        b * piece : (b + 1) * piece, q * 128 : (q + 1) * 128]
+            return carry
+
+        lax.fori_loop(0, width // 256, out_block, 0)
+        poll(14)
+
+        def blocks_back(side, hp):
+            blocks = q_blocks(side)
+            cols = pl.ds(pl.multiple_of(hp * 128, 128), 128)
+            spans = [
+                (pl.ds(row * EIGHTH, EIGHTH), pl.ds(key * EIGHTH, count * EIGHTH)) for row, key, count, _ in blocks
+            ]
+            qs = [two_heads(queries[r, cols]) * HD ** (-0.5) for r, kr in spans]
+            dstack = [two_heads(dcontext[r, cols]) for r, kr in spans]
+            scores = [
+                masked_scores(keys[kr, cols], qs[bi], block_mask(docs, side, blocks[bi]))
+                for bi, (r, kr) in enumerate(spans)
+            ]
+            dprobs = [nt(values[kr, cols], dstack[bi]) for bi, (r, kr) in enumerate(spans)]
+            probs = [jnp.exp(score - lse[pl.ds(bi * 8 + hp, 1), :]) for bi, score in enumerate(scores)]
+            inner = [jnp.sum(p * dp, axis=0, keepdims=True) for p, dp in zip(probs, dprobs)]
+            dscores = [(p * (dp - i)).astype(bf16) for p, dp, i in zip(probs, dprobs, inner)]
+            for bi, (r, kr) in enumerate(spans):
+                dkeys[kr] += nn(dscores[bi], qs[bi])
+                dvalues[kr] += nn(probs[bi].astype(bf16), dstack[bi])
+            dqs = [tn(keys[kr, cols], dscores[bi]) for bi, (r, kr) in enumerate(spans)]
+            for bi, (r, kr) in enumerate(spans):
+                dq = one_pair(dqs[bi]) * HD ** (-0.5)
+                dproject[r, cols] = (dq * cosine[r] - swapped(dq) * sine[r]).astype(bf16)
+
+        shared = pl.ds(EIGHTH, 3 * EIGHTH)
+
+        key_rows, value_rows = pl.ds(0, 3 * EIGHTH), pl.ds(3 * EIGHTH, 3 * EIGHTH)
+
+        def turned_back(dk):
+            return (dk * cosine[...] - swapped(dk) * sine[...]).astype(bf16)
+
+        def pair_back(hp, carry):
+            cols = pl.ds(pl.multiple_of(hp * 128, 128), 128)
+            key_cols = pl.ds(pl.multiple_of(width + hp * 128, 128), 128)
+            value_cols = pl.ds(pl.multiple_of(2 * width + hp * 128, 128), 128)
+            dkeys[...] = jnp.zeros_like(dkeys)
+            dvalues[...] = jnp.zeros_like(dvalues)
+
+            @pl.when(zero)
+            def _():
+                blocks_back(0, hp)
+                own_keys[:, cols] = dkeys[pl.ds(0, rows)]
+                own_values[:, cols] = dvalues[pl.ds(0, rows)]
+
+            @pl.when(one)
+            def _():
+                blocks_back(1, hp)
+                kv_box[key_rows, cols] = dkeys[shared].astype(bf16)
+                kv_box[value_rows, cols] = dvalues[shared].astype(bf16)
+                kv_copy(hp).start()
+                dproject[:, key_cols] = turned_back(dkeys[pl.ds(rows, rows)])
+                dproject[:, value_cols] = dvalues[pl.ds(rows, rows)].astype(bf16)
+
+            poll_loop(15, width // 128, hp)
+            return carry
+
+        lax.fori_loop(0, width // 128, pair_back, 0)
+
+        @pl.when(zero)
+        def _():
+            def finish(hp, carry):
+                cols = pl.ds(pl.multiple_of(hp * 128, 128), 128)
+                key_cols = pl.ds(pl.multiple_of(width + hp * 128, 128), 128)
+                value_cols = pl.ds(pl.multiple_of(2 * width + hp * 128, 128), 128)
+                kv_copy(hp).wait_recv()
+                own_keys[shared, cols] += kv_box[key_rows, cols].astype(f32)
+                own_values[shared, cols] += kv_box[value_rows, cols].astype(f32)
+                dproject[:, key_cols] = turned_back(own_keys[:, cols])
+                dproject[:, value_cols] = own_values[:, cols].astype(bf16)
+                return carry
+
+            lax.fori_loop(0, width // 128, finish, 0)
+
+        @pl.when(one)
+        def _():
+            def finish(hp, carry):
+                kv_copy(hp).wait_send()
+                return carry
+
+            lax.fori_loop(0, width // 128, finish, 0)
+
+        poll(21)
+        loads[1].wait()
+        turned[...] = normed[...].T
+
+        for j in range(w_in.shape[1] // width):
+            def in_block(cb, carry, j=j):
+                cols = pl.ds(pl.multiple_of(j * width + cb * 256, 256), 256)
+                part = nn(turned[...], dproject[:, cols]).astype(bf16)
+                for b in range(width // piece):
+                    zi, yi, xi = b // (ny * nx), (b // nx) % ny, b % nx
+                    for q in range(2):
+                        grads[0, zi, yi, xi, j, pl.ds(pl.multiple_of((2 * cb + q) * piece, piece), piece)] = part[
+                            b * piece : (b + 1) * piece, q * 128 : (q + 1) * 128]
+                return carry
+
+            lax.fori_loop(0, width // 256, in_block, 0)
+            poll(22 + j)
+
+        def dnormed_block(j, carry):
+            cols = pl.ds(pl.multiple_of(j * 256, 256), 256)
+            gfirst[:, cols] = nt(dproject[...], w_in[cols])
+            return carry
+
+        lax.fori_loop(0, width // 256, dnormed_block, 0)
+        poll(25)
+
+    pl.run_scoped(
+        attention_scope,
+        pltpu.VMEM(attn_in.shape, bf16), pltpu.VMEM(attn_out.shape, bf16),
+        pltpu.VMEM((rows, width), bf16), pltpu.VMEM((rows, width), bf16),
+        pltpu.VMEM((2 * rows, 128), f32), pltpu.VMEM((2 * rows, 128), f32),
+        pltpu.VMEM((rows, width), f32), pltpu.VMEM((rows, width), f32),
+        pltpu.VMEM((rows, 3 * width), bf16), pltpu.VMEM((width, rows), bf16),
+    )
+
+    def tail_scope(raw_h, raw_g, new_box, back_box, state, flat, sums_box):
+        axes = [(s, [core], 2), (x, x_peers, nx), (y, y_peers, ny), (z, z_peers, nz)]
+
+        def small_copies(k):
+            first = sum(len(axis[1]) for axis in axes[:k])
+            place, others, count = axes[k]
+            return [
+                pltpu.make_async_remote_copy(
+                    small_box.at[k, place], small_box.at[k, place], small_send.at[first + i], small_recv.at[first + i],
+                    device_id=peer, device_id_type=MESH)
+                for i, peer in enumerate(others)
+            ]
+
+        def small_stage(v, k):
+            if k > 0:
+                for copy in small_copies(k - 1):
+                    copy.wait()
+                total = small_box[k - 1, 0]
+                for j in range(1, axes[k - 1][2]):
+                    total = total + small_box[k - 1, j]
+            if k == len(axes):
+                grad = total * (1.0 / token_count)
+                new = adam_step((small_rows[0], small_rows[1], small_rows[2]), grad)
+                for k2, value in enumerate(new + (grad,)):
+                    small_out[k2] = value
+                return
+            if k > 0:
+                small_box[k, axes[k][0]] = total
+            for copy in small_copies(k):
+                copy.start()
+
+        stages[SMALL] = small_stage
+        stages[OWNER] = lambda v, c: owner_update((v,), state, flat, sums_box)
+        loads = [load(streams, raw_h, load_sem.at[9]), load(cotangent, raw_g, load_sem.at[10]),
+                 load(state_in, state, load_sem.at[0])]
+        for copy in loads[:2]:
+            copy.wait()
+        poll(26)
+        mixed_read = [sum(mix[i][j] * read_two[j] for j in range(NS)) for i in range(NS)]
+        pairs = 33
+        block = 32
+
+        def out_copies(i, slot):
+            r = pl.ds(i * block, block)
+            return [pltpu.make_async_copy(new_box.at[slot], new_out.at[r], out_sem.at[0, slot]),
+                    pltpu.make_async_copy(back_box.at[slot], stream_grad_out.at[r], out_sem.at[1, slot])]
+
+        def body(i, carry):
+            gain_one, sums = carry
+            r = pl.ds(i * block, block)
+            slot = i % 2
+
+            @pl.when(i >= 2)
+            def _():
+                for copy in out_copies(i, slot):
+                    copy.wait()
+
+            hs, gs = unpacked(raw_h[r]), unpacked(raw_g[r])
+            first_r, second_r, dread_r = first[r], second[r], dread[r]
+            branch = sum(hs[k] * read_one[k] for k in range(NS))
+            normal, scaling = normal_of(branch)
+            grad = gfirst[r]
+            gain_one = gain_one + jnp.sum((grad * normal).reshape(block // 8, 8, width), axis=0)
+            scaled = grad * gains[0:1].astype(f32)
+            centre = jnp.mean(scaled, axis=-1, keepdims=True)
+            along = jnp.mean(scaled * normal, axis=-1, keepdims=True)
+            dbranch = scaling * (scaled - centre - normal * along)
+            back = [
+                (sum(gs[j] * mix[k][j] for j in range(NS)) + dread_r * mixed_read[k] + dbranch * read_one[k]).astype(bf16)
+                for k in range(NS)
+            ]
+            back_box[slot] = packed_streams(back)
+            new = [
+                (sum(hs[k] * mix[k][j] for k in range(NS)) + first_r * depth_one[j] + second_r * depth_two[j]).astype(bf16)
+                for j in range(NS)
+            ]
+            new_box[slot] = packed_streams(new)
+            for copy in out_copies(i, slot):
+                copy.start()
+            products = [(hs[a], gs[b]) for a in range(NS) for b in range(NS)]
+            products += [(hs[a], dread_r) for a in range(NS)]
+            products += [(hs[a], dbranch) for a in range(NS)]
+            products += [(first_r, gs[b]) for b in range(NS)] + [(first_r, dread_r)]
+            products += [(second_r, gs[b]) for b in range(NS)]
+            new_sums = []
+            for total, (a, b) in zip(sums, products):
+                p = jnp.sum((a * b).reshape(block // 8, 8, width), axis=0)
+                new_sums.append(total + sum(p[:, q * 128 : (q + 1) * 128] for q in range(width // 128)))
+            poll_loop(27, rows // block - 1, i)
+            return gain_one, tuple(new_sums)
+
+        zero_tile = jnp.zeros((8, 128), f32)
+        gain_one, sums = lax.fori_loop(
+            0, rows // block, body, (jnp.zeros((8, width), f32), tuple(zero_tile for _ in range(pairs))))
+        for i in (rows // block - 2, rows // block - 1):
+            for copy in out_copies(i, i % 2):
+                copy.wait()
+        row = jnp.sum(gain_one, axis=0, keepdims=True)
+        for k in range(width // 128):
+            small_box[0, s, k : k + 1, :] = row[:, k * 128 : (k + 1) * 128]
+        sums = [jnp.sum(jnp.sum(t, axis=0, keepdims=True), axis=1, keepdims=True) for t in sums]
+        hg = [[sums[a * NS + b] for b in range(NS)] for a in range(NS)]
+        h_read = sums[16:20]
+        h_branch = sums[20:24]
+        first_g, first_read, second_g = sums[24:28], sums[28], sums[29:33]
+        lane = lax.broadcasted_iota(jnp.int32, (1, 128), 1)
+        line = jnp.zeros((1, 128), f32)
+        for i in range(NS):
+            entries = [hg[i][j] + read_two[j] * h_read[i] for j in range(NS)]
+            entries.append(h_branch[i])
+            entries.append(first_g[i] + read_two[i] * first_read)
+            entries.append(sum(mix[k][i] * h_read[k] for k in range(NS)) + depth_one[i] * first_read)
+            entries.append(second_g[i])
+            for j, value in enumerate(entries):
+                line = jnp.where(lane == i * 2 * NS + j, value, line)
+        last = 2 * width // 128
+        small_box[0, s, last : last + 1, :] = line
+        small_box[0, s, last + 1 :, :] = jnp.zeros((small_box.shape[2] - last - 1, 128), f32)
+
+        poll(42)
+        wait_sends()
+        pltpu.make_async_copy(read.at[pl.ds(0, shard)], grad_out, store_sem.at[0]).wait()
+
+    pl.run_scoped(
+        tail_scope,
+        pltpu.VMEM((rows, NS, width), bf16), pltpu.VMEM((rows, NS, width), bf16),
+        pltpu.VMEM((2, 32, NS, width), bf16), pltpu.VMEM((2, 32, NS, width), bf16),
+        pltpu.VMEM((3, shard, width), f32), pltpu.VMEM((6, shard, 128), f32),
+        pltpu.VMEM((3, unit, 128), f32),
+    )
+    assert ids["send"] <= send_sem.shape[0] and ids["recv"] <= recv_sem.shape[0], ids
+
+
+def finish_kernel(
+    new_in, back_in, copy_in, grad_in, state_in,
+    new_out, back_out, copy_out, weight_out, first_out, second_out, grad_out,
+    new_box, back_box, copy_box, grad, state, weight, first, second, in_sem, out_sem, copy_sem,
+):
+    parts = 4
+    rows = grad.shape[0] // parts
+    tokens = new_box.shape[0] // parts
+
+    def of_rows(k):
+        return pl.ds(k * rows, rows)
+
+    def of_tokens(k):
+        return pl.ds(k * tokens, tokens)
+
+    def loads(k):
+        return [
+            pltpu.make_async_copy(grad_in.at[of_rows(k)], grad.at[of_rows(k)], in_sem.at[0, k]),
+            pltpu.make_async_copy(state_in.at[:, of_rows(k)], state.at[:, of_rows(k)], in_sem.at[1, k]),
+            pltpu.make_async_copy(new_in.at[of_tokens(k)], new_box.at[of_tokens(k)], in_sem.at[2, k]),
+            pltpu.make_async_copy(back_in.at[of_tokens(k)], back_box.at[of_tokens(k)], in_sem.at[3, k]),
+        ]
+
+    def stores(k):
+        pairs = [(box.at[of_rows(k)], out.at[of_rows(k)]) for box, out in (
+            (grad, grad_out), (weight, weight_out), (first, first_out), (second, second_out))]
+        pairs += [(new_box.at[of_tokens(k)], new_out.at[of_tokens(k)]), (back_box.at[of_tokens(k)], back_out.at[of_tokens(k)])]
+        return [pltpu.make_async_copy(a, b, out_sem.at[i, k]) for i, (a, b) in enumerate(pairs)]
+
+    pieces = copy_sem.shape[1]
+    copy_rows = copy_box.shape[0] // pieces
+
+    def move(k, out):
+        r = pl.ds(k * copy_rows, copy_rows)
+        if out:
+            return pltpu.make_async_copy(copy_box.at[r], copy_out.at[r], copy_sem.at[1, k])
+        return pltpu.make_async_copy(copy_in.at[r], copy_box.at[r], copy_sem.at[0, k])
+
+    for k in range(parts):
+        for copy in loads(k):
+            copy.start()
+    for k in range(pieces):
+        move(k, False).start()
+    for k in range(parts):
+        for copy in loads(k):
+            copy.wait()
+
+        def body(i, carry, k=k):
+            r = pl.ds(k * rows + i * 16, 16)
+            weight[r], first[r], second[r] = adam_step((state[0, r], state[1, r], state[2, r]), grad[r])
+            return carry
+
+        lax.fori_loop(0, rows // 16, body, 0)
+        for copy in stores(k):
+            copy.start()
+    for k in range(pieces):
+        move(k, False).wait()
+        move(k, True).start()
+    for k in range(parts):
+        for copy in stores(k):
+            copy.wait()
+    for k in range(pieces):
+        move(k, True).wait()
+
+
+def finish(new, back, copy, grad, big_state):
+    shape = jax.ShapeDtypeStruct
+    hbm = pl.BlockSpec(memory_space=pl.ANY)
+    like = shape(grad.shape, grad.dtype)
+    box = pltpu.VMEM(grad.shape, grad.dtype)
+    return pl.pallas_call(
+        finish_kernel,
+        out_shape=[shape(new.shape, new.dtype), shape(back.shape, back.dtype), shape(copy.shape, copy.dtype),
+                   like, like, like, like],
+        in_specs=[hbm] * 5,
+        out_specs=[hbm] * 7,
+        scratch_shapes=[
+            pltpu.VMEM(new.shape, new.dtype), pltpu.VMEM(back.shape, back.dtype),
+            pltpu.VMEM(copy.shape, copy.dtype), box, pltpu.VMEM(big_state.shape, big_state.dtype), box, box, box,
+            pltpu.SemaphoreType.DMA((4, 4)), pltpu.SemaphoreType.DMA((6, 4)), pltpu.SemaphoreType.DMA((2, 12)),
+        ],
+        compiler_params=pltpu.CompilerParams(vmem_limit_bytes=60 * 2**20),
+        name="finish",
+    )(new, back, copy, grad, big_state)
+
+
+def layer_part(dims, token_count, docs, small_state, gains, streams, cotangent, weights, big_state):
+    attn_in, attn_out, ffn_in, ffn_out = weights
+    nz, ny, nx = dims
+    rows, width = streams.shape[0], attn_out.shape[0]
+    shard = big_state.shape[1]
+    unit, half, hidden = 2 * shard, shard, ffn_out.shape[0]
+    bf16, f32 = jnp.bfloat16, jnp.float32
+    shape = jax.ShapeDtypeStruct
+    cos_table, sin_table = rope_constants(6 * EIGHTH, HD)
+    small_count = small_state.shape[1]
+    small_rows = jnp.pad(small_state, ((0, 0), (0, -small_count % 1024))).reshape(3, -1, 128)
+    small_shape = small_rows.shape[1:]
+    smem = pl.BlockSpec(memory_space=pltpu.SMEM)
+    vmem = pl.BlockSpec(memory_space=pltpu.VMEM)
+    hbm = pl.BlockSpec(memory_space=pl.ANY)
+    state_shape = shape((shard, width), f32)
+    stream_shape = shape((rows, NS, width), bf16)
+    outs = pl.pallas_call(
+        functools.partial(layer_kernel, dims, token_count),
+        out_shape=[
+            stream_shape, stream_shape, shape((2, nz, ny, nx, shard, width), bf16),
+            state_shape, shape((4,) + small_shape, f32),
+            shape((nz, ny, nx, 3, unit, 128), bf16),
+        ],
+        in_specs=[smem, smem, vmem, vmem] + [hbm] * 9,
+        out_specs=[hbm] * 4 + [vmem, hbm],
+        scratch_shapes=[
+            pltpu.VMEM((2, nz, ny, nx, 3, unit, 128), bf16),
+            pltpu.VMEM((max(nx - 1, 1), nz, ny, 3, half, 128), bf16),
+            pltpu.VMEM((max(ny - 1, 1), nz, nx, 3, half, 128), bf16),
+            pltpu.VMEM((max(ny - 1, 1), nz, 3, half, 128), bf16),
+            pltpu.VMEM((max(nx - 1, 1), nz, 3, half, 128), bf16),
+            pltpu.VMEM((2, 3, 3, unit, 128), bf16),
+            pltpu.VMEM((nz // 2, ny, nx, unit, 128), bf16),
+            pltpu.VMEM((6 * EIGHTH, width), bf16),
+            pltpu.VMEM((rows, width), f32), pltpu.VMEM((rows, width), f32), pltpu.VMEM((rows, width), f32),
+            pltpu.VMEM((rows, width), f32), pltpu.VMEM((rows, width), f32),
+            pltpu.VMEM((rows, width), bf16), pltpu.VMEM((rows, width), bf16),
+            pltpu.VMEM((2 * rows, width), bf16), pltpu.VMEM((2 * rows, width), bf16),
+            pltpu.VMEM((rows, width), bf16), pltpu.VMEM((32, 2 * EIGHTH), f32),
+            pltpu.VMEM((rows, 128), f32), pltpu.VMEM((rows, 128), f32), pltpu.VMEM((2, EIGHTH, EIGHTH), f32),
+            pltpu.VMEM((shard, width), bf16),
+            pltpu.VMEM((4, max(2, nx, ny, nz)) + small_shape, f32),
+            pltpu.SemaphoreType.DMA((8,)), pltpu.SemaphoreType.DMA((8,)),
+            pltpu.SemaphoreType.DMA((240,)), pltpu.SemaphoreType.DMA((180,)),
+            pltpu.SemaphoreType.DMA((16,)), pltpu.SemaphoreType.DMA((2, 3, 8)),
+            pltpu.SemaphoreType.DMA((2,)), pltpu.SemaphoreType.DMA((5,)), pltpu.SemaphoreType.DMA((2, 2)),
+            pltpu.SemaphoreType.DMA((8,)), pltpu.SemaphoreType.DMA((8,)),
+        ],
+        compiler_params=pltpu.CompilerParams(
+            collective_id=1, has_side_effects=True, vmem_limit_bytes=255 * 2**18
+        ),
+        name="layer_step",
+    )(docs, small_state, gains, small_rows, streams, cotangent, attn_in, attn_out, ffn_in, ffn_out, big_state,
+      jnp.asarray(cos_table), jnp.asarray(sin_table))
+    small_out = outs[4].reshape(4, -1)[:, :small_count]
+    copy = outs[2].reshape(-1, width)
+    new, back, copy, weight_new, first_new, second_new, grad = finish(outs[0], outs[1], copy, outs[3], big_state)
+    return new, back, copy, weight_new, first_new, second_new, grad, small_out
+
+
 def torus(mesh):
     wide = mesh.shape["wide"]
     where = [getattr(d, "coords", None) for d in mesh.devices.flat]
@@ -620,6 +2148,21 @@
 ):
     row_count = streams.shape[1]
     model_width = attn_out.shape[0]
+    fits = (
+        big_state.shape[1] == 384 and model_width == 768 and row_count == 512
+        and ffn_out.shape[0] == 3072 and dims == (4, 2, 2)
+    )
+    if fits:
+        token_count = 2 * row_count * lax.axis_size("wide")
+        result, stream_grad, gathered, weight_new, first_new, second_new, owned_grads, small_out = layer_part(
+            dims, token_count, doc_lengths, small_state, norm_gains.T, streams[0], cotangent[0],
+            (attn_in, attn_out, ffn_in, ffn_out), big_state,
+        )
+        gains_copy = small_out[0, : 2 * model_width].reshape(2, model_width).T.astype(jnp.bfloat16)
+        return (
+            result[None], stream_grad[None], weight_new, first_new, second_new, owned_grads,
+            small_out[0], small_out[1], small_out[2], small_out[3], gathered, gains_copy,
+        )
     member = lax.axis_index("seq")
     token_total = row_count * lax.axis_size("seq")
     token_count = token_total * lax.axis_size("wide")

time: 570 us -> 236 us (0.41); the launches traced: 559 us -> 235 us
  other arithmetic: 147 us -> 0 us
  matrix products: 137 us -> 0 us
  local copies, waits for them, and re-layouts: 95.4 us -> 2.68 us
  Pallas kernels: 172 us -> 232 us
    dot_general x18 -> x0, matrix products: 137 us -> none  [the longest x4 27.4 us: right_product(): lax.dot_general(left, right, (((1,), (1,)), ((), ())), preferred_element_...]
    pallas_call x1 -> x2, Pallas kernels: 172 us -> 232 us  [the longest x1 212 us: layer_part(): pl.pallas_call(functools.partial(layer_kernel, dims, token_count), out_sh...]
    reduce_sum x10 -> x0, other arithmetic: 42.5 us -> none  [the longest x1 10.9 us: backward_layer(): grad_depth_one = jnp.sum(mid_grad * first_out[:, None, :], axis=(0, 2))]
    unnamed x123 -> x5, local copies, waits for them, and re-layouts: 41.1 us -> 1.38 us
    sub x3 -> x0, other arithmetic: 35.3 us -> none  [the longest x1 34 us: forward_layer(): lifted = jnp.exp(scores - row_top)]
    concatenate x7 -> x0, other arithmetic: 32.2 us -> none  [the longest x1 25 us: on_device(): jnp.concatenate([grad.astype(jnp.bfloat16).reshape(-1, model_width) for g...]
    convert_element_type x7 -> x0, other arithmetic: 23.9 us -> none  [the longest x1 16.6 us: backward_layer(): score_low = (attend * (attend_grad - inner_sum)).astype(jnp.bfloat16)]
    reshape x4 -> x0, local copies, waits for them, and re-layouts: 22.1 us -> none  [the longest x2 20.8 us: on_device(): grad.astype(jnp.bfloat16).reshape(-1, model_width)]
  transfers between devices with their start and end apart: 2 -> 0, of which waited for: 0 -> 0; matrix products, arithmetic and copies ran while one was open for 8% -> 0% of each run, Pallas kernels for 0% -> 0%
where the time goes in v3:
time: 236 us; the launch traced here: 235 us
  Pallas kernels  232 us (98%)
  local copies, waits for them, and re-layouts  2.68 us (1%)
    pallas_call x1, Pallas kernels, layer_part(): pl.pallas_call(functools.partial(layer_kernel, dims, token_count), out_sh...  212 us
    pallas_call x1, Pallas kernels, finish(): pl.pallas_call(finish_kernel, out_shape=[shape(new.shape, new.dtype), sha...  20.2 us

profile of v3, /device:TPU:0, one launch (start us, length us, event | category | flops | bytes accessed | tf_op | source)
XLA Modules:
  0.0 235.3 jit_solution(3290206479922291664)
XLA Ops:
  0.6 0.8 pad_bitcast_fusion
  1.4 0.6 copy.29
  2.0 211.8 %layer_step.1 = (bf16[512,4,768]{2,1,0:T(4,128)(2,1)}, bf16[512,4,768]{2,1,0:T(4,128)(2,1)}, bf16[2,4,2,2,384,768]{5,4,3,2,1,0:T(8,128)(2,1)}, f32[384,768]{1,0:...) custom-call(s32[1,8]{1,0:T(1,128)} %docs.1, f32[3,1568]{1,0:T(4,128)} %small.1, ...), custom_call_target="tpu_custom_call" | custom-call | tf_op jit(solution)/shard_map/layer_step/pallas_call | solution.py:1768
  213.8 0.0 copy-start
  213.8 20.2 %finish.1 = (bf16[512,4,768]{2,1,0:T(4,128)(2,1)}, bf16[512,4,768]{2,1,0:T(4,128)(2,1)}, bf16[12288,768]{1,0:T(8,128)(2,1)}, f32[384,768]{1,0:T(8,128)}, f32[384...) custom-call(bf16[512,4,768]{2,1,0:T(4,128)(2,1)} %get-tuple-element.24.new_in, ...), custom_call_target="tpu_custom_call" | custom-call | tf_op jit(solution)/shard_map/finish/pallas_call | solution.py:1735
  234.0 0.0 copy-done
  234.0 0.7 slice_reduce_fusion
  234.7 0.6 convert_element_type.9
  (2 shorter events, 0.0 us)
Async XLA Ops:
  213.8 20.2 %copy-start = (f32[4,16,128]{2,1,0:T(8,128)S(1)}, f32[4,16,128]{2,1,0:T(8,128)}, u32[]{:S(2)}) copy-start(f32[4,16,128]{2,1,0:T(8,128)} %get-tuple-element.34) | copy-start | bytes 98308

commit v4 on v3

--- a/solution.py
+++ b/solution.py
@@ -428,142 +428,154 @@
         ((ADD_CORE, UP, 0),),
     ),
     8: (
-        ((CORE_SEND, UP, 1), (CORE_SEND, EARLY, 0),),
-        ((ADD_CORE, UP, 1), (CORE_SEND, UP, 1),),
+        ((CORE_SEND, EARLY, 1), (CORE_SEND, UP, 1), (ADD_CORE, UP, 0),),
+        ((CORE_SEND, UP, 1), (ADD_A, UP, 0), (ADD_CORE, EARLY, 1),),
     ),
     9: (
-        ((ADD_CORE, UP, 0),),
-        ((ADD_A, UP, 0), (ADD_CORE, EARLY, 1),),
-    ),
-    10: (
-        ((CORE_SEND, EARLY, 1),),
         (),
+        ((ADD_CORE, UP, 1), (ADD_B, UP, 0),),
+    ),
+    11: (
+        ((ADD_A, UP, 0),),
+        (),
     ),
     12: (
-        ((CORE_SEND, UP, 2), (CORE_SEND, EARLY, 2), (ADD_A, UP, 0),),
-        ((ADD_A, UP, 1), (ADD_B, UP, 0), (ADD_CORE, EARLY, 0), (CORE_SEND, UP, 2), (ADD_A, EARLY, 1),
-         (ADD_CORE, UP, 2), (ADD_CORE, EARLY, 2),),
+        ((CORE_SEND, EARLY, 2), (CORE_SEND, UP, 2), (ADD_CORE, UP, 1),),
+        (),
+    ),
+    13: (
+        (),
+        ((ADD_A, EARLY, 1), (ADD_CORE, UP, 2), (CORE_SEND, UP, 2),),
     ),
     14: (
-        ((ADD_B, UP, 0),),
-        ((Z_MID, UP, 0), (ADD_B, UP, 1),),
+        ((ADD_A, UP, 1), (ADD_B, UP, 0),),
+        (),
+    ),
+    15: (
+        ((ADD_CORE, UP, 2),),
+        ((ADD_A, UP, 1), (ADD_B, EARLY, 1),),
     ),
     16: (
-        ((ADD_CORE, UP, 2), (Z_MID, UP, 0),),
+        ((CORE_SEND, EARLY, 0), (ADD_B, UP, 1), (Z_MID, UP, 1),),
+        ((ADD_A, UP, 2), (Z_MID, UP, 0),),
+    ),
+    17: (
+        ((Z_MID, UP, 0),),
+        ((ADD_CORE, EARLY, 2),),
+    ),
+    18: (
         (),
-    ),
-    17: (
+        ((ADD_B, UP, 1), (ADD_CORE, EARLY, 0), (ADD_B, UP, 2), (Z_MID, UP, 1),),
+    ),
+    19: (
         (),
-        ((ADD_B, EARLY, 1), (ADD_A, UP, 2), (Z_MID, UP, 1), (ADD_A, EARLY, 2),),
-    ),
-    18: (
-        ((ADD_A, UP, 2),),
+        ((ADD_A, EARLY, 2),),
+    ),
+    20: (
+        ((ADD_A, UP, 2), (ADD_B, UP, 2), (Z_LAST, UP, 1),),
         (),
     ),
-    19: (
-        ((ADD_CORE, UP, 1), (ADD_B, UP, 2),),
-        ((ADD_B, UP, 2),),
-    ),
     22: (
-        ((ADD_A, UP, 1), (ADD_CORE, LATE, 0),),
-        ((CORE_SEND, LATE, 0), (Z_MID, UP, 2), (ADD_B, EARLY, 2), (Z_LAST, UP, 1), (ADD_A, EARLY, 0), (Z_LAST,
-         UP, 0), (Z_MID, EARLY, 1),),
+        ((Z_MID, UP, 2),),
+        ((CORE_SEND, LATE, 0), (Z_MID, UP, 2),),
     ),
     23: (
-        ((ADD_CORE, LATE, 1), (Z_MID, UP, 2), (Z_LAST, UP, 0),),
-        ((CORE_SEND, LATE, 1), (Z_MID, EARLY, 2), (ADD_B, EARLY, 0),),
+        ((Z_LAST, UP, 0), (ADD_CORE, LATE, 0),),
+        ((ADD_A, EARLY, 0), (CORE_SEND, LATE, 1), (Z_MID, EARLY, 1), (Z_LAST, UP, 0), (ADD_B, EARLY, 2),),
     ),
     24: (
-        ((ADD_A, LATE, 0), (ADD_B, UP, 1), (ADD_CORE, LATE, 2), (ADD_A, LATE, 1), (ADD_B, LATE, 0), (Z_MID,
-         UP, 1),),
-        ((CORE_SEND, LATE, 2), (Z_LAST, UP, 2),),
+        ((ADD_CORE, LATE, 1),),
+        (),
     ),
     25: (
-        ((Z_LAST, UP, 2),),
-        ((Z_LAST, EARLY, 1), (Z_MID, EARLY, 0),),
+        ((Z_LAST, UP, 2), (ADD_A, LATE, 0), (ADD_CORE, LATE, 2),),
+        ((Z_LAST, UP, 1), (ADD_B, EARLY, 0),),
     ),
     26: (
-        ((ADD_A, LATE, 2), (ADD_B, LATE, 1),),
-        ((OWNER, UP, 0), (GATHER_Z, UP, 3),),
+        ((OWNER, UP, 0), (GATHER_Z, UP, 1), (H_B, UP, 0), (GATHER_Z, UP, 3),),
+        ((Z_MID, EARLY, 2), (Z_LAST, UP, 2), (CORE_SEND, LATE, 2),),
     ),
     27: (
+        ((ADD_A, LATE, 1), (ADD_B, LATE, 0),),
         (),
-        ((Z_LAST, EARLY, 2), (Z_LAST, EARLY, 0), (OWNER, EARLY, 0), (GATHER_Z, EARLY, 1), (RELAY_TWO, UP, 3),
-         (H_B, EARLY, 0), (RELAY_ONE, UP, 3), (GATHER_Z, UP, 1),),
     ),
     28: (
-        ((Z_LAST, UP, 1),),
-        ((GATHER_Z, UP, 2),),
+        ((RELAY_ONE, UP, 1), (ADD_A, LATE, 2),),
+        ((Z_MID, EARLY, 0), (OWNER, UP, 0), (GATHER_Z, UP, 2), (Z_LAST, EARLY, 1),),
     ),
     29: (
-        ((Z_MID, LATE, 0), (Z_LAST, LATE, 0), (ADD_B, LATE, 2), (Z_MID, LATE, 1), (OWNER, UP, 0), (Z_LAST,
-         LATE, 1), (Z_MID, LATE, 2), (GATHER_Z, UP, 2),),
+        ((RELAY_TWO, UP, 1), (Z_LAST, LATE, 0), (RELAY_ONE, UP, 3), (Z_MID, LATE, 0), (GATHER_B, UP, 1),),
+        ((Z_LAST, EARLY, 2), (GATHER_Z, UP, 3), (GATHER_Z, UP, 1),),
+    ),
+    30: (
+        ((RELAY_TWO, UP, 3), (ADD_B, LATE, 1), (Z_LAST, LATE, 1),),
         (),
     ),
-    30: (
-        ((Z_LAST, LATE, 2), (H_B, UP, 0),),
-        ((RELAY_ONE, UP, 2), (GATHER_B, UP, 3), (RELAY_TWO, UP, 2), (H_B, UP, 0),),
-    ),
     31: (
-        ((RELAY_ONE, UP, 2), (RELAY_TWO, UP, 2), (GATHER_Z, UP, 1),),
-        ((GATHER_Z, EARLY, 3), (RELAY_TWO, UP, 1), (H_A, EARLY, 0),),
+        ((H_A, UP, 0), (ADD_B, LATE, 2), (Z_MID, LATE, 1),),
+        ((Z_LAST, EARLY, 0), (RELAY_ONE, UP, 2), (OWNER, EARLY, 0), (H_B, UP, 0), (GATHER_Z, EARLY, 1),
+         (RELAY_TWO, UP, 2), (H_B, EARLY, 0),),
     ),
     32: (
-        ((GATHER_Z, UP, 3), (OWNER, LATE, 0), (GATHER_Z, LATE, 2), (RELAY_ONE, UP, 1), (GATHER_B, UP, 2),),
-        ((RELAY_ONE, UP, 1), (GATHER_Z, EARLY, 2), (GATHER_B, UP, 2), (RELAY_ONE, EARLY, 1), (GATHER_A, UP,
-         3),),
+        (),
+        ((GATHER_B, UP, 2), (RELAY_ONE, UP, 3), (RELAY_TWO, UP, 3), (GATHER_Z, EARLY, 3), (H_A, EARLY, 0),),
     ),
     33: (
-        ((RELAY_TWO, UP, 1), (RELAY_TWO, UP, 3), (RELAY_ONE, UP, 3), (GATHER_Z, LATE, 0),),
-        ((H_A, UP, 0), (GATHER_A, UP, 2), (GATHER_B, UP, 1), (RELAY_ONE, EARLY, 3),),
+        (),
+        ((RELAY_ONE, UP, 1), (GATHER_Z, EARLY, 2), (GATHER_B, UP, 3), (GATHER_A, UP, 2), (RELAY_ONE, EARLY,
+         1), (RELAY_ONE, EARLY, 2), (GATHER_A, UP, 3), (RELAY_TWO, EARLY, 1), (RELAY_ONE, EARLY, 3), (H_Z,
+         EARLY, 0), (GATHER_CORE, UP, 2), (GATHER_B, EARLY, 1), (RELAY_TWO, EARLY, 2), (GATHER_B, EARLY, 2),
+         (RELAY_TWO, EARLY, 3), (GATHER_B, EARLY, 3),),
     ),
     34: (
-        ((GATHER_B, UP, 1), (GATHER_Z, LATE, 1),),
+        ((GATHER_B, UP, 3), (Z_MID, LATE, 2), (GATHER_Z, UP, 2), (Z_LAST, LATE, 2),),
         (),
     ),
     35: (
-        ((H_A, UP, 0), (GATHER_Z, LATE, 3), (H_Z, UP, 0),),
-        ((RELAY_ONE, EARLY, 2), (RELAY_TWO, EARLY, 1), (H_Z, EARLY, 0), (GATHER_CORE, UP, 3),),
+        (),
+        ((H_A, UP, 0),),
     ),
     36: (
-        ((RELAY_ONE, LATE, 0), (GATHER_A, UP, 2),),
-        ((RELAY_TWO, EARLY, 3), (GATHER_B, EARLY, 1), (GATHER_B, EARLY, 3),),
+        ((GATHER_A, UP, 1),),
+        (),
     ),
     37: (
-        ((RELAY_ONE, LATE, 2), (GATHER_B, UP, 3),),
+        ((RELAY_ONE, UP, 2), (RELAY_TWO, UP, 2), (OWNER, LATE, 0), (GATHER_Z, LATE, 1), (GATHER_Z, LATE, 2),
+         (H_Z, UP, 0),),
         (),
     ),
     38: (
-        ((RELAY_TWO, LATE, 2), (RELAY_TWO, LATE, 0),),
-        ((RELAY_TWO, EARLY, 2), (GATHER_A, UP, 1), (GATHER_A, EARLY, 3), (H_Z, UP, 0), (GATHER_CORE, UP, 2),
-         (H_R1, EARLY, 0),),
+        ((GATHER_B, UP, 2),),
+        ((GATHER_A, EARLY, 1), (GATHER_A, EARLY, 3),),
     ),
     39: (
-        ((GATHER_A, UP, 1), (H_R1, UP, 0),),
+        ((H_R1, UP, 0), (GATHER_Z, LATE, 3), (GATHER_A, UP, 3),),
         (),
     ),
     40: (
-        (),
-        ((GATHER_A, EARLY, 1),),
+        ((RELAY_ONE, LATE, 1),),
+        ((GATHER_A, EARLY, 2),),
     ),
     41: (
-        ((GATHER_A, UP, 3), (GATHER_CORE, UP, 2), (GATHER_B, LATE, 0), (RELAY_ONE, LATE, 1), (GATHER_B, LATE,
-         2), (RELAY_TWO, LATE, 1),),
-        (),
+        ((GATHER_CORE, UP, 1),),
+        ((H_R1, EARLY, 0),),
     ),
     42: (
-        ((RELAY_ONE, LATE, 3), (GATHER_B, LATE, 1), (GATHER_A, LATE, 0), (GATHER_A, LATE, 2), (GATHER_CORE,
-         UP, 3), (RELAY_TWO, LATE, 3), (H_R2, UP, 0), (GATHER_END, EARLY, 1), (SMALL, UP, 0), (GATHER_END, UP,
-         1), (GATHER_END, EARLY, 3), (SMALL, UP, 1), (GATHER_CORE, LATE, 0), (GATHER_B, LATE, 3), (GATHER_A,
-         LATE, 1), (GATHER_CORE, UP, 1), (GATHER_END, EARLY, 2), (GATHER_CORE, UP, 0), (GATHER_A, LATE, 3),
-         (GATHER_CORE, LATE, 2), (GATHER_CORE, LATE, 1), (SMALL, UP, 2), (GATHER_CORE, LATE, 3), (SMALL, UP,
-         3), (GATHER_END, UP, 2), (SMALL, UP, 4), (GATHER_END, UP, 0), (GATHER_END, UP, 3), (GATHER_END,
-         EARLY, 0),),
-        ((GATHER_B, EARLY, 2), (GATHER_CORE, EARLY, 3), (GATHER_CORE, EARLY, 1), (SMALL, UP, 0), (GATHER_CORE,
-         UP, 1), (GATHER_A, EARLY, 2), (H_R1, UP, 0), (SMALL, UP, 1), (H_R2, UP, 0), (GATHER_CORE, EARLY, 2),
-         (GATHER_END, UP, 2), (H_R2, EARLY, 0), (GATHER_END, LATE, 0), (GATHER_CORE, EARLY, 0), (GATHER_END,
-         UP, 1), (SMALL, UP, 2), (GATHER_CORE, UP, 0), (GATHER_END, UP, 3), (GATHER_END, LATE, 1), (SMALL, UP,
-         3), (SMALL, UP, 4), (GATHER_END, UP, 0), (GATHER_END, LATE, 2), (GATHER_END, LATE, 3),),
+        ((SMALL, UP, 0), (RELAY_ONE, LATE, 2), (SMALL, UP, 1), (GATHER_A, UP, 2), (RELAY_TWO, LATE, 1),
+         (GATHER_B, LATE, 1), (RELAY_TWO, LATE, 2), (GATHER_Z, LATE, 0), (RELAY_ONE, LATE, 3), (GATHER_B,
+         LATE, 2), (RELAY_TWO, LATE, 3), (H_R2, UP, 0), (RELAY_TWO, LATE, 0), (RELAY_ONE, LATE, 0), (GATHER_A,
+         LATE, 1), (SMALL, UP, 2), (GATHER_CORE, UP, 2), (GATHER_B, LATE, 3), (GATHER_A, LATE, 2), (GATHER_B,
+         LATE, 0), (GATHER_END, UP, 1), (GATHER_END, EARLY, 3), (GATHER_END, UP, 2), (GATHER_CORE, LATE, 1),
+         (GATHER_A, LATE, 3), (GATHER_CORE, UP, 3), (GATHER_CORE, UP, 0), (GATHER_CORE, LATE, 2), (GATHER_A,
+         LATE, 0), (GATHER_CORE, LATE, 3), (GATHER_CORE, LATE, 0), (SMALL, UP, 3), (GATHER_END, UP, 0),
+         (GATHER_END, EARLY, 2), (SMALL, UP, 4), (GATHER_END, EARLY, 0), (GATHER_END, UP, 3), (GATHER_END,
+         EARLY, 1),),
+        ((SMALL, UP, 0), (GATHER_CORE, UP, 3), (RELAY_TWO, UP, 1), (H_Z, UP, 0), (GATHER_B, UP, 1),
+         (GATHER_CORE, EARLY, 3), (GATHER_CORE, EARLY, 1), (SMALL, UP, 1), (H_R1, UP, 0), (GATHER_A, UP, 1),
+         (GATHER_CORE, UP, 1), (H_R2, UP, 0), (H_R2, EARLY, 0), (GATHER_CORE, EARLY, 0), (SMALL, UP, 2),
+         (GATHER_CORE, EARLY, 2), (SMALL, UP, 3), (GATHER_END, LATE, 1), (GATHER_CORE, UP, 0), (GATHER_END,
+         UP, 2), (SMALL, UP, 4), (GATHER_END, UP, 0), (GATHER_END, UP, 3), (GATHER_END, UP, 1), (GATHER_END,
+         LATE, 2), (GATHER_END, LATE, 3), (GATHER_END, LATE, 0),),
     ),
 }
 

time: 236 us -> 226 us (0.958)
  Pallas kernels: 232 us -> 222 us
    pallas_call x1, Pallas kernels: 212 us -> 202 us  [layer_part(): pl.pallas_call(functools.partial(layer_kernel, dims, token_count), out_sh...]
where the time goes in v4:
time: 226 us
  Pallas kernels  222 us (98%)
  local copies, waits for them, and re-layouts  2.68 us (1%)
    pallas_call x1, Pallas kernels, layer_part(): pl.pallas_call(functools.partial(layer_kernel, dims, token_count), out_sh...  202 us
    pallas_call x1, Pallas kernels, finish(): pl.pallas_call(finish_kernel, out_shape=[shape(new.shape, new.dtype), sha...  20.2 us

profile of v4, /device:TPU:0, one launch (start us, length us, event | category | flops | bytes accessed | tf_op | source)
XLA Modules:
  0.0 225.7 jit_solution(11369264487873510070)
XLA Ops:
  0.6 0.8 pad_bitcast_fusion
  1.4 0.6 copy.29
  2.0 202.1 %layer_step.1 = (bf16[512,4,768]{2,1,0:T(4,128)(2,1)}, bf16[512,4,768]{2,1,0:T(4,128)(2,1)}, bf16[2,4,2,2,384,768]{5,4,3,2,1,0:T(8,128)(2,1)}, f32[384,768]{1,0:...) custom-call(s32[1,8]{1,0:T(1,128)} %docs.1, f32[3,1568]{1,0:T(4,128)} %small.1, ...), custom_call_target="tpu_custom_call" | custom-call | tf_op jit(solution)/shard_map/layer_step/pallas_call | solution.py:1780
  204.1 0.0 copy-start
  204.1 20.2 %finish.1 = (bf16[512,4,768]{2,1,0:T(4,128)(2,1)}, bf16[512,4,768]{2,1,0:T(4,128)(2,1)}, bf16[12288,768]{1,0:T(8,128)(2,1)}, f32[384,768]{1,0:T(8,128)}, f32[384...) custom-call(bf16[512,4,768]{2,1,0:T(4,128)(2,1)} %get-tuple-element.24.new_in, ...), custom_call_target="tpu_custom_call" | custom-call | tf_op jit(solution)/shard_map/finish/pallas_call | solution.py:1747
  224.3 0.0 copy-done
  224.4 0.7 slice_reduce_fusion
  225.1 0.6 convert_element_type.9
  (2 shorter events, 0.0 us)
Async XLA Ops:
  204.1 20.2 %copy-start = (f32[4,16,128]{2,1,0:T(8,128)S(1)}, f32[4,16,128]{2,1,0:T(8,128)}, u32[]{:S(2)}) copy-start(f32[4,16,128]{2,1,0:T(8,128)} %get-tuple-element.34) | copy-start | bytes 98308

commit v5 on v4

--- a/solution.py
+++ b/solution.py
@@ -679,16 +679,16 @@
             ("core", group_of[v], c),
             lambda: (grads.at[1 - s, zs_of(v), :, :, c], from_core.at[zs_of(v), :, :, c], core))]
 
-    def a_moves(v, c):
-        g = group_of[v]
+    def a_moves(v, c, only=None):
+        planes_of = [zd for zd in zlist(v) if only is None or zd == only]
         return [
-            (("a0", g, c, d), lambda d=d: (
-                grads.at[s, zs_of(v), :, (x + d) % nx, c, lo], from_a0.at[d - 1, zs_of(v), :, c], x_peers[d - 1]))
-            for d in range(1, nx)
+            (("a0", zd, c, d), lambda d=d, zd=zd: (
+                grads.at[s, zd, :, (x + d) % nx, c, lo], from_a0.at[d - 1, zd, :, c], x_peers[d - 1]))
+            for zd in planes_of for d in range(1, nx)
         ] + [
-            (("a1", g, c, d), lambda d=d: (
-                grads.at[s, zs_of(v), (y + d) % ny, :, c, hi], from_a1.at[d - 1, zs_of(v), :, c], y_peers[d - 1]))
-            for d in range(1, ny)
+            (("a1", zd, c, d), lambda d=d, zd=zd: (
+                grads.at[s, zd, (y + d) % ny, :, c, hi], from_a1.at[d - 1, zd, :, c], y_peers[d - 1]))
+            for zd in planes_of for d in range(1, ny)
         ]
 
     def b_moves(v, c):
@@ -729,6 +729,23 @@
     def gc_moves(v, k):
         return [(("gc", group_of[v], k), lambda: same(copy_out.at[s, zs_of(v), :, :, part(k)], core))]
 
+    def gc_first(v, k):
+        g = group_of[v]
+        return [
+            (("gc0", g, k), lambda: same(copy_out.at[s, zs_of(v), :, x, part_lo(k)], core)),
+            (("gc1", g, k), lambda: same(copy_out.at[s, zs_of(v), y, :, part_hi(k)], core)),
+        ]
+
+    def gc_second(v, k):
+        g = group_of[v]
+        return [
+            (("gc2", g, k, d), lambda d=d: same(copy_out.at[s, zs_of(v), :, (x + d) % nx, part_lo(k)], core))
+            for d in range(1, nx)
+        ] + [
+            (("gc3", g, k, d), lambda d=d: same(copy_out.at[s, zs_of(v), (y + d) % ny, :, part_hi(k)], core))
+            for d in range(1, ny)
+        ]
+
     def start(moves, v, c, guard="unit"):
         for key, ends in moves(v, c):
             remote(key, ends, guard=guard_of[v] if guard == "unit" else guard)
@@ -757,7 +774,7 @@
                     return carry
 
                 lax.fori_loop(0, ny * nx, body, 0)
-            start(a_moves, v, c)
+                start(functools.partial(a_moves, only=planes * g + plane), v, c)
 
         guarded(v, go)
 
@@ -999,6 +1016,7 @@
             wait_recvs(gb_moves, v, k)
             g = group_of[v]
             start(ga_moves, v, k)
+            start(gc_first, v, k)
 
         guarded(v, go)
 
@@ -1070,14 +1088,19 @@
                 plane_wait(v, k, 0, 2)
                 plane_wait(v, k, 0, 3)
                 plane_wait(v, k, 3, 2)
+                start(gc_moves, v, k)
             else:
                 wait_recvs(ga_moves, v, k)
-            start(gc_moves, v, k)
+                start(gc_second, v, k)
 
         guarded(v, go)
 
     def gather_end(v, k):
-        wait_recvs(gc_moves, v, k)
+        if (v, k) in Z_LAST:
+            wait_recvs(gc_moves, v, k)
+        else:
+            wait_recvs(gc_first, v, k)
+            wait_recvs(gc_second, v, k)
 
     wide_piece = piece
     tile = hidden // 3
@@ -1554,6 +1577,16 @@
                 for i, peer in enumerate(others)
             ]
 
+        def rows_of(j):
+            line = small_rows[j : j + 1]
+            count = line.shape[1]
+            pieces = [line[:, k * 128 : (k + 1) * 128] for k in range(count // 128)]
+            rest = count % 128
+            if rest:
+                pieces.append(jnp.concatenate([line[:, count - rest :], jnp.zeros((1, 128 - rest), f32)], axis=1))
+            pieces.append(jnp.zeros((small_box.shape[2] - len(pieces), 128), f32))
+            return jnp.concatenate(pieces, axis=0)
+
         def small_stage(v, k):
             if k > 0:
                 for copy in small_copies(k - 1):
@@ -1563,7 +1596,7 @@
                     total = total + small_box[k - 1, j]
             if k == len(axes):
                 grad = total * (1.0 / token_count)
-                new = adam_step((small_rows[0], small_rows[1], small_rows[2]), grad)
+                new = adam_step(tuple(rows_of(j) for j in range(3)), grad)
                 for k2, value in enumerate(new + (grad,)):
                     small_out[k2] = value
                 return
@@ -1770,8 +1803,7 @@
     shape = jax.ShapeDtypeStruct
     cos_table, sin_table = rope_constants(6 * EIGHTH, HD)
     small_count = small_state.shape[1]
-    small_rows = jnp.pad(small_state, ((0, 0), (0, -small_count % 1024))).reshape(3, -1, 128)
-    small_shape = small_rows.shape[1:]
+    small_shape = (-(-small_count // 1024) * 8, 128)
     smem = pl.BlockSpec(memory_space=pltpu.SMEM)
     vmem = pl.BlockSpec(memory_space=pltpu.VMEM)
     hbm = pl.BlockSpec(memory_space=pl.ANY)
@@ -1804,7 +1836,7 @@
             pltpu.VMEM((shard, width), bf16),
             pltpu.VMEM((4, max(2, nx, ny, nz)) + small_shape, f32),
             pltpu.SemaphoreType.DMA((8,)), pltpu.SemaphoreType.DMA((8,)),
-            pltpu.SemaphoreType.DMA((240,)), pltpu.SemaphoreType.DMA((180,)),
+            pltpu.SemaphoreType.DMA((260,)), pltpu.SemaphoreType.DMA((220,)),
             pltpu.SemaphoreType.DMA((16,)), pltpu.SemaphoreType.DMA((2, 3, 8)),
             pltpu.SemaphoreType.DMA((2,)), pltpu.SemaphoreType.DMA((5,)), pltpu.SemaphoreType.DMA((2, 2)),
             pltpu.SemaphoreType.DMA((8,)), pltpu.SemaphoreType.DMA((8,)),
@@ -1813,7 +1845,7 @@
             collective_id=1, has_side_effects=True, vmem_limit_bytes=255 * 2**18
         ),
         name="layer_step",
-    )(docs, small_state, gains, small_rows, streams, cotangent, attn_in, attn_out, ffn_in, ffn_out, big_state,
+    )(docs, small_state, gains, small_state, streams, cotangent, attn_in, attn_out, ffn_in, ffn_out, big_state,
       jnp.asarray(cos_table), jnp.asarray(sin_table))
     small_out = outs[4].reshape(4, -1)[:, :small_count]
     copy = outs[2].reshape(-1, width)

time: 226 us -> 225 us (level)
  no operation moved by 1% of the time
where the time goes in v5:
time: 225 us; the launch traced here: 224 us
  Pallas kernels  222 us (99%)
    pallas_call x1, Pallas kernels, layer_part(): pl.pallas_call(functools.partial(layer_kernel, dims, token_count), out_sh...  202 us
    pallas_call x1, Pallas kernels, finish(): pl.pallas_call(finish_kernel, out_shape=[shape(new.shape, new.dtype), sha...  20.2 us

profile of v5, /device:TPU:0, one launch (start us, length us, event | category | flops | bytes accessed | tf_op | source)
XLA Modules:
  0.0 224.4 jit_solution(3619584600008397030)
XLA Ops:
  0.6 202.2 %layer_step.1 = (bf16[512,4,768]{2,1,0:T(4,128)(2,1)}, bf16[512,4,768]{2,1,0:T(4,128)(2,1)}, bf16[2,4,2,2,384,768]{5,4,3,2,1,0:T(8,128)(2,1)}, f32[384,768]{1,0:...) custom-call(s32[1,8]{1,0:T(1,128)} %docs.1, f32[3,1568]{1,0:T(4,128)} %small_rows.1, ...), custom_call_target="tpu_custom_call" | custom-call | tf_op jit(solution)/shard_map/layer_step/pallas_call | solution.py:1812
  202.8 0.0 copy-start
  202.8 20.2 %finish.1 = (bf16[512,4,768]{2,1,0:T(4,128)(2,1)}, bf16[512,4,768]{2,1,0:T(4,128)(2,1)}, bf16[12288,768]{1,0:T(8,128)(2,1)}, f32[384,768]{1,0:T(8,128)}, f32[384...) custom-call(bf16[512,4,768]{2,1,0:T(4,128)(2,1)} %get-tuple-element.24.new_in, ...), custom_call_target="tpu_custom_call" | custom-call | tf_op jit(solution)/shard_map/finish/pallas_call | solution.py:1780
  223.0 0.0 copy-done
  223.1 0.7 slice_reduce_fusion
  223.8 0.6 convert_element_type.7
  (2 shorter events, 0.0 us)
Async XLA Ops:
  202.8 20.2 %copy-start = (f32[4,16,128]{2,1,0:T(8,128)S(1)}, f32[4,16,128]{2,1,0:T(8,128)}, u32[]{:S(2)}) copy-start(f32[4,16,128]{2,1,0:T(8,128)} %get-tuple-element.34) | copy-start | bytes 98308
